TPU v7x, 256 devices: a whole 4x4x8 slice. The times are simulated.
256 devices in a mesh: section: 8 (over z), dp: 32 (over y, x, core).
Axes of the slice: x: 4, y: 4, z: 8, core: 2. Of those that a mesh axis runs over, the one named last changes fastest.
Arguments:
- inputs: bfloat16 [4096, 4608], P('dp'), may hold values from -6 to 6
- w_in: bfloat16 [8, 4608, 128], P('section'), may hold values from -0.09375 to 0.09375
- w_out: bfloat16 [8, 128, 4608], P('section'), may hold values from -0.5 to 0.5
- layer_scale: float32 [8, 4608], P('section'), may hold values from 0.1 to 1.6, as said below
- cotangent: bfloat16 [4096, 4608], P('dp'), may hold values from -200 to 200
Outputs:
- grad_in: float32 [8, 4608, 128], P('section', 'dp')
- grad_out: float32 [8, 128, 4608], P('section', 'dp')
Inputs may be any that keep to these rules, and one draw needn't show every extreme that they name: `layer_scale`: positive scales.
All inputs are finite; a program needn't handle non-finite values.
Results may differ from a plain program's by a relative error of at most 0.028.
Values may be sent and summed in bfloat16 or wider, within the bound.
No kernel may reach another device: no remote copies, remote signals or barrier semaphores. Data moves between devices by JAX's collectives and lax.ppermute only.
A program may use at most 64 MiB of HBM per device.

v0:
```python
import jax
import jax.numpy as jnp
from jax import lax
from jax.sharding import PartitionSpec as P

SEQ = 128


EPS = 1e-06
CLIP_NORM = 256.0
CLIP_OFFSET = 0.01
CONTRACT_ROWS = (((0,), (0,)), ((), ()))
CONTRACT_COLS = (((1,), (1,)), ((), ()))


def passed_along(block, axis, distance):
    devices = range(lax.axis_size(axis))
    route = [(i - distance, i) for i in devices if i - distance in devices]
    return lax.ppermute(block, axis, route)


def row_scale(current):
    widened = current.astype(jnp.float32)
    inv_rms = lax.rsqrt(jnp.mean(widened * widened, axis=1, keepdims=True) + EPS)
    return (widened, inv_rms)


def forward_layer(current, in_matrix, out_matrix, branch_scale):
    widened, inv_rms = row_scale(current)
    normed = (widened * inv_rms).astype(jnp.bfloat16)
    pre_act = jnp.dot(normed, in_matrix, preferred_element_type=jnp.float32)
    hidden = jax.nn.gelu(pre_act).astype(jnp.bfloat16)
    branch = jnp.dot(hidden, out_matrix, preferred_element_type=jnp.float32)
    output = (widened + branch_scale * branch).astype(jnp.bfloat16)
    return (output, (current, pre_act))


def gram_norms(first_op, second_op):
    left_rows = first_op.reshape(-1, SEQ, first_op.shape[1])
    right_rows = second_op.reshape(-1, SEQ, second_op.shape[1])
    left_gram = jnp.einsum("eia,eja->eij", left_rows, left_rows, preferred_element_type=jnp.float32)
    right_gram = jnp.einsum(
        "eia,eja->eij", right_rows, right_rows, preferred_element_type=jnp.float32
    )
    return jnp.sum(left_gram * right_gram, axis=(1, 2))


def rebuild(stored):
    current, pre_act = stored
    widened, inv_rms = row_scale(current)
    unit_rows = widened * inv_rms
    normed = unit_rows.astype(jnp.bfloat16)
    hidden = jax.nn.gelu(pre_act).astype(jnp.bfloat16)
    return (inv_rms, unit_rows, normed, hidden)


def backward_layer(incoming, stored, in_matrix, out_matrix, branch_scale):
    pre_act = stored[1]
    inv_rms, unit_rows, normed, hidden = rebuild(stored)
    wide_grad = incoming.astype(jnp.float32)
    out_grad = (branch_scale * wide_grad).astype(jnp.bfloat16)
    hidden_grad = lax.dot_general(
        out_grad, out_matrix, CONTRACT_COLS, preferred_element_type=jnp.float32
    )
    _, pullback = jax.vjp(jax.nn.gelu, pre_act)
    pre_grad = pullback(hidden_grad)[0].astype(jnp.bfloat16)
    normed_grad = lax.dot_general(
        pre_grad, in_matrix, CONTRACT_COLS, preferred_element_type=jnp.float32
    )
    center = jnp.mean(normed_grad * unit_rows, axis=1, keepdims=True)
    new_grad = (wide_grad + inv_rms * (normed_grad - unit_rows * center)).astype(jnp.bfloat16)
    sq_norms = gram_norms(hidden, out_grad) + gram_norms(normed, pre_grad)
    return (new_grad, out_grad, pre_grad, sq_norms)


def forward_pass(inputs, in_matrix, out_matrix, branch_scale, section_index):
    section_count = lax.axis_size("section")
    token_count = inputs.shape[0]
    bottleneck = in_matrix.shape[1]
    current = inputs
    stored = (inputs, jnp.zeros((token_count, bottleneck), jnp.float32))
    for turn_index in range(section_count):

        def forward_active(carried):
            return forward_layer(carried[0], in_matrix, out_matrix, branch_scale)

        def forward_waiting(carried):
            return carried

        current, stored = lax.cond(
            section_index == turn_index, forward_active, forward_waiting, (current, stored)
        )
        if turn_index + 1 < section_count:
            current = passed_along(current, "section", 1)
    return stored


def backward_pass(cotangent, stored, in_matrix, out_matrix, branch_scale, section_index):
    section_count = lax.axis_size("section")
    token_count = cotangent.shape[0]
    bottleneck = in_matrix.shape[1]
    examples = token_count // SEQ
    carried_state = (
        cotangent,
        jnp.zeros_like(cotangent),
        jnp.zeros((token_count, bottleneck), jnp.bfloat16),
        jnp.zeros((examples,), jnp.float32),
    )
    for turn_index in reversed(range(section_count)):

        def backward_active(carried):
            return backward_layer(carried[0], stored, in_matrix, out_matrix, branch_scale)

        def backward_waiting(carried):
            return carried

        carried_state = lax.cond(
            section_index == turn_index, backward_active, backward_waiting, carried_state
        )
        if turn_index > 0:
            passed = passed_along(carried_state[0], "section", -1)
            carried_state = (passed,) + carried_state[1:]
    return (carried_state[1], carried_state[2], carried_state[3])


def per_device(inputs, w_in, w_out, layer_scale, cotangent):
    in_matrix = w_in[0]
    out_matrix = w_out[0]
    branch_scale = layer_scale[0]
    section_index = lax.axis_index("section")
    stored = forward_pass(inputs, in_matrix, out_matrix, branch_scale, section_index)
    out_grad, pre_grad, sq_norms = backward_pass(
        cotangent, stored, in_matrix, out_matrix, branch_scale, section_index
    )
    totals = lax.psum(sq_norms, "section")
    inv_rms, unit_rows, normed, hidden = rebuild(stored)
    clip_factor = CLIP_NORM / (jnp.sqrt(totals) + CLIP_OFFSET)
    row_factor = jnp.repeat(clip_factor, SEQ)[:, None]
    scaled_out = (out_grad.astype(jnp.float32) * row_factor).astype(jnp.bfloat16)
    scaled_in = (pre_grad.astype(jnp.float32) * row_factor).astype(jnp.bfloat16)
    columns = hidden
    grad_out = lax.psum_scatter(
        lax.dot_general(
            columns, scaled_out, CONTRACT_ROWS, preferred_element_type=jnp.float32
        ).astype(jnp.bfloat16),
        "dp",
        scatter_dimension=0,
        tiled=True,
    ).astype(jnp.float32)
    columns = normed
    grad_in = lax.psum_scatter(
        lax.dot_general(
            columns, scaled_in, CONTRACT_ROWS, preferred_element_type=jnp.float32
        ).astype(jnp.bfloat16),
        "dp",
        scatter_dimension=0,
        tiled=True,
    ).astype(jnp.float32)
    return (grad_in[None], grad_out[None])


def solution(mesh):
    return jax.shard_map(
        per_device,
        mesh=mesh,
        in_specs=(
            P("dp", None),
            P("section", None, None),
            P("section", None, None),
            P("section", None),
            P("dp", None),
        ),
        out_specs=(P("section", "dp", None), P("section", "dp", None)),
        check_vma=False,
    )
```

profile of v0, /device:TPU:2, one launch (start us, length us, event | category | flops | bytes accessed | tf_op | source)
XLA Modules:
  0.0 785.6 jit_solution(1912735046380478401)
XLA Ops:
  7.2 1.3 copy-done.11
  8.5 1.0 copy.119
  9.5 0.8 copy-done
  10.6 5.2 conditional.16
  10.9 1.2 fusion.9
  12.1 1.4 reduce.32
  13.5 2.3 fusion.6
  15.8 2.3 collective-permute-start
  18.1 24.8 %collective-permute-done = bf16[128,4608]{1,0:T(8,128)(2,1)} collective-permute-done((bf16[128,4608]{1,0:T(8,128)(2,1)}, bf16[128,4608]{1,0:T(8,128)(2,1)}, u32[]{:S(2)}, u32[]{:S(2)}) %collective-permute-start) | collective-permute-done | bytes 1179680 | tf_op jit(solution)/shard_map/ppermute | solution.py:19
  42.9 2.4 conditional.17
  42.9 2.4 copy.11
  45.3 11.2 %collective-permute-start.1 = (bf16[128,4608]{1,0:T(8,128)(2,1)}, bf16[128,4608]{1,0:T(8,128)(2,1)}, u32[]{:S(2)}, u32[]{:S(2)}) collective-permute-start(bf16[128,4608]{1,0:T(8,128)(2,1)} %get-tuple-element.425), channel_id=1, source_target_pairs={{0,32},{32,64},{64,96},{96,128},{128,160},{160,192},{192,224},{1,3... | collective-permute-start | bytes 3538952 | tf_op jit(solution)/shard_map/ppermute | solution.py:19
  56.5 23.9 %collective-permute-done.1 = bf16[128,4608]{1,0:T(8,128)(2,1)} collective-permute-done((bf16[128,4608]{1,0:T(8,128)(2,1)}, bf16[128,4608]{1,0:T(8,128)(2,1)}, u32[]{:S(2)}, u32[]{:S(2)}) %collective-permute-start.1) | collective-permute-done | bytes 1179680 | tf_op jit(solution)/shard_map/ppermute | solution.py:19
  80.4 2.4 conditional.18
  80.4 2.4 copy.17
  82.8 5.4 collective-permute-start.2
  88.2 23.0 %collective-permute-done.2 = bf16[128,4608]{1,0:T(8,128)(2,1)} collective-permute-done((bf16[128,4608]{1,0:T(8,128)(2,1)}, bf16[128,4608]{1,0:T(8,128)(2,1)}, u32[]{:S(2)}, u32[]{:S(2)}) %collective-permute-start.2) | collective-permute-done | bytes 1179680 | tf_op jit(solution)/shard_map/ppermute | solution.py:19
  111.2 2.4 conditional.19
  111.2 2.4 copy.23
  113.5 9.3 %collective-permute-start.3 = (bf16[128,4608]{1,0:T(8,128)(2,1)}, bf16[128,4608]{1,0:T(8,128)(2,1)}, u32[]{:S(2)}, u32[]{:S(2)}) collective-permute-start(bf16[128,4608]{1,0:T(8,128)(2,1)} %get-tuple-element.431), channel_id=1, source_target_pairs={{0,32},{32,64},{64,96},{96,128},{128,160},{160,192},{192,224},{1,3... | collective-permute-start | bytes 3538952 | tf_op jit(solution)/shard_map/ppermute | solution.py:19
  122.9 22.4 %collective-permute-done.3 = bf16[128,4608]{1,0:T(8,128)(2,1)} collective-permute-done((bf16[128,4608]{1,0:T(8,128)(2,1)}, bf16[128,4608]{1,0:T(8,128)(2,1)}, u32[]{:S(2)}, u32[]{:S(2)}) %collective-permute-start.3) | collective-permute-done | bytes 1179680 | tf_op jit(solution)/shard_map/ppermute | solution.py:19
  145.2 2.4 conditional.20
  145.2 2.4 copy.29
  147.6 5.4 collective-permute-start.4
  153.0 21.4 %collective-permute-done.4 = bf16[128,4608]{1,0:T(8,128)(2,1)} collective-permute-done((bf16[128,4608]{1,0:T(8,128)(2,1)}, bf16[128,4608]{1,0:T(8,128)(2,1)}, u32[]{:S(2)}, u32[]{:S(2)}) %collective-permute-start.4) | collective-permute-done | bytes 1179680 | tf_op jit(solution)/shard_map/ppermute | solution.py:19
  174.5 2.4 conditional.21
  174.5 2.4 copy.35
  176.8 9.6 %collective-permute-start.5 = (bf16[128,4608]{1,0:T(8,128)(2,1)}, bf16[128,4608]{1,0:T(8,128)(2,1)}, u32[]{:S(2)}, u32[]{:S(2)}) collective-permute-start(bf16[128,4608]{1,0:T(8,128)(2,1)} %get-tuple-element.437), channel_id=1, source_target_pairs={{0,32},{32,64},{64,96},{96,128},{128,160},{160,192},{192,224},{1,3... | collective-permute-start | bytes 3538952 | tf_op jit(solution)/shard_map/ppermute | solution.py:19
  186.4 20.8 %collective-permute-done.5 = bf16[128,4608]{1,0:T(8,128)(2,1)} collective-permute-done((bf16[128,4608]{1,0:T(8,128)(2,1)}, bf16[128,4608]{1,0:T(8,128)(2,1)}, u32[]{:S(2)}, u32[]{:S(2)}) %collective-permute-start.5) | collective-permute-done | bytes 1179680 | tf_op jit(solution)/shard_map/ppermute | solution.py:19
  207.2 2.4 conditional.22
  207.2 2.4 copy.41
  209.6 5.4 collective-permute-start.6
  215.0 19.9 %collective-permute-done.6 = bf16[128,4608]{1,0:T(8,128)(2,1)} collective-permute-done((bf16[128,4608]{1,0:T(8,128)(2,1)}, bf16[128,4608]{1,0:T(8,128)(2,1)}, u32[]{:S(2)}, u32[]{:S(2)}) %collective-permute-start.6) | collective-permute-done | bytes 1179680 | tf_op jit(solution)/shard_map/ppermute | solution.py:19
  234.9 1.7 conditional.24
  234.9 1.1 broadcast_in_dim.19
  236.6 1.3 collective-permute-start.7
  237.9 29.8 %collective-permute-done.7 = bf16[128,4608]{1,0:T(8,128)(2,1)} collective-permute-done((bf16[128,4608]{1,0:T(8,128)(2,1)}, bf16[128,4608]{1,0:T(8,128)(2,1)}, u32[]{:S(2)}, u32[]{:S(2)}) %collective-permute-start.7) | collective-permute-done | bytes 1179680 | tf_op jit(solution)/shard_map/ppermute | solution.py:19
  267.6 1.3 collective-permute-start.8
  268.9 24.7 %collective-permute-done.8 = bf16[128,4608]{1,0:T(8,128)(2,1)} collective-permute-done((bf16[128,4608]{1,0:T(8,128)(2,1)}, bf16[128,4608]{1,0:T(8,128)(2,1)}, u32[]{:S(2)}, u32[]{:S(2)}) %collective-permute-start.8) | collective-permute-done | bytes 1179680 | tf_op jit(solution)/shard_map/ppermute | solution.py:19
  293.6 1.3 collective-permute-start.9
  294.9 26.9 %collective-permute-done.9 = bf16[128,4608]{1,0:T(8,128)(2,1)} collective-permute-done((bf16[128,4608]{1,0:T(8,128)(2,1)}, bf16[128,4608]{1,0:T(8,128)(2,1)}, u32[]{:S(2)}, u32[]{:S(2)}) %collective-permute-start.9) | collective-permute-done | bytes 1179680 | tf_op jit(solution)/shard_map/ppermute | solution.py:19
  321.7 1.3 collective-permute-start.10
  323.0 23.7 %collective-permute-done.10 = bf16[128,4608]{1,0:T(8,128)(2,1)} collective-permute-done((bf16[128,4608]{1,0:T(8,128)(2,1)}, bf16[128,4608]{1,0:T(8,128)(2,1)}, u32[]{:S(2)}, u32[]{:S(2)}) %collective-permute-start.10) | collective-permute-done | bytes 1179680 | tf_op jit(solution)/shard_map/ppermute | solution.py:19
  346.8 1.3 collective-permute-start.11
  348.1 24.6 %collective-permute-done.11 = bf16[128,4608]{1,0:T(8,128)(2,1)} collective-permute-done((bf16[128,4608]{1,0:T(8,128)(2,1)}, bf16[128,4608]{1,0:T(8,128)(2,1)}, u32[]{:S(2)}, u32[]{:S(2)}) %collective-permute-start.11) | collective-permute-done | bytes 1179680 | tf_op jit(solution)/shard_map/ppermute | solution.py:19
  372.7 1.3 collective-permute-start.12
  374.0 24.9 %collective-permute-done.12 = bf16[128,4608]{1,0:T(8,128)(2,1)} collective-permute-done((bf16[128,4608]{1,0:T(8,128)(2,1)}, bf16[128,4608]{1,0:T(8,128)(2,1)}, u32[]{:S(2)}, u32[]{:S(2)}) %collective-permute-start.12) | collective-permute-done | bytes 1179680 | tf_op jit(solution)/shard_map/ppermute | solution.py:19
  398.9 1.3 collective-permute-start.13
  400.2 145.4 %collective-permute-done.13 = bf16[128,4608]{1,0:T(8,128)(2,1)S(1)} collective-permute-done((bf16[128,4608]{1,0:T(8,128)(2,1)}, bf16[128,4608]{1,0:T(8,128)(2,1)S(1)}, u32[]{:S(2)}, u32[]{:S(2)}) %collective-permute-start.13) | collective-permute-done | bytes 1179680 | tf_op jit(solution)/shard_map/ppermute | solution.py:19
  545.6 13.2 %conditional.31 = (f32[1]{0:T(128)}, bf16[128,128]{1,0:T(8,128)(2,1)}, bf16[128,4608]{1,0:T(8,128)(2,1)}) conditional(s32[]{:T(128)} %convert_element_type.337, (f32[1]{0:T(128)}, bf16[128,4608]{1,0:T(8,128)(2,1)}, bf16[128,128]{1,0:T(8,128)(2,1)}) %tuple.176, (f32[128,128]{1,0:T(8,128)}, f32[1,4608]{1,0:T(1,128)}, ...), branch_computations={%region_67.68_spmd, %region_68.72_spmd} | conditional | flops 467222656 | bytes 8773680 | solution.py:117
  545.6 1.4 reduce.46
  547.0 2.2 fusion.411
  549.1 2.4 fusion.429
  551.5 1.0 fusion.480
  552.5 1.2 fusion.420
  553.7 2.1 fusion.479
  555.8 1.8 fusion.419
  558.8 15.3 %psum.7 = f32[1]{0:T(128)} all-reduce(f32[1]{0:T(128)} %get-tuple-element.500), channel_id=1, replica_groups=mesh['section'=8,'dp'=32] {'section'}, use_global_device_ids=true, to_apply=%region_72.0 | all-reduce | flops 1 | bytes 8 | tf_op jit(solution)/shard_map/psum | solution.py:135
  574.8 2.8 convolution_convert_fusion
  578.0 2.4 convolution_convert_fusion.1
  582.3 107.8 %all-reduce.3.cloned.1.call-done = bf16[128,4608]{1,0:T(8,128)(2,1)} async-done(((bf16[128,4608]{1,0:T(8,128)(2,1)}), bf16[128,4608]{1,0:T(8,128)(2,1)}) %all-reduce.3.cloned.1.call-update) | async-done | bytes 1179664
  690.1 1.5 bitcast_convert_fusion
  691.6 85.8 %reduce-scatter.2.cloned.1.call-done = bf16[144,128]{1,0:T(8,128)(2,1)} async-done(((bf16[4608,128]{1,0:T(8,128)(2,1)}), bf16[144,128]{1,0:T(8,128)(2,1)}) %reduce-scatter.2.cloned.1.call-update) | async-done | bytes 36880 | tf_op jit(solution)/shard_map/reduce_scatter | solution.py:151
  777.4 1.4 bitcast_convert_fusion.1
  (26 shorter events, 3.0 us)
Async XLA Ops:
  7.2 682.9 %all-reduce.3.cloned.1.call-start = ((), (), s32[]{:S(2)}) async-start(), calls=%async_computation.2 | async-start | bytes 2359296
  7.2 1.3 copy-start.11
  7.2 2.3 copy-start.2
  8.5 1.8 copy-start
  8.5 2.1 copy-start.1
  15.8 27.1 %collective-permute-start = (bf16[128,4608]{1,0:T(8,128)(2,1)}, bf16[128,4608]{1,0:T(8,128)(2,1)}, u32[]{:S(2)}, u32[]{:S(2)}) collective-permute-start(bf16[128,4608]{1,0:T(8,128)(2,1)} %get-tuple-element.422), channel_id=1, source_target_pairs={{0,32},{32,64},{64,96},{96,128},{128,160},{160,192},{192,224},{1,3... | collective-permute-start | bytes 3538952 | tf_op jit(solution)/shard_map/ppermute | solution.py:19
  45.3 35.1 %collective-permute-start.1 = (bf16[128,4608]{1,0:T(8,128)(2,1)}, bf16[128,4608]{1,0:T(8,128)(2,1)}, u32[]{:S(2)}, u32[]{:S(2)}) collective-permute-start(bf16[128,4608]{1,0:T(8,128)(2,1)} %get-tuple-element.425), channel_id=1, source_target_pairs={{0,32},{32,64},{64,96},{96,128},{128,160},{160,192},{192,224},{1,3... | collective-permute-start | bytes 3538952 | tf_op jit(solution)/shard_map/ppermute | solution.py:19
  82.8 28.4 %collective-permute-start.2 = (bf16[128,4608]{1,0:T(8,128)(2,1)}, bf16[128,4608]{1,0:T(8,128)(2,1)}, u32[]{:S(2)}, u32[]{:S(2)}) collective-permute-start(bf16[128,4608]{1,0:T(8,128)(2,1)} %get-tuple-element.428), channel_id=1, source_target_pairs={{0,32},{32,64},{64,96},{96,128},{128,160},{160,192},{192,224},{1,3... | collective-permute-start | bytes 3538952 | tf_op jit(solution)/shard_map/ppermute | solution.py:19
  113.5 31.7 %collective-permute-start.3 = (bf16[128,4608]{1,0:T(8,128)(2,1)}, bf16[128,4608]{1,0:T(8,128)(2,1)}, u32[]{:S(2)}, u32[]{:S(2)}) collective-permute-start(bf16[128,4608]{1,0:T(8,128)(2,1)} %get-tuple-element.431), channel_id=1, source_target_pairs={{0,32},{32,64},{64,96},{96,128},{128,160},{160,192},{192,224},{1,3... | collective-permute-start | bytes 3538952 | tf_op jit(solution)/shard_map/ppermute | solution.py:19
  147.6 26.9 %collective-permute-start.4 = (bf16[128,4608]{1,0:T(8,128)(2,1)}, bf16[128,4608]{1,0:T(8,128)(2,1)}, u32[]{:S(2)}, u32[]{:S(2)}) collective-permute-start(bf16[128,4608]{1,0:T(8,128)(2,1)} %get-tuple-element.434), channel_id=1, source_target_pairs={{0,32},{32,64},{64,96},{96,128},{128,160},{160,192},{192,224},{1,3... | collective-permute-start | bytes 3538952 | tf_op jit(solution)/shard_map/ppermute | solution.py:19
  176.8 30.4 %collective-permute-start.5 = (bf16[128,4608]{1,0:T(8,128)(2,1)}, bf16[128,4608]{1,0:T(8,128)(2,1)}, u32[]{:S(2)}, u32[]{:S(2)}) collective-permute-start(bf16[128,4608]{1,0:T(8,128)(2,1)} %get-tuple-element.437), channel_id=1, source_target_pairs={{0,32},{32,64},{64,96},{96,128},{128,160},{160,192},{192,224},{1,3... | collective-permute-start | bytes 3538952 | tf_op jit(solution)/shard_map/ppermute | solution.py:19
  209.6 25.3 %collective-permute-start.6 = (bf16[128,4608]{1,0:T(8,128)(2,1)}, bf16[128,4608]{1,0:T(8,128)(2,1)}, u32[]{:S(2)}, u32[]{:S(2)}) collective-permute-start(bf16[128,4608]{1,0:T(8,128)(2,1)} %get-tuple-element.442), channel_id=1, source_target_pairs={{0,32},{32,64},{64,96},{96,128},{128,160},{160,192},{192,224},{1,3... | collective-permute-start | bytes 3538952 | tf_op jit(solution)/shard_map/ppermute | solution.py:19
  236.6 31.0 %collective-permute-start.7 = (bf16[128,4608]{1,0:T(8,128)(2,1)}, bf16[128,4608]{1,0:T(8,128)(2,1)}, u32[]{:S(2)}, u32[]{:S(2)}) collective-permute-start(bf16[128,4608]{1,0:T(8,128)(2,1)} %get-tuple-element.447), channel_id=1, source_target_pairs={{32,0},{64,32},{96,64},{128,96},{160,128},{192,160},{224,192},{33,... | collective-permute-start | bytes 3538952 | tf_op jit(solution)/shard_map/ppermute | solution.py:19
  267.6 26.0 %collective-permute-start.8 = (bf16[128,4608]{1,0:T(8,128)(2,1)}, bf16[128,4608]{1,0:T(8,128)(2,1)}, u32[]{:S(2)}, u32[]{:S(2)}) collective-permute-start(bf16[128,4608]{1,0:T(8,128)(2,1)} %get-tuple-element.451), channel_id=1, source_target_pairs={{32,0},{64,32},{96,64},{128,96},{160,128},{192,160},{224,192},{33,... | collective-permute-start | bytes 3538952 | tf_op jit(solution)/shard_map/ppermute | solution.py:19
  293.6 28.1 %collective-permute-start.9 = (bf16[128,4608]{1,0:T(8,128)(2,1)}, bf16[128,4608]{1,0:T(8,128)(2,1)}, u32[]{:S(2)}, u32[]{:S(2)}) collective-permute-start(bf16[128,4608]{1,0:T(8,128)(2,1)} %get-tuple-element.455), channel_id=1, source_target_pairs={{32,0},{64,32},{96,64},{128,96},{160,128},{192,160},{224,192},{33,... | collective-permute-start | bytes 3538952 | tf_op jit(solution)/shard_map/ppermute | solution.py:19
  321.7 25.0 %collective-permute-start.10 = (bf16[128,4608]{1,0:T(8,128)(2,1)}, bf16[128,4608]{1,0:T(8,128)(2,1)}, u32[]{:S(2)}, u32[]{:S(2)}) collective-permute-start(bf16[128,4608]{1,0:T(8,128)(2,1)} %get-tuple-element.459), channel_id=1, source_target_pairs={{32,0},{64,32},{96,64},{128,96},{160,128},{192,160},{224,192},{33,... | collective-permute-start | bytes 3538952 | tf_op jit(solution)/shard_map/ppermute | solution.py:19
  346.8 25.9 %collective-permute-start.11 = (bf16[128,4608]{1,0:T(8,128)(2,1)}, bf16[128,4608]{1,0:T(8,128)(2,1)}, u32[]{:S(2)}, u32[]{:S(2)}) collective-permute-start(bf16[128,4608]{1,0:T(8,128)(2,1)} %get-tuple-element.463), channel_id=1, source_target_pairs={{32,0},{64,32},{96,64},{128,96},{160,128},{192,160},{224,192},{33,... | collective-permute-start | bytes 3538952 | tf_op jit(solution)/shard_map/ppermute | solution.py:19
  372.7 26.2 %collective-permute-start.12 = (bf16[128,4608]{1,0:T(8,128)(2,1)}, bf16[128,4608]{1,0:T(8,128)(2,1)}, u32[]{:S(2)}, u32[]{:S(2)}) collective-permute-start(bf16[128,4608]{1,0:T(8,128)(2,1)} %get-tuple-element.467), channel_id=1, source_target_pairs={{32,0},{64,32},{96,64},{128,96},{160,128},{192,160},{224,192},{33,... | collective-permute-start | bytes 3538952 | tf_op jit(solution)/shard_map/ppermute | solution.py:19
  398.9 146.7 %collective-permute-start.13 = (bf16[128,4608]{1,0:T(8,128)(2,1)}, bf16[128,4608]{1,0:T(8,128)(2,1)S(1)}, u32[]{:S(2)}, u32[]{:S(2)}) collective-permute-start(bf16[128,4608]{1,0:T(8,128)(2,1)} %get-tuple-element.474), channel_id=1, source_target_pairs={{32,0},{64,32},{96,64},{128,96},{160,128},{192,160},{224,192},{33,... | collective-permute-start | bytes 3538952 | tf_op jit(solution)/shard_map/ppermute | solution.py:19
  577.6 199.8 %reduce-scatter.2.cloned.1.call-start = ((), (), s32[]{:S(2)}) async-start(), calls=%async_computation.1 | async-start | bytes 1216512 | tf_op jit(solution)/shard_map/reduce_scatter | solution.py:151
  580.4 0.7 copy-start.12
Sparse Core Ops, SparseCore 0:
  577.7 112.2 all-reduce.2
  693.9 83.4 reduce-scatter.1
where the time goes:
time: 787 us; the launch traced here: 786 us
  waiting for transfers between devices  650 us (83%)
  starting transfers between devices  57.8 us (7%)
  local copies, waits for them, and re-layouts  20.5 us (3%)
  matrix products  17.1 us (2%)
  between operations  15.5 us (2%)
  blocking collectives  15.3 us (2%)
  other arithmetic  8.48 us (1%)
    ppermute x14, waiting for transfers between devices, passed_along(): return lax.ppermute(block, axis, route)  456 us
    unnamed x3, waiting for transfers between devices  108 us
    reduce_scatter x1, waiting for transfers between devices, per_device(): lax.psum_scatter(lax.dot_general(columns, scaled_in, CONTRACT_ROWS, prefe...  85.8 us
    ppermute x14, starting transfers between devices, passed_along(): return lax.ppermute(block, axis, route)  57.7 us
  transfers between devices with their start and end apart: 16, of which 16 were waited for; matrix products, arithmetic and copies ran while one was open for 1% of the time, Pallas kernels for 0%

commit v1 on v0

v1 whole, which is shorter than its diff:
```python
import jax
import jax.numpy as jnp
import numpy as np
from jax import lax
from jax.experimental import pallas as pl
from jax.experimental.pallas import tpu as pltpu
from jax.sharding import Mesh, PartitionSpec as P

EPS = 1e-06
CLIP_NORM = 256.0
CLIP_OFFSET = 0.01
S = 8
R = 128
T = 128
D = 4608
SLICE = D // S
QUARTER = SLICE // 4
Z, Y, X, C = "section", "y", "x", "core"
BF = jnp.bfloat16
F32 = jnp.float32
NN = (((1,), (0,)), ((), ()))
NT = (((1,), (1,)), ((), ()))
GELU_A = 0.7978845608028654
GELU_B = 0.044715
VMEM_LIMIT = 48 * 1024 * 1024


def mm(a, b, dims=NN):
    return lax.dot_general(a, b, dims, preferred_element_type=F32)


def halves(even, odd):
    low = lax.broadcasted_iota(jnp.int32, even.shape, 1) < 4
    return (
        jnp.where(low, even, pltpu.roll(odd, 4, axis=1)),
        jnp.where(low, pltpu.roll(even, 4, axis=1), odd),
    )


def chain_kernel(core_ref, own_ref, oth_ref, proj_ref, sq_ref, h_ref, ht_ref, p_ref, scal_ref, kmat, pre, qacc, hacc, slope):
    first = core_ref[0] == 0

    def place(s, carry):
        cols = pl.ds(pl.multiple_of(s * R, R), R)
        for x in range(4):
            own = [own_ref[s, y, x].astype(F32).reshape(4, 8, R) for y in range(4)]
            oth = [oth_ref[s, y, x].astype(F32).reshape(4, 8, R) for y in range(4)]
            for c in range(2):
                v = [jnp.where(first, a, b) if c == 0 else jnp.where(first, b, a) for a, b in zip(own, oth)]
                e01, o01 = halves(v[0], v[1])
                e23, o23 = halves(v[2], v[3])
                ev = jnp.concatenate([e01, e23], axis=1).astype(BF)
                od = jnp.concatenate([o01, o23], axis=1).astype(BF)
                for i in range(4):
                    row = (x * 2 + c) * 16
                    kmat[2 * i * R + row : 2 * i * R + row + 16, cols] = ev[i]
                    kmat[(2 * i + 1) * R + row : (2 * i + 1) * R + row + 16, cols] = od[i]
        return carry

    lax.fori_loop(0, S, place, 0)
    for s in range(S):
        block = proj_ref[s].astype(F32)
        pre[:, s * R : (s + 1) * R] = block[:, :R]
        qacc[:, s * R : (s + 1) * R] = block[:, R : 2 * R]
        hacc[:, s * R : (s + 1) * R] = block[:, 2 * R :]
    sq = sq_ref[...]
    lane = lax.broadcasted_iota(jnp.int32, (T, R), 1)
    scal = jnp.zeros((T, R), F32)
    inv = []
    for s in range(S):
        here = slice(s * R, (s + 1) * R)
        r = lax.rsqrt(sq * (1.0 / D) + EPS)
        inv.append(r)
        scal = jnp.where(lane == s, r, scal)
        v = pre[:, here] * r
        pre[:, here] = v
        th = jnp.tanh(GELU_A * (v + GELU_B * v * v * v))
        h = (0.5 * v * (1.0 + th)).astype(BF)
        slope[:, here] = 0.5 * (1.0 + th) + 0.5 * v * (1.0 - th * th) * (GELU_A * (1.0 + 3.0 * GELU_B * v * v))
        h_ref[s] = h
        hf = h.astype(F32)
        ht_ref[s] = hf.T.astype(BF)
        if s + 1 < S:
            before = qacc[:, here]
            qacc[:, s * R :] += mm(h, kmat[s * R :, here], NT)
            sq = sq + jnp.sum(hf * (before + qacc[:, here]), axis=1, keepdims=True)
            pre[:, (s + 1) * R :] += mm(h, kmat[here, (s + 1) * R :])
    gam = jnp.zeros((T, 1), F32)
    for s in reversed(range(S)):
        here = slice(s * R, (s + 1) * R)
        hg = hacc[:, here]
        if s + 1 < S:
            hg = hg - gam * qacc[:, here]
        p = (hg * slope[:, here]).astype(BF)
        p_ref[s] = p
        r = inv[s]
        cen = r * r * (jnp.sum(p.astype(F32) * pre[:, here], axis=1, keepdims=True) * (1.0 / D))
        scal = jnp.where(lane == S + s, cen, scal)
        if s > 0:
            upd = r * mm(p, kmat[: s * R, here], NT)
            if s + 1 < S:
                upd = upd - gam * mm(h_ref[s], kmat[here, : s * R])
            hacc[:, : s * R] += upd
        gam = gam + cen
    scal_ref[...] = scal.T[: 2 * S]


def chain(core, own, oth, proj, sq):
    vm = pl.BlockSpec(memory_space=pltpu.VMEM)
    return pl.pallas_call(
        chain_kernel,
        out_shape=(
            jax.ShapeDtypeStruct((S, T, R), BF),
            jax.ShapeDtypeStruct((S, R, T), BF),
            jax.ShapeDtypeStruct((S, T, R), BF),
            jax.ShapeDtypeStruct((2 * S, T), F32),
        ),
        in_specs=[pl.BlockSpec(memory_space=pltpu.SMEM), vm, vm, vm, vm],
        out_specs=(vm, vm, vm, vm),
        scratch_shapes=[
            pltpu.VMEM((S * R, S * R), BF),
            pltpu.VMEM((T, S * R), F32),
            pltpu.VMEM((T, S * R), F32),
            pltpu.VMEM((T, S * R), F32),
            pltpu.VMEM((T, S * R), F32),
        ],
        compiler_params=pltpu.CompilerParams(vmem_limit_bytes=VMEM_LIMIT),
        cost_estimate=pl.CostEstimate(flops=2 * 192 * T * R * R, bytes_accessed=6 << 20, transcendentals=S * T * R),
        name="chain",
    )(core, own, oth, proj, sq)


def grads_kernel(core_ref, wown_ref, woth_ref, xt_ref, ct_ref, ls_ref, h_ref, ht_ref, p_ref, scal_ref, gi_ref, go_ref, sq_ref, xs, gos):
    core = core_ref[0]
    first = core == 0
    total = jnp.zeros((SLICE // 4, R), F32)

    def pick(flip, s):
        a, b = wown_ref[:, s], woth_ref[:, s]
        return (jnp.where(first, b, a) if flip else jnp.where(first, a, b)).reshape(SLICE, R)

    x = xt_ref[...]
    for s in range(S):
        xs[s] = x
        xf = x.astype(F32)
        n = (xf * scal_ref[s : s + 1, :]).astype(BF)
        gi = mm(n, p_ref[s])
        for j in range(4):
            part = gi[j * QUARTER : (j + 1) * QUARTER]
            total = total + part * part
            gi_ref[core ^ (j % 2), s * 2 + j // 2] = part.astype(BF)
        if s + 1 < S:
            x = (xf + mm(pick(True, s), h_ref[s], NT)).astype(BF)
    g = ct_ref[...]
    for s in reversed(range(S)):
        gos[s] = mm(ht_ref[s], g, NT) * ls_ref[s]
        if s > 0:
            m = mm(pick(False, s), p_ref[s], NT)
            g = (g.astype(F32) + scal_ref[s : s + 1, :] * m - scal_ref[S + s : S + s + 1, :] * xs[s].astype(F32)).astype(BF)
    acc = jnp.zeros((R, SLICE), F32)
    for s in range(S):
        acc = acc + gos[s] * gos[s]
    for quad in range(2):
        v = [gos[quad * 4 + i].reshape(16, 8, SLICE) for i in range(4)]
        a0, a1 = halves(v[0], v[1])
        b0, b1 = halves(v[2], v[3])
        go_ref[core, :, quad * 16 : (quad + 1) * 16] = jnp.concatenate([a0, b0], axis=1).astype(BF)
        go_ref[core ^ 1, :, quad * 16 : (quad + 1) * 16] = jnp.concatenate([a1, b1], axis=1).astype(BF)
    one = jnp.sum(jnp.sum(total, axis=0, keepdims=True), axis=1, keepdims=True)
    two = jnp.sum(jnp.sum(acc, axis=0, keepdims=True), axis=1, keepdims=True)
    sq_ref[...] = jnp.broadcast_to(one + two, (8, 128))


def grads(core, wown, woth, xt, ct, ls, h, ht, p, scal):
    vm = pl.BlockSpec(memory_space=pltpu.VMEM)
    return pl.pallas_call(
        grads_kernel,
        out_shape=(
            jax.ShapeDtypeStruct((2, 16, QUARTER, R), BF),
            jax.ShapeDtypeStruct((2, 16, 32, SLICE), BF),
            jax.ShapeDtypeStruct((8, 128), F32),
        ),
        in_specs=[pl.BlockSpec(memory_space=pltpu.SMEM)] + [vm] * 9,
        out_specs=(vm, vm, vm),
        scratch_shapes=[pltpu.VMEM((S, SLICE, T), BF), pltpu.VMEM((S, R, SLICE), F32)],
        compiler_params=pltpu.CompilerParams(vmem_limit_bytes=VMEM_LIMIT),
        cost_estimate=pl.CostEstimate(flops=2 * 32 * SLICE * T * R, bytes_accessed=6 << 20, transcendentals=0),
        name="grads",
    )(core, wown, woth, xt, ct, ls, h, ht, p, scal)


def per_device(inputs, w_in, w_out, layer_scale, cotangent):
    w1 = w_in[0]
    scale = layer_scale[0]
    z, y, x, c = (lax.axis_index(a) for a in (Z, Y, X, C))
    core = c.reshape(1).astype(jnp.int32)
    w2 = (w_out[0].astype(F32) * scale).astype(BF)

    q = (x * 2 + c) * 4 + y
    mine = lax.dynamic_slice_in_dim(w2, q * 4, 4, 0)
    rows = lax.all_to_all(jnp.broadcast_to(mine, (S, 4, D)), Z, 0, 0).reshape(S * 4, D)

    v1 = lax.dynamic_index_in_dim(w1.reshape(S, 4, QUARTER, R), x, 1, keepdims=False)
    v2 = lax.dynamic_index_in_dim(w2.reshape(R, S, 4, QUARTER), x, 2, keepdims=False)
    v2 = jnp.transpose(v2, (1, 2, 0))
    piece = lax.all_to_all(jnp.where(c == 0, v1, v2), Z, 0, 0)
    wown = lax.all_gather(piece, X, axis=0)
    woth = lax.ppermute(wown, C, [(0, 1), (1, 0)])
    ls = lax.all_to_all(scale.reshape(S, 1, SLICE), Z, 0, 0)

    proj = jnp.concatenate([mm(inputs, w1), mm(inputs, w2, NT), mm(cotangent, w2, NT)], axis=1).astype(BF)
    proj = lax.all_to_all(jnp.broadcast_to(proj, (S, T, 3 * R)), Z, 0, 0)
    wide = inputs.astype(F32)
    sq = jnp.sum(wide * wide, axis=1, keepdims=True)
    xt = lax.dynamic_slice_in_dim(inputs, z * SLICE, SLICE, 1).T
    ct = lax.dynamic_slice_in_dim(cotangent, z * SLICE, SLICE, 1).T

    below = (lax.broadcasted_iota(jnp.int32, (S * 4, R), 0) // 4) < z
    kpart = jnp.where(below, mm(rows, w1), mm(rows, w2, NT)).astype(BF)
    kown = lax.all_to_all(jnp.broadcast_to(kpart, (S * 16, S * 4, R)), (Z, Y, X), 0, 0)
    koth = lax.ppermute(kown, C, [(0, 1), (1, 0)])
    h, ht, p, scal = chain(
        core, kown.reshape(S, 4, 4, S * 4, R), koth.reshape(S, 4, 4, S * 4, R), proj, sq
    )

    gi, go, part = grads(core, wown, woth, xt, ct, ls, h, ht, p, scal)
    swap = [(0, 1), (1, 0)]
    total = lax.psum(part[:1, :1], Z)
    factor = CLIP_NORM / (jnp.sqrt(total) + CLIP_OFFSET)
    other = lax.ppermute(factor, C, swap)
    gi_got = lax.ppermute(gi[1], C, swap)
    go_got = lax.ppermute(go[1], C, swap)
    gi_sum = (gi[0].astype(F32) * factor + gi_got.astype(F32) * other).astype(BF)
    go_sum = (go[0].astype(F32) * factor + go_got.astype(F32) * other).astype(BF)

    gi_all = lax.all_to_all(gi_sum, (Y, X), 0, 0)
    go_all = lax.all_to_all(go_sum, (Y, X), 0, 0)
    gi_row = jnp.sum(gi_all.astype(F32), axis=0).astype(BF)
    route = [(k * 32 + s * 4 + j, s * 32 + k * 4 + j) for k in range(S) for s in range(S) for j in range(4)]
    grad_in = lax.ppermute(gi_row, (Z, Y, X, C), route).astype(F32)
    go_row = jnp.sum(go_all.astype(F32), axis=0).astype(BF).reshape(S, 4, SLICE)
    grad_out = lax.all_to_all(go_row, Z, 0, 0).astype(F32)
    grad_out = jnp.transpose(grad_out, (1, 0, 2)).reshape(4, D)
    return grad_in[None], grad_out[None]


def solution(mesh):
    split = Mesh(np.asarray(mesh.devices).reshape(S, 4, 4, 2), (Z, Y, X, C))
    dp = (Y, X, C)
    return jax.shard_map(
        per_device,
        mesh=split,
        in_specs=(P(dp, None), P(Z, None, None), P(Z, None, None), P(Z, None), P(dp, None)),
        out_specs=(P(Z, dp, None), P(Z, dp, None)),
        check_vma=False,
    )
```

time: 787 us -> 216 us (0.27)
  waiting for transfers between devices: 650 us -> 78.5 us
  matrix products: 17.1 us -> 5.05 us
  starting transfers between devices: 57.8 us -> 47 us
  Pallas kernels: 0 us -> 8.74 us
    ppermute x14 -> x6, waiting for transfers between devices: 456 us -> 0.29 us  [the longest x1 0.27 us: per_device(): other = lax.ppermute(factor, C, swap)]
    unnamed x3 -> x1, waiting for transfers between devices: 108 us -> 0.68 us
    reduce_scatter x1 -> x0, waiting for transfers between devices: 85.8 us -> none  [per_device(): lax.psum_scatter(lax.dot_general(columns, scaled_in, CONTRACT_ROWS, prefe...]
    all_to_all x0 -> x8, waiting for transfers between devices: none -> 77.5 us  [the longest x1 23.8 us: per_device(): lax.all_to_all(jnp.broadcast_to(kpart, (S * 16, S * 4, R)), (Z, Y, X), 0, 0)]
    ppermute x14 -> x6, starting transfers between devices: 57.7 us -> 2.67 us  [the longest x1 0.91 us: per_device(): other = lax.ppermute(factor, C, swap)]
    all_to_all x0 -> x8, starting transfers between devices: none -> 44.2 us  [the longest x1 8.95 us: per_device(): lax.all_to_all(jnp.broadcast_to(kpart, (S * 16, S * 4, R)), (Z, Y, X), 0, 0)]
    cond x6 -> x0, local copies, waits for them, and re-layouts: 14.2 us -> none
    dot_general x9 -> x5, matrix products: 17.1 us -> 5.05 us  [mm(): return lax.dot_general(a, b, dims, preferred_element_type=F32)]
  transfers between devices with their start and end apart: 16 -> 15, of which waited for: 16 -> 8; matrix products, arithmetic and copies ran while one was open for 1% -> 12% of each run, Pallas kernels for 0% -> 3%
where the time goes in v1:
time: 216 us; the launch traced here: 213 us
  waiting for transfers between devices  78.5 us (36%)
  starting transfers between devices  47 us (22%)
  local copies, waits for them, and re-layouts  28.3 us (13%)
  blocking collectives  17.7 us (8%)
  between operations  15 us (7%)
  other arithmetic  12.5 us (6%)
  Pallas kernels  8.74 us (4%)
  matrix products  5.05 us (2%)
    all_to_all x1, waiting for transfers between devices, per_device(): lax.all_to_all(jnp.broadcast_to(kpart, (S * 16, S * 4, R)), (Z, Y, X), 0, 0)  23.8 us
    psum x1, blocking collectives, per_device(): total = lax.psum(part[:1, :1], Z)  17.7 us
    unnamed x35, local copies, waits for them, and re-layouts  12.8 us
    all_to_all x1, waiting for transfers between devices, per_device(): proj = lax.all_to_all(jnp.broadcast_to(proj, (S, T, 3 * R)), Z, 0, 0)  12.4 us
    all_to_all x1, waiting for transfers between devices, per_device(): go_all = lax.all_to_all(go_sum, (Y, X), 0, 0)  10.2 us
    all_to_all x1, waiting for transfers between devices, per_device(): gi_all = lax.all_to_all(gi_sum, (Y, X), 0, 0)  9.58 us
    all_to_all x1, starting transfers between devices, per_device(): lax.all_to_all(jnp.broadcast_to(kpart, (S * 16, S * 4, R)), (Z, Y, X), 0, 0)  8.95 us
    all_to_all x1, starting transfers between devices, per_device(): lax.all_to_all(jnp.broadcast_to(mine, (S, 4, D)), Z, 0, 0).reshape(S * 4, D)  8.47 us
  transfers between devices with their start and end apart: 15, of which 8 were waited for; matrix products, arithmetic and copies ran while one was open for 12% of the time, Pallas kernels for 3%

profile of v1, /device:TPU:2, one launch (start us, length us, event | category | flops | bytes accessed | tf_op | source)
XLA Modules:
  0.0 212.8 jit_solution(9072854439362977836)
XLA Ops:
  7.2 1.7 copy.26
  9.0 0.6 copy-done.12
  9.6 1.9 fusion
  11.5 0.4 constant_dynamic-slice_fusion
  11.9 1.0 copy.29
  13.0 1.6 broadcast_in_dim.22
  14.5 8.5 %all-to-all-start.2 = ((bf16[8,4,4608]{2,1,0:T(4,128)(2,1)}), bf16[8,4,4608]{2,1,0:T(4,128)(2,1)}, u32[]{:S(2)}, u32[]{:S(2)}) async-start(bf16[8,4,4608]{2,1,0:T(4,128)(2,1)} %broadcast_in_dim.22), calls=%async_computation.2 | async-start | bytes 589824 | tf_op jit(solution)/shard_map/all_to_all | solution.py:201
  23.0 1.4 mul.80
  24.4 1.6 convert.30
  26.1 0.8 constant_dynamic-slice_fusion.3
  26.9 2.0 fusion.25
  28.9 6.8 %all-to-all-done.2 = bf16[8,4,4608]{2,1,0:T(4,128)(2,1)} async-done(((bf16[8,4,4608]{2,1,0:T(4,128)(2,1)}), bf16[8,4,4608]{2,1,0:T(4,128)(2,1)}, u32[]{:S(2)}, u32[]{:S(2)}) %all-to-all-start.2) | async-done | bytes 294944 | tf_op jit(solution)/shard_map/all_to_all | solution.py:201
  35.7 4.1 %all-to-all-start = ((bf16[8,144,128]{2,1,0:T(8,128)(2,1)}), bf16[8,144,128]{2,1,0:T(8,128)(2,1)}, u32[]{:S(2)}, u32[]{:S(2)}) async-start(bf16[8,144,128]{2,1,0:T(8,128)(2,1)} %fusion.25), calls=%async_computation | async-start | bytes 589824 | tf_op jit(solution)/shard_map/all_to_all | solution.py:206
  39.7 1.7 reshape.46
  41.5 1.8 fusion.3
  43.3 0.3 fusion.20
  43.7 7.2 %all-to-all-done = bf16[8,144,128]{2,1,0:T(8,128)(2,1)} async-done(((bf16[8,144,128]{2,1,0:T(8,128)(2,1)}), bf16[8,144,128]{2,1,0:T(8,128)(2,1)}, u32[]{:S(2)}, u32[]{:S(2)}) %all-to-all-start) | async-done | bytes 294944 | tf_op jit(solution)/shard_map/all_to_all | solution.py:206
  50.9 1.1 broadcast_in_dim.23
  52.0 8.9 %all-to-all-start.3 = ((bf16[128,32,128]{2,1,0:T(8,128)(2,1)}), bf16[128,32,128]{2,1,0:T(8,128)(2,1)S(1)}, u32[]{:S(2)}, u32[]{:S(2)}) async-start(bf16[128,32,128]{2,1,0:T(8,128)(2,1)} %broadcast_in_dim.23), calls=%async_computation.3 | async-start | bytes 2097152 | tf_op jit(solution)/shard_map/all_to_all | solution.py:220
  61.0 0.7 all-gather.3.cloned.1.call-update
  61.7 1.9 fusion.12
  63.6 0.5 fusion.15
  64.1 0.7 copy-done.11
  64.9 0.5 fusion.16
  65.5 23.8 %all-to-all-done.3 = bf16[128,32,128]{2,1,0:T(8,128)(2,1)S(1)} async-done(((bf16[128,32,128]{2,1,0:T(8,128)(2,1)}), bf16[128,32,128]{2,1,0:T(8,128)(2,1)S(1)}, u32[]{:S(2)}, u32[]{:S(2)}) %all-to-all-start.3) | async-done | bytes 1048608 | tf_op jit(solution)/shard_map/all_to_all | solution.py:220
  89.3 1.0 broadcast_in_dim.24
  90.3 3.5 %all-to-all-start.4 = ((bf16[8,128,384]{2,1,0:T(8,128)(2,1)}), bf16[8,128,384]{2,1,0:T(8,128)(2,1)S(1)}, u32[]{:S(2)}, u32[]{:S(2)}) async-start(bf16[8,128,384]{2,1,0:T(8,128)(2,1)} %broadcast_in_dim.24), calls=%async_computation.4 | async-start | bytes 1572864 | tf_op jit(solution)/shard_map/all_to_all | solution.py:212
  94.0 0.5 collective-permute-start.1
  94.5 0.7 reshape_squeeze.7
  95.2 1.6 multiply_reduce_fusion
  96.9 1.9 constant_dynamic-slice_fusion.1
  98.9 1.1 copy.34
  99.9 12.4 %all-to-all-done.4.proj_ref = bf16[8,128,384]{2,1,0:T(8,128)(2,1)S(1)} async-done(((bf16[8,128,384]{2,1,0:T(8,128)(2,1)}), bf16[8,128,384]{2,1,0:T(8,128)(2,1)S(1)}, u32[]{:S(2)}, u32[]{:S(2)}) %all-to-all-start.4) | async-done | bytes 786464 | tf_op jit(solution)/shard_map/all_to_all | solution.py:212
  112.4 3.5 %all-to-all-start.1 = ((f32[8,1,576]{2,1,0:T(1,128)}), f32[8,1,576]{2,1,0:T(1,128)S(1)}, u32[]{:S(2)}, u32[]{:S(2)}) async-start(f32[8,1,576]{2,1,0:T(1,128)} %reshape_squeeze.7), calls=%async_computation.1 | async-start | bytes 40960 | tf_op jit(solution)/shard_map/all_to_all | solution.py:209
  115.9 5.8 %chain.1 = (bf16[8,128,128]{2,1,0:T(8,128)(2,1)S(1)}, bf16[8,128,128]{2,1,0:T(8,128)(2,1)S(1)}, bf16[8,128,128]{2,1,0:T(8,128)(2,1)S(1)}, f32[16,128]{1,0:T(8,128)S(1)}) custom-call(s32[1]{0:T(128)} %bitcast.core_ref, bf16[8,4,4,32,128]{4,3,2,1,0:T(8,128)(2,1)S(1)} %bitcast.70, bf16[8,4,4,32,128]{4,3,2,1,0:T(8,128)(2,1)} %bitcast.13.oth_ref, ...), custom_call_target="tpu_custom_call" | custom-call | flops 805306368 | bytes 6291456 | tf_op jit(solution)/shard_map/chain/pallas_call | solution.py:110
  121.7 0.7 copy-done.3
  122.4 0.7 copy-done.5
  123.1 0.7 copy-done.7
  123.8 1.0 copy-done.1
  124.8 1.3 copy-done
  126.1 1.3 copy-done.2
  127.4 0.9 copy-done.4
  128.3 0.9 copy-done.6
  129.3 0.9 copy-done.8
  130.2 3.0 %grads.1 = (bf16[2,16,144,128]{3,2,1,0:T(8,128)(2,1)S(1)}, bf16[2,16,32,576]{3,2,1,0:T(8,128)(2,1)S(1)}, f32[8,128]{1,0:T(8,128)S(1)}) custom-call(s32[1]{0:T(128)} %bitcast.core_ref, bf16[4,8,144,128]{3,2,1,0:T(8,128)(2,1)S(1)} %bitcast.69, bf16[4,8,144,128]{3,2,1,0:T(8,128)(2,1)S(1)} %copy-done.2, bf16[576,128]{1,0:T(8,128)(2,1)S(1)} %bitcast.72, ...), custom_call_target="tpu_custom_call" | custom-call | flops 603979776 | bytes 6291456 | tf_op jit(solution)/shard_map/grads/pallas_call | solution.py:176
  133.2 0.9 slice_bitcast_fusion.1
  134.1 0.9 slice_bitcast_fusion
  135.0 0.5 collective-permute-start.5
  135.5 0.5 slice.16
  136.0 17.7 %psum.7 = f32[1,1]{1,0:T(1,128)} all-reduce(f32[1,1]{1,0:T(1,128)} %slice.16), channel_id=1, replica_groups=mesh['section'=8,'y'=4,'x'=4,'core'=2] {'section'}, use_global_device_ids=true, to_apply=%region_1.2 | all-reduce | flops 1 | bytes 8 | tf_op jit(solution)/shard_map/psum | solution.py:228
  154.5 0.9 collective-permute-start.3
  155.4 0.3 collective-permute-done.3
  155.7 2.7 %fusion.5 = bf16[16,144,128]{2,1,0:T(8,128)(2,1)} fusion(bf16[16,144,128]{2,1,0:T(8,128)(2,1)} %collective-permute-done.2, f32[]{:T(128)} %bitcast.20, f32[]{:T(128)} %bitcast.17, bf16[2,16,144,128]{3,2,1,0:T(8,128)(2,1)S(1)} %get-tuple-element.13), kind=kLoop, calls=%fused_computation.9 | loop fusion | flops 1769472 | bytes 1769480 | tf_op jit(solution)/shard_map/convert_element_type | solution.py:233
  158.4 5.7 %all-to-all-start.5 = ((bf16[16,144,128]{2,1,0:T(8,128)(2,1)}), bf16[16,144,128]{2,1,0:T(8,128)(2,1)S(1)}, u32[]{:S(2)}, u32[]{:S(2)}) async-start(bf16[16,144,128]{2,1,0:T(8,128)(2,1)} %fusion.5), calls=%async_computation.5 | async-start | bytes 1179648 | tf_op jit(solution)/shard_map/all_to_all | solution.py:236
  164.1 1.7 fusion.1
  165.8 9.6 %all-to-all-done.5 = bf16[16,144,128]{2,1,0:T(8,128)(2,1)S(1)} async-done(((bf16[16,144,128]{2,1,0:T(8,128)(2,1)}), bf16[16,144,128]{2,1,0:T(8,128)(2,1)S(1)}, u32[]{:S(2)}, u32[]{:S(2)}) %all-to-all-start.5) | async-done | bytes 589856 | tf_op jit(solution)/shard_map/all_to_all | solution.py:236
  175.3 4.8 %all-to-all-start.6 = ((bf16[16,32,576]{2,1,0:T(8,128)(2,1)}), bf16[16,32,576]{2,1,0:T(8,128)(2,1)S(1)}, u32[]{:S(2)}, u32[]{:S(2)}) async-start(bf16[16,32,576]{2,1,0:T(8,128)(2,1)} %fusion.1), calls=%async_computation.6 | async-start | bytes 1310720 | tf_op jit(solution)/shard_map/all_to_all | solution.py:237
  180.3 0.7 collective-permute-start.4
  180.9 10.2 %all-to-all-done.6 = bf16[16,32,576]{2,1,0:T(8,128)(2,1)S(1)} async-done(((bf16[16,32,576]{2,1,0:T(8,128)(2,1)}), bf16[16,32,576]{2,1,0:T(8,128)(2,1)S(1)}, u32[]{:S(2)}, u32[]{:S(2)}) %all-to-all-start.6) | async-done | bytes 589856 | tf_op jit(solution)/shard_map/all_to_all | solution.py:237
  191.3 0.6 reshape.49
  191.9 5.2 %all-to-all-start.7 = ((bf16[8,4,576]{2,1,0:T(4,128)(2,1)}), bf16[8,4,576]{2,1,0:T(4,128)(2,1)S(1)}, u32[]{:S(2)}, u32[]{:S(2)}) async-start(bf16[8,4,576]{2,1,0:T(4,128)(2,1)} %reshape.49), calls=%async_computation.7 | async-start | bytes 81920 | tf_op jit(solution)/shard_map/all_to_all | solution.py:242
  197.1 0.6 bitcast_convert_fusion
  197.7 7.5 %all-to-all-done.7 = bf16[8,4,576]{2,1,0:T(4,128)(2,1)S(1)} async-done(((bf16[8,4,576]{2,1,0:T(4,128)(2,1)}), bf16[8,4,576]{2,1,0:T(4,128)(2,1)S(1)}, u32[]{:S(2)}, u32[]{:S(2)}) %all-to-all-start.7) | async-done | bytes 36896 | tf_op jit(solution)/shard_map/all_to_all | solution.py:242
  205.2 0.7 reshape.53
  (42 shorter events, 0.9 us)
Async XLA Ops:
  7.2 1.7 copy-start.15
  9.0 0.6 copy-start.12
  14.5 21.1 %all-to-all-start.2 = ((bf16[8,4,4608]{2,1,0:T(4,128)(2,1)}), bf16[8,4,4608]{2,1,0:T(4,128)(2,1)}, u32[]{:S(2)}, u32[]{:S(2)}) async-start(bf16[8,4,4608]{2,1,0:T(4,128)(2,1)} %broadcast_in_dim.22), calls=%async_computation.2 | async-start | bytes 589824 | tf_op jit(solution)/shard_map/all_to_all | solution.py:201
  24.4 2.4 %copy-start.10 = (bf16[1,4608,128]{2,1,0:T(8,128)(2,1)S(1)}, bf16[1,4608,128]{2,1,0:T(8,128)(2,1)}, u32[]{:S(2)}) copy-start(bf16[1,4608,128]{2,1,0:T(8,128)(2,1)} %param.6) | copy-start | bytes 3538948
  35.7 15.2 %all-to-all-start = ((bf16[8,144,128]{2,1,0:T(8,128)(2,1)}), bf16[8,144,128]{2,1,0:T(8,128)(2,1)}, u32[]{:S(2)}, u32[]{:S(2)}) async-start(bf16[8,144,128]{2,1,0:T(8,128)(2,1)} %fusion.25), calls=%async_computation | async-start | bytes 589824 | tf_op jit(solution)/shard_map/all_to_all | solution.py:206
  41.5 1.9 copy-start.14
  52.0 9.7 %copy-start.9 = (bf16[128,4608]{1,0:T(8,128)(2,1)S(1)}, bf16[128,4608]{1,0:T(8,128)(2,1)}, u32[]{:S(2)}) copy-start(bf16[128,4608]{1,0:T(8,128)(2,1)} %param.5) | copy-start | bytes 3538948
  52.0 37.3 %all-to-all-start.3 = ((bf16[128,32,128]{2,1,0:T(8,128)(2,1)}), bf16[128,32,128]{2,1,0:T(8,128)(2,1)S(1)}, u32[]{:S(2)}, u32[]{:S(2)}) async-start(bf16[128,32,128]{2,1,0:T(8,128)(2,1)} %broadcast_in_dim.23), calls=%async_computation.3 | async-start | bytes 2097152 | tf_op jit(solution)/shard_map/all_to_all | solution.py:220
  61.0 32.9 %all-gather.3.cloned.1.call-start = ((), (), s32[]{:S(2)}) async-start(), calls=%async_computation.8 | async-start | bytes 1474560 | tf_op jit(solution)/shard_map/all_gather | solution.py:207
  63.6 1.3 copy-start.11
  65.5 29.0 %copy-start.13 = (f32[4608]{0:T(1024)S(1)}, f32[4608]{0:T(1024)}, u32[]{:S(2)}) copy-start(f32[4608]{0:T(1024)} %copy-done.12) | copy-start | bytes 55300
  90.3 22.1 %all-to-all-start.4 = ((bf16[8,128,384]{2,1,0:T(8,128)(2,1)}), bf16[8,128,384]{2,1,0:T(8,128)(2,1)S(1)}, u32[]{:S(2)}, u32[]{:S(2)}) async-start(bf16[8,128,384]{2,1,0:T(8,128)(2,1)} %broadcast_in_dim.24), calls=%async_computation.4 | async-start | bytes 1572864 | tf_op jit(solution)/shard_map/all_to_all | solution.py:212
  93.9 29.9 %collective-permute-start = (bf16[4,8,144,128]{3,2,1,0:T(8,128)(2,1)}, bf16[4,8,144,128]{3,2,1,0:T(8,128)(2,1)S(1)}, u32[]{:S(2)}, u32[]{:S(2)}) collective-permute-start(bf16[4,8,144,128]{3,2,1,0:T(8,128)(2,1)} %bitcast.68), channel_id=1, source_target_pairs={{0,1},{1,0},{2,3},{3,2},{4,5},{5,4},{6,7},{7,6},{8,9},{9,8},{10,11... | collective-permute-start | bytes 3538952 | tf_op jit(solution)/shard_map/ppermute | solution.py:208
  94.0 21.9 %collective-permute-start.1 = (bf16[128,32,128]{2,1,0:T(8,128)(2,1)S(1)}, bf16[128,32,128]{2,1,0:T(8,128)(2,1)}, u32[]{:S(2)}, u32[]{:S(2)}) collective-permute-start(bf16[128,32,128]{2,1,0:T(8,128)(2,1)S(1)} %all-to-all-done.3), channel_id=1, source_target_pairs={{0,1},{1,0},{2,3},{3,2},{4,5},{5,4},{6,7},{7,6},{8,9},{9,8},{10,11... | collective-permute-start | bytes 3145736 | tf_op jit(solution)/shard_map/ppermute | solution.py:221
  112.4 11.4 %all-to-all-start.1 = ((f32[8,1,576]{2,1,0:T(1,128)}), f32[8,1,576]{2,1,0:T(1,128)S(1)}, u32[]{:S(2)}, u32[]{:S(2)}) async-start(f32[8,1,576]{2,1,0:T(1,128)} %reshape_squeeze.7), calls=%async_computation.1 | async-start | bytes 40960 | tf_op jit(solution)/shard_map/all_to_all | solution.py:209
  121.7 0.7 copy-start.3
  122.4 0.7 copy-start.5
  123.1 0.7 copy-start.7
  123.8 1.0 copy-start.1
  124.8 1.3 copy-start
  126.1 1.3 copy-start.2
  127.4 0.9 copy-start.4
  128.3 0.9 copy-start.6
  129.3 0.9 copy-start.8
  134.1 21.6 %collective-permute-start.2 = (bf16[16,144,128]{2,1,0:T(8,128)(2,1)}, bf16[16,144,128]{2,1,0:T(8,128)(2,1)}, u32[]{:S(2)}, u32[]{:S(2)}) collective-permute-start(bf16[16,144,128]{2,1,0:T(8,128)(2,1)} %slice_bitcast_fusion.1), channel_id=1, source_target_pairs={{0,1},{1,0},{2,3},{3,2},{4,5},{5,4},{6,7},{7,6},{8,9},{9,8},{10,11... | collective-permute-start | bytes 1769480 | tf_op jit(solution)/shard_map/ppermute | solution.py:231
  135.0 29.1 %collective-permute-start.5 = (bf16[16,32,576]{2,1,0:T(8,128)(2,1)}, bf16[16,32,576]{2,1,0:T(8,128)(2,1)S(1)}, u32[]{:S(2)}, u32[]{:S(2)}) collective-permute-start(bf16[16,32,576]{2,1,0:T(8,128)(2,1)} %slice_bitcast_fusion), channel_id=1, source_target_pairs={{0,1},{1,0},{2,3},{3,2},{4,5},{5,4},{6,7},{7,6},{8,9},{9,8},{10,11... | collective-permute-start | bytes 1769480 | tf_op jit(solution)/shard_map/ppermute | solution.py:232
  154.5 1.2 collective-permute-start.3
  158.4 17.0 %all-to-all-start.5 = ((bf16[16,144,128]{2,1,0:T(8,128)(2,1)}), bf16[16,144,128]{2,1,0:T(8,128)(2,1)S(1)}, u32[]{:S(2)}, u32[]{:S(2)}) async-start(bf16[16,144,128]{2,1,0:T(8,128)(2,1)} %fusion.5), calls=%async_computation.5 | async-start | bytes 1179648 | tf_op jit(solution)/shard_map/all_to_all | solution.py:236
  175.3 15.8 %all-to-all-start.6 = ((bf16[16,32,576]{2,1,0:T(8,128)(2,1)}), bf16[16,32,576]{2,1,0:T(8,128)(2,1)S(1)}, u32[]{:S(2)}, u32[]{:S(2)}) async-start(bf16[16,32,576]{2,1,0:T(8,128)(2,1)} %fusion.1), calls=%async_computation.6 | async-start | bytes 1310720 | tf_op jit(solution)/shard_map/all_to_all | solution.py:237
  180.3 16.8 %collective-permute-start.4 = (bf16[144,128]{1,0:T(8,128)(2,1)S(1)}, bf16[144,128]{1,0:T(8,128)(2,1)S(1)}, u32[]{:S(2)}, u32[]{:S(2)}) collective-permute-start(bf16[144,128]{1,0:T(8,128)(2,1)S(1)} %reduce_sum.34), channel_id=1, source_target_pairs={{0,0},{1,1},{2,2},{3,3},{4,32},{5,33},{6,34},{7,35},{8,64},{9,65},... | collective-permute-start | bytes 110600 | tf_op jit(solution)/shard_map/ppermute | solution.py:240
  191.9 13.3 %all-to-all-start.7 = ((bf16[8,4,576]{2,1,0:T(4,128)(2,1)}), bf16[8,4,576]{2,1,0:T(4,128)(2,1)S(1)}, u32[]{:S(2)}, u32[]{:S(2)}) async-start(bf16[8,4,576]{2,1,0:T(4,128)(2,1)} %reshape.49), calls=%async_computation.7 | async-start | bytes 81920 | tf_op jit(solution)/shard_map/all_to_all | solution.py:242
Sparse Core Ops, SparseCore 0:
  63.6 29.0 all-gather.2

commit v2 on v1

v2 whole, which is shorter than its diff:
```python
import jax
import jax.numpy as jnp
import numpy as np
from jax import lax
from jax.experimental import pallas as pl
from jax.experimental.pallas import tpu as pltpu
from jax.sharding import Mesh, PartitionSpec as P

EPS = 1e-06
CLIP_NORM = 256.0
CLIP_OFFSET = 0.01
S = 8
R = 128
T = 128
D = 4608
SLICE = D // S
QUARTER = SLICE // 4
Z, Y, X, C = "section", "y", "x", "core"
BF = jnp.bfloat16
F32 = jnp.float32
NN = (((1,), (0,)), ((), ()))
NT = (((1,), (1,)), ((), ()))
GELU_A = 0.7978845608028654
GELU_B = 0.044715
VMEM_LIMIT = 48 * 1024 * 1024
HALF = D // 2
ROWS = D * 4 // R
VM = pl.BlockSpec(memory_space=pltpu.VMEM)
SM = pl.BlockSpec(memory_space=pltpu.SMEM)


def mm(a, b, dims=NN):
    return lax.dot_general(a, b, dims, preferred_element_type=F32)


def halves(even, odd):
    low = lax.broadcasted_iota(jnp.int32, even.shape, 1) < 4
    return (
        jnp.where(low, even, pltpu.roll(odd, 4, axis=1)),
        jnp.where(low, pltpu.roll(even, 4, axis=1), odd),
    )


def call(kernel, name, outs, ins, scratch=(), flops=0, size=1 << 21, trans=0):
    return pl.pallas_call(
        kernel,
        out_shape=tuple(jax.ShapeDtypeStruct(*o) for o in outs),
        in_specs=list(ins),
        out_specs=(VM,) * len(outs),
        scratch_shapes=list(scratch),
        compiler_params=pltpu.CompilerParams(vmem_limit_bytes=VMEM_LIMIT),
        cost_estimate=pl.CostEstimate(flops=flops, bytes_accessed=size, transcendentals=trans),
        name=name,
    )


def pack_kernel(at_ref, w_in_ref, w_out_ref, ls_ref, w2_ref, pay_ref, turned):
    x, core, q = at_ref[1], at_ref[2], at_ref[3]
    ls = ls_ref[...]
    w2 = (w_out_ref[...].astype(F32) * ls).astype(BF)
    w2_ref[...] = w2
    row = lax.broadcasted_iota(jnp.int32, (8, R), 0) % 4
    col = lax.broadcasted_iota(jnp.int32, (8, R), 1)
    mine = mm((col == q * 4 + row).astype(BF), w2)
    low = lax.broadcasted_iota(jnp.int32, (8, HALF), 0) < 4
    mine = jnp.where(low, mine[:, :HALF], mine[:, HALF:])
    for u in range(9):
        two = jnp.concatenate([mine[:, 256 * u : 256 * u + R], mine[:, 256 * u + R : 256 * (u + 1)]], axis=0).astype(BF)
        for k in range(S):
            pay_ref[k, 16 * u : 16 * u + 16] = two
    top = ls.astype(BF).astype(F32)
    low_part = ls - top
    for k in range(S):
        rows = []
        for part in (top, low_part):
            rows += [part[:, SLICE * k + R * j : SLICE * k + R * (j + 1)] for j in range(4)]
            tail = part[:, SLICE * k + 512 : SLICE * (k + 1)]
            rows.append(jnp.concatenate([tail, tail], axis=1))
        rows.append(jnp.zeros((6, R), F32))
        pay_ref[k, 2 * ROWS : 2 * ROWS + 16] = jnp.concatenate(rows, axis=0).astype(BF)

    @pl.when(core == 0)
    def _():
        for k in range(S):
            start = pl.multiple_of(SLICE * k + QUARTER * x, 16)
            pay_ref[k, ROWS : 2 * ROWS] = w_in_ref[pl.ds(start, QUARTER), :]

    @pl.when(core != 0)
    def _():
        for t in range(D // R):
            turned[t * R : (t + 1) * R, :] = w2_ref[:, t * R : (t + 1) * R].astype(F32).T.astype(BF)
        for k in range(S):
            start = pl.multiple_of(SLICE * k + QUARTER * x, 16)
            pay_ref[k, ROWS : 2 * ROWS] = turned[pl.ds(start, QUARTER), :]


def project_kernel(at_ref, x_ref, c_ref, w_in_ref, w2_ref, proj_ref, sq_ref, xt_ref, ct_ref, wide):
    z = at_ref[0]
    xv = x_ref[...]
    w2 = w2_ref[...]
    proj_ref[:, :R] = mm(xv, w_in_ref[...]).astype(BF)
    proj_ref[:, R : 2 * R] = mm(xv, w2, NT).astype(BF)
    proj_ref[:, 2 * R : 3 * R] = mm(c_ref[...], w2, NT).astype(BF)
    proj_ref[:, 3 * R :] = jnp.zeros((T, R), BF)
    xf = xv.astype(F32)
    sq_ref[...] = jnp.sum(xf * xf, axis=1, keepdims=True)
    base = pl.multiple_of(((z * 9) // 2) * R, R)
    off = pl.multiple_of((z % 2) * 64, 16)
    for src, dst in ((x_ref, xt_ref), (c_ref, ct_ref)):
        for t in range(5):
            wide[t * R : (t + 1) * R, :] = src[:, pl.ds(base + t * R, R)].astype(F32).T.astype(BF)
        dst[...] = wide[pl.ds(off, SLICE), :]


def gram_kernel(at_ref, got_ref, w_in_ref, w2_ref, out_ref):
    z = at_ref[0]
    first, second = [], []
    for u in range(9):
        block = got_ref[:, 16 * u : 16 * u + 16, :].astype(F32)
        for part in (block[:, :8], block[:, 8:]):
            part = part.reshape(4, 2, 8, R)
            a, b = halves(part[:, 0], part[:, 1])
            first.append(a.reshape(32, R).astype(BF))
            second.append(b.reshape(32, R).astype(BF))
    first = jnp.concatenate(first, axis=1)
    second = jnp.concatenate(second, axis=1)
    up = mm(first, w_in_ref[:HALF]) + mm(second, w_in_ref[HALF:])
    down = mm(first, w2_ref[:, :HALF], NT) + mm(second, w2_ref[:, HALF:], NT)
    below = (lax.broadcasted_iota(jnp.int32, (32, R), 0) // 4) < z
    out = jnp.where(below, up, down).astype(BF)
    for k in range(S):
        out_ref[k] = out


def main_kernel(at_ref, own_ref, oth_ref, proj_ref, sq_ref, wown_ref, woth_ref, xt_ref, ct_ref, ls_ref, gown_ref, goth_ref, norm_ref, kmat, pre, qacc, hacc, slope, hs, hts, ps, sts, wbuf, xs, gos, sem):
    xpos, core = at_ref[1], at_ref[2]
    is0 = core == 0
    copies = []
    for i in range(4):
        slot = (xpos + 4 - i) % 4
        for n, (ref, half) in enumerate(((wown_ref, core), (woth_ref, 1 - core))):
            copies.append(pltpu.make_async_copy(ref.at[i], wbuf.at[half, slot], sem.at[i * 2 + n]))
    for cp in copies:
        cp.start()

    def place(s, carry):
        cols = pl.ds(pl.multiple_of(s * R, R), R)
        for x in range(4):
            own = [own_ref[y * 4 + x, s].astype(F32).reshape(4, 8, R) for y in range(4)]
            oth = [oth_ref[y * 4 + x, s].astype(F32).reshape(4, 8, R) for y in range(4)]
            for c in range(2):
                v = [jnp.where(is0, a, b) if c == 0 else jnp.where(is0, b, a) for a, b in zip(own, oth)]
                e01, o01 = halves(v[0], v[1])
                e23, o23 = halves(v[2], v[3])
                ev = jnp.concatenate([e01, e23], axis=1).astype(BF)
                od = jnp.concatenate([o01, o23], axis=1).astype(BF)
                for i in range(4):
                    row = (x * 2 + c) * 16
                    kmat[2 * i * R + row : 2 * i * R + row + 16, cols] = ev[i]
                    kmat[(2 * i + 1) * R + row : (2 * i + 1) * R + row + 16, cols] = od[i]
        return carry

    lax.fori_loop(0, S, place, 0)
    for s in range(S):
        block = proj_ref[s].astype(F32)
        pre[:, s * R : (s + 1) * R] = block[:, :R]
        qacc[:, s * R : (s + 1) * R] = block[:, R : 2 * R]
        hacc[:, s * R : (s + 1) * R] = block[:, 2 * R : 3 * R]
    sq = sq_ref[...]
    lane = lax.broadcasted_iota(jnp.int32, (T, R), 1)
    scal = jnp.zeros((T, R), F32)
    inv = []
    for s in range(S):
        here = slice(s * R, (s + 1) * R)
        r = lax.rsqrt(sq * (1.0 / D) + EPS)
        inv.append(r)
        scal = jnp.where(lane == s, r, scal)
        v = pre[:, here] * r
        pre[:, here] = v
        th = jnp.tanh(GELU_A * (v + GELU_B * v * v * v))
        h = (0.5 * v * (1.0 + th)).astype(BF)
        slope[:, here] = 0.5 * (1.0 + th) + 0.5 * v * (1.0 - th * th) * (GELU_A * (1.0 + 3.0 * GELU_B * v * v))
        hs[s] = h
        hf = h.astype(F32)
        hts[s] = hf.T.astype(BF)
        if s + 1 < S:
            before = qacc[:, here]
            qacc[:, s * R :] += mm(h, kmat[s * R :, here], NT)
            sq = sq + jnp.sum(hf * (before + qacc[:, here]), axis=1, keepdims=True)
            pre[:, (s + 1) * R :] += mm(h, kmat[here, (s + 1) * R :])
    gam = jnp.zeros((T, 1), F32)
    for s in reversed(range(S)):
        here = slice(s * R, (s + 1) * R)
        hg = hacc[:, here]
        if s + 1 < S:
            hg = hg - gam * qacc[:, here]
        p = (hg * slope[:, here]).astype(BF)
        ps[s] = p
        r = inv[s]
        cen = r * r * (jnp.sum(p.astype(F32) * pre[:, here], axis=1, keepdims=True) * (1.0 / D))
        scal = jnp.where(lane == S + s, cen, scal)
        if s > 0:
            upd = r * mm(p, kmat[: s * R, here], NT)
            if s + 1 < S:
                upd = upd - gam * mm(hs[s], kmat[here, : s * R])
            hacc[:, : s * R] += upd
        gam = gam + cen
    sts[...] = scal.T
    for cp in copies:
        cp.wait()

    total = jnp.zeros((QUARTER, R), F32)
    x = xt_ref[...]
    for s in range(S):
        xs[s] = x
        xf = x.astype(F32)
        n = (xf * sts[s : s + 1, :]).astype(BF)
        gi = mm(n, ps[s])
        for j1 in range(2):
            a = gi[2 * j1 * QUARTER : (2 * j1 + 1) * QUARTER]
            b = gi[(2 * j1 + 1) * QUARTER : (2 * j1 + 2) * QUARTER]
            total = total + a * a + b * b
            gown_ref[s * 2 + j1, :ROWS] = jnp.where(is0, a, b).astype(BF)
            goth_ref[s * 2 + j1, :ROWS] = jnp.where(is0, b, a).astype(BF)
        if s + 1 < S:
            x = (xf + mm(wbuf[1, :, s].reshape(SLICE, R), hs[s], NT)).astype(BF)
    g = ct_ref[...]
    for s in reversed(range(S)):
        lsf = ls_ref[s].astype(F32)
        lsf = lsf[:5] + lsf[5:10]
        lrow = jnp.concatenate([lsf[j : j + 1] for j in range(4)] + [lsf[4:5, :64]], axis=1)
        gos[s] = mm(hts[s], g, NT) * lrow
        if s > 0:
            m = mm(wbuf[0, :, s].reshape(SLICE, R), ps[s], NT)
            g = (g.astype(F32) + sts[s : s + 1, :] * m - sts[S + s : S + s + 1, :] * xs[s].astype(F32)).astype(BF)
    acc = jnp.zeros((R, SLICE), F32)
    for s in range(S):
        acc = acc + gos[s] * gos[s]
    tails = []
    for quad in range(2):
        v = [gos[quad * 4 + i].reshape(16, 8, SLICE) for i in range(4)]
        a0, a1 = halves(v[0], v[1])
        b0, b1 = halves(v[2], v[3])
        even = jnp.concatenate([a0, b0], axis=1)
        odd = jnp.concatenate([a1, b1], axis=1)
        mine = jnp.where(is0, even, odd)
        rest = jnp.where(is0, odd, even)
        for t in range(4):
            at = slice(ROWS + 32 * t + 16 * quad, ROWS + 32 * t + 16 * quad + 16)
            gown_ref[:, at] = mine[:, :, t * R : (t + 1) * R].astype(BF)
            goth_ref[:, at] = rest[:, :, t * R : (t + 1) * R].astype(BF)
        tails.append((mine[:, :, 4 * R :], rest[:, :, 4 * R :]))
    gown_ref[:, ROWS + 128 :] = jnp.concatenate([tails[0][0], tails[1][0]], axis=2).astype(BF)
    goth_ref[:, ROWS + 128 :] = jnp.concatenate([tails[0][1], tails[1][1]], axis=2).astype(BF)
    one = jnp.sum(jnp.sum(total, axis=0, keepdims=True), axis=1, keepdims=True)
    two = jnp.sum(jnp.sum(acc, axis=0, keepdims=True), axis=1, keepdims=True)
    norm_ref[...] = jnp.broadcast_to((one + two).reshape(1, 1, 1), (S, 8, R))


def sum_kernel(got_ref, gi_ref, go_ref):
    total = got_ref[0].astype(F32)
    for i in range(1, 16):
        total = total + got_ref[i].astype(F32)
    gi_ref[...] = total[:ROWS].astype(BF)
    go = total[ROWS:]
    last = go[4 * 32 :]
    tail = jnp.concatenate([last[:, :64], last[:, 64:]], axis=0)
    go = jnp.concatenate([go[32 * t : 32 * t + 32] for t in range(4)] + [tail], axis=1).reshape(4, 8, SLICE)
    for i in range(4):
        go_ref[2 * i] = go[i]
        go_ref[2 * i + 1] = pltpu.roll(go[i], 4, axis=0)


def join_kernel(got_ref, out_ref):
    out_ref[0] = jnp.concatenate([got_ref[k, :4] for k in range(S)], axis=1)


def per_device(inputs, w_in, w_out, layer_scale, cotangent):
    z, y, x, c = (lax.axis_index(a) for a in (Z, Y, X, C))
    at = jnp.stack([z, x, c, (x * 2 + c) * 4 + y]).astype(jnp.int32)
    swap = [(0, 1), (1, 0)]
    w1 = w_in[0]
    flops = 2 * T * D * R

    w2, pay = call(
        pack_kernel, "pack",
        [((R, D), BF), ((S, 2 * ROWS + 16, R), BF)],
        [SM, VM, VM, VM],
        [pltpu.VMEM((D, R), BF)], flops=flops // 16, size=4 << 20,
    )(at, w1, w_out[0], layer_scale)
    got = lax.all_to_all(pay, Z, 0, 0)

    proj, sq, xt, ct = call(
        project_kernel, "project",
        [((T, 4 * R), BF), ((T, 1), F32), ((SLICE, T), BF), ((SLICE, T), BF)],
        [SM, VM, VM, VM, VM],
        [pltpu.VMEM((5 * R, T), BF)], flops=3 * flops, size=5 << 20,
    )(at, inputs, cotangent, w1, w2)
    proj = lax.all_gather(proj, Z, axis=0)

    (part,) = call(gram_kernel, "gram", [((S, 32, R), BF)], [SM, VM, VM, VM], flops=flops // 2, size=3 << 20)(at, got, w1, w2)
    part = lax.all_to_all(part, Z, 0, 0)
    piece = got[:, ROWS : 2 * ROWS]
    shifts = [lax.ppermute(piece, X, [(i, (i + d) % 4) for i in range(4)]) for d in (1, 2, 3)]
    wown = jnp.stack([piece] + shifts)
    woth = lax.ppermute(wown, C, swap)
    ls = got[:, 2 * ROWS :]

    kown = lax.all_to_all(jnp.broadcast_to(part, (16, S, 32, R)), (Y, X), 0, 0)
    koth = lax.ppermute(kown, C, swap)

    anywhere = pl.BlockSpec(memory_space=pl.ANY)
    gown, goth, norm = call(
        main_kernel, "main",
        [((16, 2 * ROWS, R), BF), ((16, 2 * ROWS, R), BF), ((S, 8, R), F32)],
        [SM, VM, VM, VM, VM, anywhere, anywhere, VM, VM, VM],
        [
            pltpu.VMEM((S * R, S * R), BF),
            pltpu.VMEM((T, S * R), F32),
            pltpu.VMEM((T, S * R), F32),
            pltpu.VMEM((T, S * R), F32),
            pltpu.VMEM((T, S * R), F32),
            pltpu.VMEM((S, T, R), BF),
            pltpu.VMEM((S, R, T), BF),
            pltpu.VMEM((S, T, R), BF),
            pltpu.VMEM((R, T), F32),
            pltpu.VMEM((2, 4, S, QUARTER, R), BF),
            pltpu.VMEM((S, SLICE, T), BF),
            pltpu.VMEM((S, R, SLICE), F32),
            pltpu.SemaphoreType.DMA((8,)),
        ],
        flops=2 * 32 * SLICE * T * R + 2 * 192 * T * R * R, size=10 << 20, trans=S * T * R,
    )(at, kown, koth, proj, sq, wown, woth, xt, ct, ls)

    ggot = lax.ppermute(goth, C, swap)
    total = jnp.sum(lax.all_to_all(norm, Z, 0, 0), axis=0)
    factor = CLIP_NORM / (jnp.sqrt(total) + CLIP_OFFSET)
    other = lax.ppermute(factor, C, swap)
    both = (gown.astype(F32) * factor[0, 0] + ggot.astype(F32) * other[0, 0]).astype(BF)
    both = lax.all_to_all(both, (Y, X), 0, 0)
    gi, go = call(sum_kernel, "sum", [((ROWS, R), BF), ((S, 8, SLICE), F32)], [VM], size=2 << 20)(both)
    route = [(k * 32 + s * 4 + j, s * 32 + k * 4 + j) for k in range(S) for s in range(S) for j in range(4)]
    grad_in = lax.ppermute(gi, (Z, Y, X, C), route).astype(F32)[None]
    go = lax.all_to_all(go, Z, 0, 0)
    (grad_out,) = call(join_kernel, "join", [((1, 4, D), F32)], [VM])(go)
    return grad_in, grad_out


def solution(mesh):
    split = Mesh(np.asarray(mesh.devices).reshape(S, 4, 4, 2), (Z, Y, X, C))
    dp = (Y, X, C)
    return jax.shard_map(
        per_device,
        mesh=split,
        in_specs=(P(dp, None), P(Z, None, None), P(Z, None, None), P(Z, None), P(dp, None)),
        out_specs=(P(Z, dp, None), P(Z, dp, None)),
        check_vma=False,
    )
```

time: 216 us -> 183 us (0.85); the launches traced: 213 us -> 182 us
  blocking collectives: 17.7 us -> 75.9 us
  waiting for transfers between devices: 78.5 us -> 37.3 us
  starting transfers between devices: 47 us -> 22.3 us
  local copies, waits for them, and re-layouts: 28.3 us -> 15.2 us
  other arithmetic: 12.5 us -> 2.64 us
  Pallas kernels: 8.74 us -> 14.6 us
  matrix products: 5.05 us -> 0 us
    all_to_all x0 -> x4, blocking collectives: none -> 75.9 us  [the longest x1 28.3 us: per_device(): got = lax.all_to_all(pay, Z, 0, 0)]
    all_to_all x8 -> x2, waiting for transfers between devices: 77.5 us -> 8.79 us  [the longest x1 8.78 us: per_device(): go = lax.all_to_all(go, Z, 0, 0)]
    all_to_all x8 -> x2, starting transfers between devices: 44.2 us -> 16.5 us  [the longest x1 8.93 us: per_device(): go = lax.all_to_all(go, Z, 0, 0)]
    psum x1 -> x0, blocking collectives: 17.7 us -> none  [per_device(): total = lax.psum(part[:1, :1], Z)]
    all_gather x1, waiting for transfers between devices: 0.02 us -> 16.4 us  [per_device(): proj = lax.all_gather(proj, Z, axis=0)]
    ppermute x5 -> x7, waiting for transfers between devices: 0.01 us -> 11.5 us  [the longest x3 11.5 us: per_device(): lax.ppermute(piece, X, [(i, (i + d) % 4) for i in range(4)])]
    convert_element_type x4 -> x1, other arithmetic: 7.97 us -> 1.75 us  [per_device(): (gown.astype(F32) * factor[0, 0] + ggot.astype(F32) * other[0, 0]).astype...]
    pallas_call x2 -> x6, Pallas kernels: 8.74 us -> 14.6 us  [the longest x1 9.24 us: per_device(): call(main_kernel, 'main', [((16, 2 * ROWS, R), BF), ((16, 2 * ROWS, R), B...]
  transfers between devices with their start and end apart: 15 -> 11, of which waited for: 8 -> 6; matrix products, arithmetic and copies ran while one was open for 12% -> 2% of each run, Pallas kernels for 3% -> 1%
where the time goes in v2:
time: 183 us; the launch traced here: 182 us
  blocking collectives  75.9 us (41%)
  waiting for transfers between devices  37.3 us (20%)
  starting transfers between devices  22.3 us (12%)
  local copies, waits for them, and re-layouts  15.2 us (8%)
  Pallas kernels  14.6 us (8%)
  between operations  14.2 us (8%)
  other arithmetic  2.64 us (1%)
    all_to_all x1, blocking collectives, per_device(): got = lax.all_to_all(pay, Z, 0, 0)  28.3 us
    all_to_all x1, blocking collectives, per_device(): both = lax.all_to_all(both, (Y, X), 0, 0)  24.6 us
    all_gather x1, waiting for transfers between devices, per_device(): proj = lax.all_gather(proj, Z, axis=0)  16.4 us
    all_to_all x1, blocking collectives, per_device(): total = jnp.sum(lax.all_to_all(norm, Z, 0, 0), axis=0)  12.3 us
    ppermute x3, waiting for transfers between devices, per_device(): lax.ppermute(piece, X, [(i, (i + d) % 4) for i in range(4)])  11.5 us
    unnamed x34, local copies, waits for them, and re-layouts  11.2 us
    all_to_all x1, blocking collectives, per_device(): part = lax.all_to_all(part, Z, 0, 0)  10.8 us
    pallas_call x1, Pallas kernels, per_device(): call(main_kernel, 'main', [((16, 2 * ROWS, R), BF), ((16, 2 * ROWS, R), B...  9.24 us
  transfers between devices with their start and end apart: 11, of which 6 were waited for; matrix products, arithmetic and copies ran while one was open for 2% of the time, Pallas kernels for 1%

profile of v2, /device:TPU:2, one launch (start us, length us, event | category | flops | bytes accessed | tf_op | source)
XLA Modules:
  0.0 182.2 jit_solution(5973189279985654073)
XLA Ops:
  7.2 0.1 pad_add_fusion.at_ref
  7.2 0.0 copy-start.13
  7.3 1.3 copy-done
  8.5 1.3 copy-done.5
  9.8 0.7 copy-done.12
  10.5 0.9 pack.1
  11.4 28.3 %all_to_all.30.got_ref = bf16[8,304,128]{2,1,0:T(8,128)(2,1)S(1)} all-to-all(bf16[8,304,128]{2,1,0:T(8,128)(2,1)S(1)} %get-tuple-element.13), channel_id=1, replica_groups=mesh['section'=8,'y'=4,'x'=4,'core'=2] {'section'}, dimensions={0} | all-to-all | bytes 1245184 | tf_op jit(solution)/shard_map/all_to_all | solution.py:291
  39.7 0.0 copy-done.13
  39.7 1.2 gram.1
  40.9 0.0 copy-done.2
  40.9 10.8 %all_to_all.31 = bf16[8,32,128]{2,1,0:T(8,128)(2,1)S(1)} all-to-all(bf16[8,32,128]{2,1,0:T(8,128)(2,1)S(1)} %gram.1), channel_id=1, replica_groups=mesh['section'=8,'y'=4,'x'=4,'core'=2] {'section'}, dimensions={0} | all-to-all | bytes 131072 | tf_op jit(solution)/shard_map/all_to_all | solution.py:302
  51.7 1.2 broadcast_in_dim.9
  52.9 7.6 %all-to-all-start.2 = ((bf16[16,8,32,128]{3,2,1,0:T(8,128)(2,1)}), bf16[16,8,32,128]{3,2,1,0:T(8,128)(2,1)S(1)}, u32[]{:S(2)}, u32[]{:S(2)}) async-start(bf16[16,8,32,128]{3,2,1,0:T(8,128)(2,1)} %broadcast_in_dim.9), calls=%async_computation.2 | async-start | bytes 2097152 | tf_op jit(solution)/shard_map/all_to_all | solution.py:309
  60.5 0.0 all-gather.3.cloned.1.call-start
  60.5 0.0 copy-done.1
  60.5 0.0 copy-start.3
  60.5 1.3 copy-done.3
  61.8 1.3 copy-done.4
  63.1 0.7 copy-done.14
  63.7 1.6 project.1
  65.4 0.0 copy-start.7
  65.4 0.7 copy-done.7
  66.0 0.7 copy-done.9
  66.7 0.6 copy-done.10
  67.3 0.0 all-gather.3.cloned.1.call-update
  67.3 1.0 slice_bitcast_fusion
  68.4 2.2 %collective-permute-start.2 = (bf16[8,144,128]{2,1,0:T(8,128)(2,1)S(1)}, bf16[8,144,128]{2,1,0:T(8,128)(2,1)S(1)}, u32[]{:S(2)}, u32[]{:S(2)}) collective-permute-start(bf16[8,144,128]{2,1,0:T(8,128)(2,1)S(1)} %get-tuple-element.25), channel_id=1, source_target_pairs={{0,4},{2,6},{4,0},{6,2},{1,5},{3,7},{5,1},{7,3},{8,12},{10,14},{12... | collective-permute-start | bytes 884744 | tf_op jit(solution)/shard_map/ppermute | solution.py:304
  70.5 0.0 collective-permute-start.1
  70.6 2.0 %collective-permute-start.3 = (bf16[8,144,128]{2,1,0:T(8,128)(2,1)S(1)}, bf16[8,144,128]{2,1,0:T(8,128)(2,1)S(1)}, u32[]{:S(2)}, u32[]{:S(2)}) collective-permute-start(bf16[8,144,128]{2,1,0:T(8,128)(2,1)S(1)} %get-tuple-element.25), channel_id=1, source_target_pairs={{0,6},{2,0},{4,2},{6,4},{1,7},{3,1},{5,3},{7,5},{8,14},{10,8},{12,... | collective-permute-start | bytes 884744 | tf_op jit(solution)/shard_map/ppermute | solution.py:304
  72.6 8.7 %collective-permute-done.2 = bf16[8,144,128]{2,1,0:T(8,128)(2,1)S(1)} collective-permute-done((bf16[8,144,128]{2,1,0:T(8,128)(2,1)S(1)}, bf16[8,144,128]{2,1,0:T(8,128)(2,1)S(1)}, u32[]{:S(2)}, u32[]{:S(2)}) %collective-permute-start.2) | collective-permute-done | bytes 294944 | tf_op jit(solution)/shard_map/ppermute | solution.py:304
  81.3 1.9 %collective-permute-done.1 = bf16[8,144,128]{2,1,0:T(8,128)(2,1)S(1)} collective-permute-done((bf16[8,144,128]{2,1,0:T(8,128)(2,1)S(1)}, bf16[8,144,128]{2,1,0:T(8,128)(2,1)S(1)}, u32[]{:S(2)}, u32[]{:S(2)}) %collective-permute-start.1) | collective-permute-done | bytes 294944 | tf_op jit(solution)/shard_map/ppermute | solution.py:304
  83.2 0.9 collective-permute-done.3
  84.1 0.1 pad_maximum_fusion.wown_ref
  84.2 0.0 copy-start.16
  84.2 0.1 collective-permute-start.4
  84.3 0.0 all-to-all-done.2.own_ref
  84.3 0.5 collective-permute-start
  84.8 0.8 slice.17.ls_ref
  85.6 16.4 %all-gather.3.cloned.1.call-done = bf16[1024,512]{1,0:T(8,128)(2,1)} async-done(((bf16[128,512]{1,0:T(8,128)(2,1)}), bf16[1024,512]{1,0:T(8,128)(2,1)}) %all-gather.3.cloned.1.call-update) | async-done | bytes 1048592 | tf_op jit(solution)/shard_map/all_gather | solution.py:299
  102.0 0.0 collective-permute-done.4.woth_ref
  102.0 0.0 collective-permute-done.oth_ref
  102.0 0.0 copy-done.16
  102.0 0.0 copy-done.11
  102.0 0.0 copy-start.6
  102.0 1.2 copy-done.6
  103.2 0.9 copy-done.8
  104.2 0.7 copy-done.15
  104.8 9.2 %main.1 = (bf16[16,288,128]{2,1,0:T(8,128)(2,1)S(1)}, bf16[16,288,128]{2,1,0:T(8,128)(2,1)}, f32[8,8,128]{2,1,0:T(8,128)S(1)}) custom-call(s32[4]{0:T(128)S(1)} %copy-done.15, bf16[16,8,32,128]{3,2,1,0:T(8,128)(2,1)S(1)} %all-to-all-done.2.own_ref, bf16[16,8,32,128]{3,2,1,0:T(8,128)(2,1)S(1)} %collective-permute-done.oth_ref, ...), custom_call_target="tpu_custom_call" | custom-call | flops 1409286144 | bytes 10485760 | tf_op jit(solution)/shard_map/main/pallas_call | solution.py:313
  114.1 0.3 collective-permute-start.5
  114.3 12.3 %all_to_all.32 = f32[8,8,128]{2,1,0:T(8,128)S(1)} all-to-all(f32[8,8,128]{2,1,0:T(8,128)S(1)} %get-tuple-element.20), channel_id=1, replica_groups=mesh['section'=8,'y'=4,'x'=4,'core'=2] {'section'}, dimensions={0} | all-to-all | bytes 65536 | tf_op jit(solution)/shard_map/all_to_all | solution.py:336
  126.7 0.1 collective-permute-start.6
  126.8 0.5 slice.14
  127.3 0.6 collective-permute-done.6
  127.9 0.5 slice.15
  128.5 0.0 collective-permute-done.5
  128.5 1.8 add_convert_fusion
  130.2 24.6 %all_to_all.33.got_ref = bf16[16,288,128]{2,1,0:T(8,128)(2,1)S(1)} all-to-all(bf16[16,288,128]{2,1,0:T(8,128)(2,1)S(1)} %add_convert_fusion), channel_id=1, replica_groups=mesh['section'=8,'y'=4,'x'=4,'core'=2] {'y','x'}, dimensions={0} | all-to-all | bytes 2359296 | tf_op jit(solution)/shard_map/all_to_all | solution.py:340
  154.8 0.8 sum.1
  155.7 0.7 collective-permute-start.7
  156.3 8.9 %all-to-all-start.5 = ((f32[8,8,576]{2,1,0:T(8,128)}), f32[8,8,576]{2,1,0:T(8,128)S(1)}, u32[]{:S(2)}, u32[]{:S(2)}) async-start(f32[8,8,576]{2,1,0:T(8,128)} %get-tuple-element.23), calls=%async_computation.5 | async-start | bytes 327680 | tf_op jit(solution)/shard_map/all_to_all | solution.py:344
  165.2 0.0 collective-permute-done.7
  165.2 0.6 bitcast_convert_fusion
  165.9 8.8 %all-to-all-done.5.got_ref = f32[8,8,576]{2,1,0:T(8,128)S(1)} async-done(((f32[8,8,576]{2,1,0:T(8,128)}), f32[8,8,576]{2,1,0:T(8,128)S(1)}, u32[]{:S(2)}, u32[]{:S(2)}) %all-to-all-start.5) | async-done | bytes 147488 | tf_op jit(solution)/shard_map/all_to_all | solution.py:344
  174.7 0.7 join.1
  (14 shorter events, 0.0 us)
Async XLA Ops:
  7.2 32.4 %copy-start.13 = (s32[4]{0:T(128)}, s32[4]{0:T(128)S(1)}, u32[]{:S(2)}) copy-start(s32[4]{0:T(128)S(1)} %pad_add_fusion.at_ref) | copy-start | bytes 52
  7.3 1.3 copy-start
  8.5 1.3 copy-start.5
  9.8 0.7 copy-start.12
  39.7 1.2 copy-start.2
  52.9 7.7 %copy-start.1 = (bf16[1,4608,128]{2,1,0:T(8,128)(2,1)S(1)}, bf16[1,4608,128]{2,1,0:T(8,128)(2,1)}, u32[]{:S(2)}) copy-start(bf16[1,4608,128]{2,1,0:T(8,128)(2,1)} %param.6) | copy-start | bytes 3538948
  52.9 31.5 %all-to-all-start.2 = ((bf16[16,8,32,128]{3,2,1,0:T(8,128)(2,1)}), bf16[16,8,32,128]{3,2,1,0:T(8,128)(2,1)S(1)}, u32[]{:S(2)}, u32[]{:S(2)}) async-start(bf16[16,8,32,128]{3,2,1,0:T(8,128)(2,1)} %broadcast_in_dim.9), calls=%async_computation.2 | async-start | bytes 2097152 | tf_op jit(solution)/shard_map/all_to_all | solution.py:309
  60.5 41.5 %all-gather.3.cloned.1.call-start = ((), (), s32[]{:S(2)}) async-start(), calls=%async_computation.6 | async-start | bytes 1179648 | tf_op jit(solution)/shard_map/all_gather | solution.py:299
  60.5 1.3 copy-start.3
  61.8 1.3 copy-start.4
  63.1 0.7 copy-start.14
  65.4 0.7 copy-start.7
  66.0 0.7 copy-start.9
  66.7 0.6 copy-start.10
  68.4 12.9 %collective-permute-start.2 = (bf16[8,144,128]{2,1,0:T(8,128)(2,1)S(1)}, bf16[8,144,128]{2,1,0:T(8,128)(2,1)S(1)}, u32[]{:S(2)}, u32[]{:S(2)}) collective-permute-start(bf16[8,144,128]{2,1,0:T(8,128)(2,1)S(1)} %get-tuple-element.25), channel_id=1, source_target_pairs={{0,4},{2,6},{4,0},{6,2},{1,5},{3,7},{5,1},{7,3},{8,12},{10,14},{12... | collective-permute-start | bytes 884744 | tf_op jit(solution)/shard_map/ppermute | solution.py:304
  70.5 12.6 %collective-permute-start.1 = (bf16[8,144,128]{2,1,0:T(8,128)(2,1)S(1)}, bf16[8,144,128]{2,1,0:T(8,128)(2,1)S(1)}, u32[]{:S(2)}, u32[]{:S(2)}) collective-permute-start(bf16[8,144,128]{2,1,0:T(8,128)(2,1)S(1)} %get-tuple-element.25), channel_id=1, source_target_pairs={{0,2},{2,4},{4,6},{6,0},{1,3},{3,5},{5,7},{7,1},{8,10},{10,12},{12... | collective-permute-start | bytes 884744 | tf_op jit(solution)/shard_map/ppermute | solution.py:304
  70.6 13.5 %collective-permute-start.3 = (bf16[8,144,128]{2,1,0:T(8,128)(2,1)S(1)}, bf16[8,144,128]{2,1,0:T(8,128)(2,1)S(1)}, u32[]{:S(2)}, u32[]{:S(2)}) collective-permute-start(bf16[8,144,128]{2,1,0:T(8,128)(2,1)S(1)} %get-tuple-element.25), channel_id=1, source_target_pairs={{0,6},{2,0},{4,2},{6,4},{1,7},{3,1},{5,3},{7,5},{8,14},{10,8},{12,... | collective-permute-start | bytes 884744 | tf_op jit(solution)/shard_map/ppermute | solution.py:304
  84.1 17.9 %copy-start.11 = (f32[128,1]{1,0:T(8,128)S(1)}, f32[128,1]{1,0:T(8,128)}, u32[]{:S(2)}) copy-start(f32[128,1]{1,0:T(8,128)} %copy-done.10) | copy-start | bytes 1540
  84.2 17.8 %copy-start.16 = (bf16[4,8,144,128]{3,2,1,0:T(8,128)(2,1)}, bf16[4,8,144,128]{3,2,1,0:T(8,128)(2,1)S(1)}, u32[]{:S(2)}) copy-start(bf16[4,8,144,128]{3,2,1,0:T(8,128)(2,1)S(1)} %pad_maximum_fusion.wown_ref) | copy-start | bytes 3538948
  84.2 17.8 %collective-permute-start.4 = (bf16[4,8,144,128]{3,2,1,0:T(8,128)(2,1)S(1)}, bf16[4,8,144,128]{3,2,1,0:T(8,128)(2,1)}, u32[]{:S(2)}, u32[]{:S(2)}) collective-permute-start(bf16[4,8,144,128]{3,2,1,0:T(8,128)(2,1)S(1)} %pad_maximum_fusion.wown_ref), channel_id=1, source_target_pairs={{0,1},{1,0},{2,3},{3,2},{4,5},{5,4},{6,7},{7,6},{8,9},{9,8},{10,11... | collective-permute-start | bytes 3538952 | tf_op jit(solution)/shard_map/ppermute | solution.py:306
  84.3 17.7 %collective-permute-start = (bf16[16,8,32,128]{3,2,1,0:T(8,128)(2,1)S(1)}, bf16[16,8,32,128]{3,2,1,0:T(8,128)(2,1)S(1)}, u32[]{:S(2)}, u32[]{:S(2)}) collective-permute-start(bf16[16,8,32,128]{3,2,1,0:T(8,128)(2,1)S(1)} %all-to-all-done.2.own_ref), channel_id=1, source_target_pairs={{0,1},{1,0},{2,3},{3,2},{4,5},{5,4},{6,7},{7,6},{8,9},{9,8},{10,11... | collective-permute-start | bytes 3145736 | tf_op jit(solution)/shard_map/ppermute | solution.py:310
  102.0 1.2 copy-start.6
  103.2 0.9 copy-start.8
  104.2 0.7 copy-start.15
  114.1 14.4 %collective-permute-start.5 = (bf16[16,288,128]{2,1,0:T(8,128)(2,1)}, bf16[16,288,128]{2,1,0:T(8,128)(2,1)S(1)}, u32[]{:S(2)}, u32[]{:S(2)}) collective-permute-start(bf16[16,288,128]{2,1,0:T(8,128)(2,1)} %get-tuple-element.21), channel_id=1, source_target_pairs={{0,1},{1,0},{2,3},{3,2},{4,5},{5,4},{6,7},{7,6},{8,9},{9,8},{10,11... | collective-permute-start | bytes 3538952 | tf_op jit(solution)/shard_map/ppermute | solution.py:335
  126.7 1.2 collective-permute-start.6
  155.7 9.6 %collective-permute-start.7 = (bf16[144,128]{1,0:T(8,128)(2,1)S(1)}, bf16[144,128]{1,0:T(8,128)(2,1)S(1)}, u32[]{:S(2)}, u32[]{:S(2)}) collective-permute-start(bf16[144,128]{1,0:T(8,128)(2,1)S(1)} %get-tuple-element.22), channel_id=1, source_target_pairs={{0,0},{1,1},{2,2},{3,3},{4,32},{5,33},{6,34},{7,35},{8,64},{9,65},... | collective-permute-start | bytes 110600 | tf_op jit(solution)/shard_map/ppermute | solution.py:343
  156.3 18.4 %all-to-all-start.5 = ((f32[8,8,576]{2,1,0:T(8,128)}), f32[8,8,576]{2,1,0:T(8,128)S(1)}, u32[]{:S(2)}, u32[]{:S(2)}) async-start(f32[8,8,576]{2,1,0:T(8,128)} %get-tuple-element.23), calls=%async_computation.5 | async-start | bytes 327680 | tf_op jit(solution)/shard_map/all_to_all | solution.py:344
Sparse Core Ops, SparseCore 0:
  67.5 34.4 all-gather.2

commit v3 on v2

--- a/solution.py
+++ b/solution.py
@@ -15,6 +15,7 @@
 D = 4608
 SLICE = D // S
 QUARTER = SLICE // 4
+PACK_VMEM = 60
 Z, Y, X, C = "section", "y", "x", "core"
 BF = jnp.bfloat16
 F32 = jnp.float32
@@ -22,11 +23,9 @@
 NT = (((1,), (1,)), ((), ()))
 GELU_A = 0.7978845608028654
 GELU_B = 0.044715
-VMEM_LIMIT = 48 * 1024 * 1024
 HALF = D // 2
 ROWS = D * 4 // R
 VM = pl.BlockSpec(memory_space=pltpu.VMEM)
-SM = pl.BlockSpec(memory_space=pltpu.SMEM)
 
 
 def mm(a, b, dims=NN):
@@ -41,33 +40,45 @@
     )
 
 
-def call(kernel, name, outs, ins, scratch=(), flops=0, size=1 << 21, trans=0):
+def call(kernel, name, outs, ins, scratch=(), flops=0, size=1 << 21, trans=0, vmem=8):
     return pl.pallas_call(
         kernel,
         out_shape=tuple(jax.ShapeDtypeStruct(*o) for o in outs),
         in_specs=list(ins),
         out_specs=(VM,) * len(outs),
         scratch_shapes=list(scratch),
-        compiler_params=pltpu.CompilerParams(vmem_limit_bytes=VMEM_LIMIT),
+        compiler_params=pltpu.CompilerParams(vmem_limit_bytes=vmem << 20),
         cost_estimate=pl.CostEstimate(flops=flops, bytes_accessed=size, transcendentals=trans),
         name=name,
     )
 
 
-def pack_kernel(at_ref, w_in_ref, w_out_ref, ls_ref, w2_ref, pay_ref, turned):
-    x, core, q = at_ref[1], at_ref[2], at_ref[3]
+def pack_kernel(w_in_ref, w_out_ref, ls_ref, w2_ref, pay_ref, wide, turned, sem):
+    y, x, core = lax.axis_index(Y), lax.axis_index(X), lax.axis_index(C)
+    q = (x * 2 + core) * 4 + y
+    step = D // 4
+    loads = [
+        pltpu.make_async_copy(w_out_ref.at[:, pl.ds(i * step, step)], wide.at[:, pl.ds(i * step, step)], sem.at[i])
+        for i in range(4)
+    ]
+    for cp in loads:
+        cp.start()
+
+    def piece(k):
+        return pl.ds(pl.multiple_of(SLICE * k + QUARTER * x, 16), QUARTER)
+
+    def feature_copies():
+        return [
+            pltpu.make_async_copy(w_in_ref.at[piece(k)], pay_ref.at[k, pl.ds(ROWS, QUARTER)], sem.at[4 + k])
+            for k in range(S)
+        ]
+
+    @pl.when(core == 0)
+    def _():
+        for cp in feature_copies():
+            cp.start()
+
     ls = ls_ref[...]
-    w2 = (w_out_ref[...].astype(F32) * ls).astype(BF)
-    w2_ref[...] = w2
-    row = lax.broadcasted_iota(jnp.int32, (8, R), 0) % 4
-    col = lax.broadcasted_iota(jnp.int32, (8, R), 1)
-    mine = mm((col == q * 4 + row).astype(BF), w2)
-    low = lax.broadcasted_iota(jnp.int32, (8, HALF), 0) < 4
-    mine = jnp.where(low, mine[:, :HALF], mine[:, HALF:])
-    for u in range(9):
-        two = jnp.concatenate([mine[:, 256 * u : 256 * u + R], mine[:, 256 * u + R : 256 * (u + 1)]], axis=0).astype(BF)
-        for k in range(S):
-            pay_ref[k, 16 * u : 16 * u + 16] = two
     top = ls.astype(BF).astype(F32)
     low_part = ls - top
     for k in range(S):
@@ -78,30 +89,44 @@
             rows.append(jnp.concatenate([tail, tail], axis=1))
         rows.append(jnp.zeros((6, R), F32))
         pay_ref[k, 2 * ROWS : 2 * ROWS + 16] = jnp.concatenate(rows, axis=0).astype(BF)
+    row = lax.broadcasted_iota(jnp.int32, (8, R), 0) % 4
+    col = lax.broadcasted_iota(jnp.int32, (8, R), 1)
+    pick = (col == q * 4 + row).astype(BF)
+    mine = []
+    for i, cp in enumerate(loads):
+        cp.wait()
+        at = slice(i * step, (i + 1) * step)
+        part = (wide[:, at].astype(F32) * ls[:, at]).astype(BF)
+        w2_ref[:, at] = part
+        mine.append(mm(pick, part))
+    mine = jnp.concatenate(mine, axis=1)
+    low = lax.broadcasted_iota(jnp.int32, (8, HALF), 0) < 4
+    mine = jnp.where(low, mine[:, :HALF], mine[:, HALF:])
+    for u in range(9):
+        two = jnp.concatenate([mine[:, 256 * u : 256 * u + R], mine[:, 256 * u + R : 256 * (u + 1)]], axis=0).astype(BF)
+        for k in range(S):
+            pay_ref[k, 16 * u : 16 * u + 16] = two
 
     @pl.when(core == 0)
     def _():
-        for k in range(S):
-            start = pl.multiple_of(SLICE * k + QUARTER * x, 16)
-            pay_ref[k, ROWS : 2 * ROWS] = w_in_ref[pl.ds(start, QUARTER), :]
+        for cp in feature_copies():
+            cp.wait()
 
     @pl.when(core != 0)
     def _():
         for t in range(D // R):
             turned[t * R : (t + 1) * R, :] = w2_ref[:, t * R : (t + 1) * R].astype(F32).T.astype(BF)
         for k in range(S):
-            start = pl.multiple_of(SLICE * k + QUARTER * x, 16)
-            pay_ref[k, ROWS : 2 * ROWS] = turned[pl.ds(start, QUARTER), :]
-
-
-def project_kernel(at_ref, x_ref, c_ref, w_in_ref, w2_ref, proj_ref, sq_ref, xt_ref, ct_ref, wide):
-    z = at_ref[0]
+            pay_ref[k, ROWS : 2 * ROWS] = turned[piece(k), :]
+
+
+def project_kernel(x_ref, c_ref, w_in_ref, w2_ref, proj_ref, sq_ref, xt_ref, ct_ref, wide):
+    z = lax.axis_index(Z)
     xv = x_ref[...]
     w2 = w2_ref[...]
     proj_ref[:, :R] = mm(xv, w_in_ref[...]).astype(BF)
     proj_ref[:, R : 2 * R] = mm(xv, w2, NT).astype(BF)
-    proj_ref[:, 2 * R : 3 * R] = mm(c_ref[...], w2, NT).astype(BF)
-    proj_ref[:, 3 * R :] = jnp.zeros((T, R), BF)
+    proj_ref[:, 2 * R :] = mm(c_ref[...], w2, NT).astype(BF)
     xf = xv.astype(F32)
     sq_ref[...] = jnp.sum(xf * xf, axis=1, keepdims=True)
     base = pl.multiple_of(((z * 9) // 2) * R, R)
@@ -112,8 +137,8 @@
         dst[...] = wide[pl.ds(off, SLICE), :]
 
 
-def gram_kernel(at_ref, got_ref, w_in_ref, w2_ref, out_ref):
-    z = at_ref[0]
+def gram_kernel(got_ref, w_in_ref, w2_ref, proj_ref, out_ref):
+    z = lax.axis_index(Z)
     first, second = [], []
     for u in range(9):
         block = got_ref[:, 16 * u : 16 * u + 16, :].astype(F32)
@@ -129,15 +154,19 @@
     below = (lax.broadcasted_iota(jnp.int32, (32, R), 0) // 4) < z
     out = jnp.where(below, up, down).astype(BF)
     for k in range(S):
-        out_ref[k] = out
-
-
-def main_kernel(at_ref, own_ref, oth_ref, proj_ref, sq_ref, wown_ref, woth_ref, xt_ref, ct_ref, ls_ref, gown_ref, goth_ref, norm_ref, kmat, pre, qacc, hacc, slope, hs, hts, ps, sts, wbuf, xs, gos, sem):
-    xpos, core = at_ref[1], at_ref[2]
+        out_ref[k, :32] = out
+        for i in range(3):
+            out_ref[k, 32 + T * i : 32 + T * (i + 1)] = proj_ref[:, i * R : (i + 1) * R]
+
+
+def main_kernel(own_ref, oth_ref, *refs):
+    proj_ref, sq_ref, wown_ref, woth_ref, xt_ref, ct_ref, ls_ref, gown_ref, goth_ref, norm_ref = refs[:10]
+    kmat, pre, qacc, hacc, slope, hs, hts, ps, sts, wbuf, xs, gos, sem = refs[10:]
+    core = lax.axis_index(C)
     is0 = core == 0
     copies = []
     for i in range(4):
-        slot = (xpos + 4 - i) % 4
+        slot = (lax.axis_index(X) + 4 - i) % 4
         for n, (ref, half) in enumerate(((wown_ref, core), (woth_ref, 1 - core))):
             copies.append(pltpu.make_async_copy(ref.at[i], wbuf.at[half, slot], sem.at[i * 2 + n]))
     for cp in copies:
@@ -162,10 +191,8 @@
 
     lax.fori_loop(0, S, place, 0)
     for s in range(S):
-        block = proj_ref[s].astype(F32)
-        pre[:, s * R : (s + 1) * R] = block[:, :R]
-        qacc[:, s * R : (s + 1) * R] = block[:, R : 2 * R]
-        hacc[:, s * R : (s + 1) * R] = block[:, 2 * R : 3 * R]
+        for i, acc in enumerate((pre, qacc, hacc)):
+            acc[:, s * R : (s + 1) * R] = proj_ref[s, 32 + T * i : 32 + T * (i + 1)].astype(F32)
     sq = sq_ref[...]
     lane = lax.broadcasted_iota(jnp.int32, (T, R), 1)
     scal = jnp.zeros((T, R), F32)
@@ -209,6 +236,9 @@
     for cp in copies:
         cp.wait()
 
+    def weights(kind, s):
+        return wbuf[kind, :, s].reshape(SLICE, R)
+
     total = jnp.zeros((QUARTER, R), F32)
     x = xt_ref[...]
     for s in range(S):
@@ -223,7 +253,7 @@
             gown_ref[s * 2 + j1, :ROWS] = jnp.where(is0, a, b).astype(BF)
             goth_ref[s * 2 + j1, :ROWS] = jnp.where(is0, b, a).astype(BF)
         if s + 1 < S:
-            x = (xf + mm(wbuf[1, :, s].reshape(SLICE, R), hs[s], NT)).astype(BF)
+            x = (xf + mm(weights(1, s), hs[s], NT)).astype(BF)
     g = ct_ref[...]
     for s in reversed(range(S)):
         lsf = ls_ref[s].astype(F32)
@@ -231,7 +261,7 @@
         lrow = jnp.concatenate([lsf[j : j + 1] for j in range(4)] + [lsf[4:5, :64]], axis=1)
         gos[s] = mm(hts[s], g, NT) * lrow
         if s > 0:
-            m = mm(wbuf[0, :, s].reshape(SLICE, R), ps[s], NT)
+            m = mm(weights(0, s), ps[s], NT)
             g = (g.astype(F32) + sts[s : s + 1, :] * m - sts[S + s : S + s + 1, :] * xs[s].astype(F32)).astype(BF)
     acc = jnp.zeros((R, SLICE), F32)
     for s in range(S):
@@ -254,15 +284,31 @@
     goth_ref[:, ROWS + 128 :] = jnp.concatenate([tails[0][1], tails[1][1]], axis=2).astype(BF)
     one = jnp.sum(jnp.sum(total, axis=0, keepdims=True), axis=1, keepdims=True)
     two = jnp.sum(jnp.sum(acc, axis=0, keepdims=True), axis=1, keepdims=True)
-    norm_ref[...] = jnp.broadcast_to((one + two).reshape(1, 1, 1), (S, 8, R))
-
-
-def sum_kernel(got_ref, gi_ref, go_ref):
-    total = got_ref[0].astype(F32)
+    norm_ref[...] = jnp.broadcast_to((one + two).reshape(1, 1, 1), (2 * S, 8, R))
+
+
+def mix_kernel(norm_ref, own_ref, got_ref, out_ref):
+    core = lax.axis_index(C)
+    sums = [norm_ref[0][:1], norm_ref[1][:1]]
+    for k in range(1, S):
+        for c in range(2):
+            sums[c] = sums[c] + norm_ref[2 * k + c][:1]
+    even, odd = (CLIP_NORM / (jnp.sqrt(v) + CLIP_OFFSET) for v in sums)
+    mine = jnp.where(core == 0, even, odd)
+    other = jnp.where(core == 0, odd, even)
+    for i in range(16):
+        out_ref[i] = (own_ref[i].astype(F32) * mine + got_ref[i].astype(F32) * other).astype(BF)
+
+
+def fold(ref, rows):
+    total = ref[0, rows].astype(F32)
     for i in range(1, 16):
-        total = total + got_ref[i].astype(F32)
-    gi_ref[...] = total[:ROWS].astype(BF)
-    go = total[ROWS:]
+        total = total + ref[i, rows].astype(F32)
+    return total
+
+
+def sum_out_kernel(got_ref, go_ref):
+    go = fold(got_ref, slice(ROWS, 2 * ROWS))
     last = go[4 * 32 :]
     tail = jnp.concatenate([last[:, :64], last[:, 64:]], axis=0)
     go = jnp.concatenate([go[32 * t : 32 * t + 32] for t in range(4)] + [tail], axis=1).reshape(4, 8, SLICE)
@@ -271,49 +317,59 @@
         go_ref[2 * i + 1] = pltpu.roll(go[i], 4, axis=0)
 
 
+def sum_in_kernel(got_ref, gi_ref):
+    gi_ref[...] = fold(got_ref, slice(0, ROWS)).astype(BF)
+
+
 def join_kernel(got_ref, out_ref):
     out_ref[0] = jnp.concatenate([got_ref[k, :4] for k in range(S)], axis=1)
 
 
+def shifted(value, axis, size):
+    return [lax.ppermute(value, axis, [(i, (i + d) % size) for i in range(size)]) for d in range(1, size)]
+
+
 def per_device(inputs, w_in, w_out, layer_scale, cotangent):
-    z, y, x, c = (lax.axis_index(a) for a in (Z, Y, X, C))
-    at = jnp.stack([z, x, c, (x * 2 + c) * 4 + y]).astype(jnp.int32)
     swap = [(0, 1), (1, 0)]
     w1 = w_in[0]
     flops = 2 * T * D * R
+    anywhere = pl.BlockSpec(memory_space=pl.ANY)
 
     w2, pay = call(
         pack_kernel, "pack",
         [((R, D), BF), ((S, 2 * ROWS + 16, R), BF)],
-        [SM, VM, VM, VM],
-        [pltpu.VMEM((D, R), BF)], flops=flops // 16, size=4 << 20,
-    )(at, w1, w_out[0], layer_scale)
+        [anywhere, anywhere, VM],
+        [pltpu.VMEM((R, D), BF), pltpu.VMEM((D, R), BF), pltpu.SemaphoreType.DMA((12,))],
+        flops=flops // 16, size=4 << 20, vmem=PACK_VMEM,
+    )(w1, w_out[0], layer_scale)
     got = lax.all_to_all(pay, Z, 0, 0)
 
     proj, sq, xt, ct = call(
         project_kernel, "project",
-        [((T, 4 * R), BF), ((T, 1), F32), ((SLICE, T), BF), ((SLICE, T), BF)],
-        [SM, VM, VM, VM, VM],
-        [pltpu.VMEM((5 * R, T), BF)], flops=3 * flops, size=5 << 20,
-    )(at, inputs, cotangent, w1, w2)
-    proj = lax.all_gather(proj, Z, axis=0)
-
-    (part,) = call(gram_kernel, "gram", [((S, 32, R), BF)], [SM, VM, VM, VM], flops=flops // 2, size=3 << 20)(at, got, w1, w2)
+        [((T, 3 * R), BF), ((T, 1), F32), ((SLICE, T), BF), ((SLICE, T), BF)],
+        [VM, VM, VM, VM],
+        [pltpu.VMEM((5 * R, T), BF)], flops=3 * flops, size=5 << 20, vmem=12,
+    )(inputs, cotangent, w1, w2)
+
+    (part,) = call(
+        gram_kernel, "gram", [((S, 32 + 3 * T, R), BF)], [VM, VM, VM, VM], flops=flops // 2, size=3 << 20, vmem=12
+    )(got, w1, w2, proj)
+    part, got = lax.optimization_barrier((part, got))
     part = lax.all_to_all(part, Z, 0, 0)
-    piece = got[:, ROWS : 2 * ROWS]
-    shifts = [lax.ppermute(piece, X, [(i, (i + d) % 4) for i in range(4)]) for d in (1, 2, 3)]
-    wown = jnp.stack([piece] + shifts)
-    woth = lax.ppermute(wown, C, swap)
+    own_w = got[:, ROWS : 2 * ROWS]
     ls = got[:, 2 * ROWS :]
-
-    kown = lax.all_to_all(jnp.broadcast_to(part, (16, S, 32, R)), (Y, X), 0, 0)
+    own_w = jnp.stack([own_w] + shifted(own_w, X, 4))
+    part, own_w = lax.optimization_barrier((part, own_w))
+
+    kown = lax.all_to_all(jnp.broadcast_to(part[:, :32], (16, S, 32, R)), (Y, X), 0, 0)
+    other_w = lax.ppermute(own_w, C, swap)
+    kown, other_w = lax.optimization_barrier((kown, other_w))
     koth = lax.ppermute(kown, C, swap)
 
-    anywhere = pl.BlockSpec(memory_space=pl.ANY)
     gown, goth, norm = call(
         main_kernel, "main",
-        [((16, 2 * ROWS, R), BF), ((16, 2 * ROWS, R), BF), ((S, 8, R), F32)],
-        [SM, VM, VM, VM, VM, anywhere, anywhere, VM, VM, VM],
+        [((16, 2 * ROWS, R), BF), ((16, 2 * ROWS, R), BF), ((2 * S, 8, R), F32)],
+        [VM, VM, VM, VM, anywhere, anywhere, VM, VM, VM],
         [
             pltpu.VMEM((S * R, S * R), BF),
             pltpu.VMEM((T, S * R), F32),
@@ -329,19 +385,18 @@
             pltpu.VMEM((S, R, SLICE), F32),
             pltpu.SemaphoreType.DMA((8,)),
         ],
-        flops=2 * 32 * SLICE * T * R + 2 * 192 * T * R * R, size=10 << 20, trans=S * T * R,
-    )(at, kown, koth, proj, sq, wown, woth, xt, ct, ls)
+        flops=2 * 32 * SLICE * T * R + 2 * 192 * T * R * R, size=10 << 20, trans=S * T * R, vmem=28,
+    )(kown, koth, part, sq, own_w, other_w, xt, ct, ls)
 
     ggot = lax.ppermute(goth, C, swap)
-    total = jnp.sum(lax.all_to_all(norm, Z, 0, 0), axis=0)
-    factor = CLIP_NORM / (jnp.sqrt(total) + CLIP_OFFSET)
-    other = lax.ppermute(factor, C, swap)
-    both = (gown.astype(F32) * factor[0, 0] + ggot.astype(F32) * other[0, 0]).astype(BF)
+    norm = lax.all_to_all(norm, (Z, C), 0, 0)
+    (both,) = call(mix_kernel, "mix", [((16, 2 * ROWS, R), BF)], [VM, VM, VM], size=4 << 20)(norm, gown, ggot)
     both = lax.all_to_all(both, (Y, X), 0, 0)
-    gi, go = call(sum_kernel, "sum", [((ROWS, R), BF), ((S, 8, SLICE), F32)], [VM], size=2 << 20)(both)
+    (go,) = call(sum_out_kernel, "sum_out", [((S, 8, SLICE), F32)], [VM], size=1 << 20)(both)
+    go = lax.all_to_all(go, Z, 0, 0)
+    (gi,) = call(sum_in_kernel, "sum_in", [((ROWS, R), BF)], [VM], size=1 << 20)(both)
     route = [(k * 32 + s * 4 + j, s * 32 + k * 4 + j) for k in range(S) for s in range(S) for j in range(4)]
     grad_in = lax.ppermute(gi, (Z, Y, X, C), route).astype(F32)[None]
-    go = lax.all_to_all(go, Z, 0, 0)
     (grad_out,) = call(join_kernel, "join", [((1, 4, D), F32)], [VM])(go)
     return grad_in, grad_out
 

time: 183 us -> 152 us (0.83)
  blocking collectives: 75.9 us -> 56.2 us
  between operations: 14.2 us -> 0.76 us
  local copies, waits for them, and re-layouts: 15.2 us -> 5 us
  waiting for transfers between devices: 37.3 us -> 46.8 us
  starting transfers between devices: 22.3 us -> 26.3 us
  other arithmetic: 2.64 us -> 0.79 us
    all_to_all x1 -> x2, waiting for transfers between devices: 0.01 us -> 22.8 us  [the longest x1 15.1 us: per_device(): got = lax.all_to_all(pay, Z, 0, 0)]
    all_to_all x3 -> x2, blocking collectives: 51.3 us -> 34.2 us  [the longest x1 23.8 us: per_device(): lax.all_to_all(jnp.broadcast_to(part[:, :32], (16, S, 32, R)), (Y, X), 0, 0)]
    all_gather x1 -> x0, waiting for transfers between devices: 16.4 us -> none  [per_device(): proj = lax.all_gather(proj, Z, axis=0)]
    unnamed x34 -> x12, local copies, waits for them, and re-layouts: 11.2 us -> 4.72 us
    all_to_all x1 -> x2, starting transfers between devices: 7.61 us -> 12.2 us  [the longest x1 8.61 us: per_device(): got = lax.all_to_all(pay, Z, 0, 0)]
    ppermute x1, waiting for transfers between devices: 0.01 us -> 2.65 us  [per_device(): koth = lax.ppermute(kown, C, swap)]
    all_to_all x1, blocking collectives: 24.6 us -> 22 us  [per_device(): both = lax.all_to_all(both, (Y, X), 0, 0)]
    pallas_call x4 -> x6, Pallas kernels: 4.6 us -> 6.81 us  [the longest x1 3.77 us: per_device(): call(pack_kernel, 'pack', [((R, D), BF), ((S, 2 * ROWS + 16, R), BF)], [a...]
  transfers between devices with their start and end apart: 11 -> 10, of which waited for: 6 -> 6; matrix products, arithmetic and copies ran while one was open for 2% -> 1% of each run, Pallas kernels for 1% -> 1%
where the time goes in v3:
time: 152 us
  blocking collectives  56.2 us (37%)
  waiting for transfers between devices  46.8 us (31%)
  starting transfers between devices  26.3 us (17%)
  Pallas kernels  15.7 us (10%)
  local copies, waits for them, and re-layouts  5 us (3%)
    all_to_all x1, blocking collectives, per_device(): lax.all_to_all(jnp.broadcast_to(part[:, :32], (16, S, 32, R)), (Y, X), 0, 0)  23.8 us
    all_to_all x1, blocking collectives, per_device(): both = lax.all_to_all(both, (Y, X), 0, 0)  22 us
    all_to_all x1, waiting for transfers between devices, per_device(): got = lax.all_to_all(pay, Z, 0, 0)  15.1 us
    ppermute x3, waiting for transfers between devices, shifted(): lax.ppermute(value, axis, [(i, (i + d) % size) for i in range(size)])  12.6 us
    all_to_all x1, blocking collectives, per_device(): norm = lax.all_to_all(norm, (Z, C), 0, 0)  10.4 us
    all_to_all x1, starting transfers between devices, per_device(): go = lax.all_to_all(go, Z, 0, 0)  8.9 us
    all_to_all x1, waiting for transfers between devices, per_device(): go = lax.all_to_all(go, Z, 0, 0)  8.78 us
    all_to_all x1, starting transfers between devices, per_device(): got = lax.all_to_all(pay, Z, 0, 0)  8.61 us
  transfers between devices with their start and end apart: 10, of which 6 were waited for; matrix products, arithmetic and copies ran while one was open for 1% of the time, Pallas kernels for 1%

profile of v3, /device:TPU:2, one launch (start us, length us, event | category | flops | bytes accessed | tf_op | source)
XLA Modules:
  0.0 151.5 jit_solution(13668390008044338890)
XLA Ops:
  0.6 3.8 %pack.1 = (bf16[128,4608]{1,0:T(8,128)(2,1)}, bf16[8,304,128]{2,1,0:T(8,128)(2,1)}) custom-call(bf16[4608,128]{1,0:T(8,128)(2,1)} %bitcast.10, bf16[128,4608]{1,0:T(8,128)(2,1)} %bitcast.13, f32[1,4608]{1,0:T(1,128)} %ls_ref.1), custom_call_target="tpu_custom_call" | custom-call | flops 9437184 | bytes 4194304 | tf_op jit(solution)/shard_map/pack/pallas_call | solution.py:338
  4.4 0.0 copy-start
  4.4 8.6 %all-to-all-start = ((bf16[8,304,128]{2,1,0:T(8,128)(2,1)}), bf16[8,304,128]{2,1,0:T(8,128)(2,1)S(1)}, u32[]{:S(2)}, u32[]{:S(2)}) async-start(bf16[8,304,128]{2,1,0:T(8,128)(2,1)} %get-tuple-element.17), calls=%async_computation | async-start | bytes 1245184 | tf_op jit(solution)/shard_map/all_to_all | solution.py:345
  13.0 0.0 copy-done
  13.0 0.0 copy-start.1
  13.0 1.3 copy-done.1
  14.3 0.0 copy-start.4
  14.3 1.3 copy-done.4
  15.6 0.0 copy-start.5
  15.6 1.3 copy-done.5
  16.9 0.0 copy-start.2
  16.9 1.1 project.1
  18.0 15.1 %all-to-all-done.got_ref = bf16[8,304,128]{2,1,0:T(8,128)(2,1)S(1)} async-done(((bf16[8,304,128]{2,1,0:T(8,128)(2,1)}), bf16[8,304,128]{2,1,0:T(8,128)(2,1)S(1)}, u32[]{:S(2)}, u32[]{:S(2)}) %all-to-all-start) | async-done | bytes 622624 | tf_op jit(solution)/shard_map/all_to_all | solution.py:345
  33.0 0.0 copy-done.2
  33.0 0.7 gram.1
  33.7 0.0 copy-start.3
  33.7 0.9 copy-done.3
  34.6 3.5 %all-to-all-start.1 = ((bf16[8,416,128]{2,1,0:T(8,128)(2,1)}), bf16[8,416,128]{2,1,0:T(8,128)(2,1)S(1)}, u32[]{:S(2)}, u32[]{:S(2)}) async-start(bf16[8,416,128]{2,1,0:T(8,128)(2,1)} %copy-done.3), calls=%async_computation.1 | async-start | bytes 1703936 | tf_op jit(solution)/shard_map/all_to_all | solution.py:358
  38.2 0.1 slice_bitcast_fusion
  38.3 2.3 %collective-permute-start.1 = (bf16[8,144,128]{2,1,0:T(8,128)(2,1)S(1)}, bf16[8,144,128]{2,1,0:T(8,128)(2,1)S(1)}, u32[]{:S(2)}, u32[]{:S(2)}) collective-permute-start(bf16[8,144,128]{2,1,0:T(8,128)(2,1)S(1)} %get-tuple-element.33), channel_id=1, source_target_pairs={{0,4},{2,6},{4,0},{6,2},{1,5},{3,7},{5,1},{7,3},{8,12},{10,14},{12... | collective-permute-start | bytes 884744 | tf_op jit(solution)/shard_map/ppermute | solution.py:329
  40.6 0.0 collective-permute-start
  40.6 2.0 %collective-permute-start.2 = (bf16[8,144,128]{2,1,0:T(8,128)(2,1)S(1)}, bf16[8,144,128]{2,1,0:T(8,128)(2,1)S(1)}, u32[]{:S(2)}, u32[]{:S(2)}) collective-permute-start(bf16[8,144,128]{2,1,0:T(8,128)(2,1)S(1)} %get-tuple-element.33), channel_id=1, source_target_pairs={{0,6},{2,0},{4,2},{6,4},{1,7},{3,1},{5,3},{7,5},{8,14},{10,8},{12,... | collective-permute-start | bytes 884744 | tf_op jit(solution)/shard_map/ppermute | solution.py:329
  42.6 7.2 %collective-permute-done.1 = bf16[8,144,128]{2,1,0:T(8,128)(2,1)S(1)} collective-permute-done((bf16[8,144,128]{2,1,0:T(8,128)(2,1)S(1)}, bf16[8,144,128]{2,1,0:T(8,128)(2,1)S(1)}, u32[]{:S(2)}, u32[]{:S(2)}) %collective-permute-start.1) | collective-permute-done | bytes 294944 | tf_op jit(solution)/shard_map/ppermute | solution.py:329
  49.8 5.4 %collective-permute-done = bf16[8,144,128]{2,1,0:T(8,128)(2,1)S(1)} collective-permute-done((bf16[8,144,128]{2,1,0:T(8,128)(2,1)S(1)}, bf16[8,144,128]{2,1,0:T(8,128)(2,1)S(1)}, u32[]{:S(2)}, u32[]{:S(2)}) %collective-permute-start) | collective-permute-done | bytes 294944 | tf_op jit(solution)/shard_map/ppermute | solution.py:329
  55.2 0.0 collective-permute-done.2
  55.2 0.1 pad_maximum_fusion.refs_2_
  55.4 7.7 %all-to-all-done.1.refs_0_ = bf16[8,416,128]{2,1,0:T(8,128)(2,1)S(1)} async-done(((bf16[8,416,128]{2,1,0:T(8,128)(2,1)}), bf16[8,416,128]{2,1,0:T(8,128)(2,1)S(1)}, u32[]{:S(2)}, u32[]{:S(2)}) %all-to-all-start.1) | async-done | bytes 852000 | tf_op jit(solution)/shard_map/all_to_all | solution.py:358
  63.1 0.0 collective-permute-start.3
  63.1 0.2 broadcast_in_dim.9
  63.3 23.8 %all_to_all.30.own_ref = bf16[16,8,32,128]{3,2,1,0:T(8,128)(2,1)S(1)} all-to-all(bf16[16,8,32,128]{3,2,1,0:T(8,128)(2,1)S(1)} %broadcast_in_dim.9), channel_id=1, replica_groups=mesh['section'=8,'y'=4,'x'=4,'core'=2] {'y','x'}, dimensions={0} | all-to-all | bytes 2097152 | tf_op jit(solution)/shard_map/all_to_all | solution.py:364
  87.1 0.0 collective-permute-done.3.refs_3_
  87.1 0.0 collective-permute-start.4
  87.1 2.7 %collective-permute-done.4.oth_ref = bf16[16,8,32,128]{3,2,1,0:T(8,128)(2,1)S(1)} collective-permute-done((bf16[16,8,32,128]{3,2,1,0:T(8,128)(2,1)S(1)}, bf16[16,8,32,128]{3,2,1,0:T(8,128)(2,1)S(1)}, u32[]{:S(2)}, u32[]{:S(2)}) %collective-permute-start.4) | collective-permute-done | bytes 1048608 | tf_op jit(solution)/shard_map/ppermute | solution.py:367
  89.7 8.1 %main.1 = (bf16[16,288,128]{2,1,0:T(8,128)(2,1)S(1)}, bf16[16,288,128]{2,1,0:T(8,128)(2,1)S(1)}, f32[16,8,128]{2,1,0:T(8,128)S(1)}) custom-call(bf16[16,8,32,128]{3,2,1,0:T(8,128)(2,1)S(1)} %all_to_all.30.own_ref, bf16[16,8,32,128]{3,2,1,0:T(8,128)(2,1)S(1)} %collective-permute-done.4.oth_ref, bf16[8,416,128]{2,1,0:T(8,128)(2,1)S(1)} %all-to-all-done.1.refs_0_, ...), custom_call_target="tpu_custom_call" | custom-call | flops 1409286144 | bytes 10485760 | tf_op jit(solution)/shard_map/main/pallas_call | solution.py:369
  97.9 0.2 collective-permute-start.5
  98.1 10.4 %all_to_all.31.norm_ref = f32[16,8,128]{2,1,0:T(8,128)S(1)} all-to-all(f32[16,8,128]{2,1,0:T(8,128)S(1)} %get-tuple-element.29), channel_id=1, replica_groups=mesh['section'=8,'y'=4,'x'=4,'core'=2] {'section','core'}, dimensions={0} | all-to-all | bytes 131072 | tf_op jit(solution)/shard_map/all_to_all | solution.py:392
  108.5 0.0 collective-permute-done.5.got_ref
  108.5 0.4 mix.1
  108.9 22.0 %all_to_all.32.got_ref = bf16[16,288,128]{2,1,0:T(8,128)(2,1)S(1)} all-to-all(bf16[16,288,128]{2,1,0:T(8,128)(2,1)S(1)} %mix.1), channel_id=1, replica_groups=mesh['section'=8,'y'=4,'x'=4,'core'=2] {'y','x'}, dimensions={0} | all-to-all | bytes 2359296 | tf_op jit(solution)/shard_map/all_to_all | solution.py:394
  130.9 0.1 sum_in.1
  131.0 0.7 collective-permute-start.6
  131.7 0.8 sum_out.1
  132.5 8.9 %all-to-all-start.5 = ((f32[8,8,576]{2,1,0:T(8,128)}), f32[8,8,576]{2,1,0:T(8,128)S(1)}, u32[]{:S(2)}, u32[]{:S(2)}) async-start(f32[8,8,576]{2,1,0:T(8,128)} %sum_out.1), calls=%async_computation.5 | async-start | bytes 327680 | tf_op jit(solution)/shard_map/all_to_all | solution.py:396
  141.4 0.0 collective-permute-done.6
  141.4 0.6 bitcast_convert_fusion
  142.0 8.8 %all-to-all-done.5.got_ref = f32[8,8,576]{2,1,0:T(8,128)S(1)} async-done(((f32[8,8,576]{2,1,0:T(8,128)}), f32[8,8,576]{2,1,0:T(8,128)S(1)}, u32[]{:S(2)}, u32[]{:S(2)}) %all-to-all-start.5) | async-done | bytes 147488 | tf_op jit(solution)/shard_map/all_to_all | solution.py:396
  150.8 0.7 join.1
  (2 shorter events, 0.0 us)
Async XLA Ops:
  4.4 8.6 %copy-start = (bf16[1,4608,128]{2,1,0:T(8,128)(2,1)S(1)}, bf16[1,4608,128]{2,1,0:T(8,128)(2,1)}, u32[]{:S(2)}) copy-start(bf16[1,4608,128]{2,1,0:T(8,128)(2,1)} %param.6) | copy-start | bytes 3538948
  4.4 28.6 %all-to-all-start = ((bf16[8,304,128]{2,1,0:T(8,128)(2,1)}), bf16[8,304,128]{2,1,0:T(8,128)(2,1)S(1)}, u32[]{:S(2)}, u32[]{:S(2)}) async-start(bf16[8,304,128]{2,1,0:T(8,128)(2,1)} %get-tuple-element.17), calls=%async_computation | async-start | bytes 1245184 | tf_op jit(solution)/shard_map/all_to_all | solution.py:345
  13.0 1.3 copy-start.1
  14.3 1.3 copy-start.4
  15.6 1.3 copy-start.5
  16.9 16.2 %copy-start.2 = (bf16[128,4608]{1,0:T(8,128)(2,1)S(1)}, bf16[128,4608]{1,0:T(8,128)(2,1)}, u32[]{:S(2)}) copy-start(bf16[128,4608]{1,0:T(8,128)(2,1)} %get-tuple-element.18.w2_ref) | copy-start | bytes 3538948
  33.7 0.9 copy-start.3
  34.6 28.4 %all-to-all-start.1 = ((bf16[8,416,128]{2,1,0:T(8,128)(2,1)}), bf16[8,416,128]{2,1,0:T(8,128)(2,1)S(1)}, u32[]{:S(2)}, u32[]{:S(2)}) async-start(bf16[8,416,128]{2,1,0:T(8,128)(2,1)} %copy-done.3), calls=%async_computation.1 | async-start | bytes 1703936 | tf_op jit(solution)/shard_map/all_to_all | solution.py:358
  38.3 11.5 %collective-permute-start.1 = (bf16[8,144,128]{2,1,0:T(8,128)(2,1)S(1)}, bf16[8,144,128]{2,1,0:T(8,128)(2,1)S(1)}, u32[]{:S(2)}, u32[]{:S(2)}) collective-permute-start(bf16[8,144,128]{2,1,0:T(8,128)(2,1)S(1)} %get-tuple-element.33), channel_id=1, source_target_pairs={{0,4},{2,6},{4,0},{6,2},{1,5},{3,7},{5,1},{7,3},{8,12},{10,14},{12... | collective-permute-start | bytes 884744 | tf_op jit(solution)/shard_map/ppermute | solution.py:329
  40.6 14.6 %collective-permute-start = (bf16[8,144,128]{2,1,0:T(8,128)(2,1)S(1)}, bf16[8,144,128]{2,1,0:T(8,128)(2,1)S(1)}, u32[]{:S(2)}, u32[]{:S(2)}) collective-permute-start(bf16[8,144,128]{2,1,0:T(8,128)(2,1)S(1)} %get-tuple-element.33), channel_id=1, source_target_pairs={{0,2},{2,4},{4,6},{6,0},{1,3},{3,5},{5,7},{7,1},{8,10},{10,12},{12... | collective-permute-start | bytes 884744 | tf_op jit(solution)/shard_map/ppermute | solution.py:329
  40.6 14.6 %collective-permute-start.2 = (bf16[8,144,128]{2,1,0:T(8,128)(2,1)S(1)}, bf16[8,144,128]{2,1,0:T(8,128)(2,1)S(1)}, u32[]{:S(2)}, u32[]{:S(2)}) collective-permute-start(bf16[8,144,128]{2,1,0:T(8,128)(2,1)S(1)} %get-tuple-element.33), channel_id=1, source_target_pairs={{0,6},{2,0},{4,2},{6,4},{1,7},{3,1},{5,3},{7,5},{8,14},{10,8},{12,... | collective-permute-start | bytes 884744 | tf_op jit(solution)/shard_map/ppermute | solution.py:329
  63.1 24.0 %collective-permute-start.3 = (bf16[4,8,144,128]{3,2,1,0:T(8,128)(2,1)S(1)}, bf16[4,8,144,128]{3,2,1,0:T(8,128)(2,1)S(1)}, u32[]{:S(2)}, u32[]{:S(2)}) collective-permute-start(bf16[4,8,144,128]{3,2,1,0:T(8,128)(2,1)S(1)} %pad_maximum_fusion.refs_2_), channel_id=1, source_target_pairs={{0,1},{1,0},{2,3},{3,2},{4,5},{5,4},{6,7},{7,6},{8,9},{9,8},{10,11... | collective-permute-start | bytes 3538952 | tf_op jit(solution)/shard_map/ppermute | solution.py:365
  87.1 2.7 %collective-permute-start.4 = (bf16[16,8,32,128]{3,2,1,0:T(8,128)(2,1)S(1)}, bf16[16,8,32,128]{3,2,1,0:T(8,128)(2,1)S(1)}, u32[]{:S(2)}, u32[]{:S(2)}) collective-permute-start(bf16[16,8,32,128]{3,2,1,0:T(8,128)(2,1)S(1)} %all_to_all.30.own_ref), channel_id=1, source_target_pairs={{0,1},{1,0},{2,3},{3,2},{4,5},{5,4},{6,7},{7,6},{8,9},{9,8},{10,11... | collective-permute-start | bytes 3145736 | tf_op jit(solution)/shard_map/ppermute | solution.py:367
  97.9 10.6 %collective-permute-start.5 = (bf16[16,288,128]{2,1,0:T(8,128)(2,1)S(1)}, bf16[16,288,128]{2,1,0:T(8,128)(2,1)S(1)}, u32[]{:S(2)}, u32[]{:S(2)}) collective-permute-start(bf16[16,288,128]{2,1,0:T(8,128)(2,1)S(1)} %get-tuple-element.31), channel_id=1, source_target_pairs={{0,1},{1,0},{2,3},{3,2},{4,5},{5,4},{6,7},{7,6},{8,9},{9,8},{10,11... | collective-permute-start | bytes 3538952 | tf_op jit(solution)/shard_map/ppermute | solution.py:391
  131.0 10.3 %collective-permute-start.6 = (bf16[144,128]{1,0:T(8,128)(2,1)S(1)}, bf16[144,128]{1,0:T(8,128)(2,1)S(1)}, u32[]{:S(2)}, u32[]{:S(2)}) collective-permute-start(bf16[144,128]{1,0:T(8,128)(2,1)S(1)} %sum_in.1), channel_id=1, source_target_pairs={{0,0},{1,1},{2,2},{3,3},{4,32},{5,33},{6,34},{7,35},{8,64},{9,65},... | collective-permute-start | bytes 110600 | tf_op jit(solution)/shard_map/ppermute | solution.py:399
  132.5 18.3 %all-to-all-start.5 = ((f32[8,8,576]{2,1,0:T(8,128)}), f32[8,8,576]{2,1,0:T(8,128)S(1)}, u32[]{:S(2)}, u32[]{:S(2)}) async-start(f32[8,8,576]{2,1,0:T(8,128)} %sum_out.1), calls=%async_computation.5 | async-start | bytes 327680 | tf_op jit(solution)/shard_map/all_to_all | solution.py:396

commit v4 on v3

--- a/solution.py
+++ b/solution.py
@@ -15,7 +15,9 @@
 D = 4608
 SLICE = D // S
 QUARTER = SLICE // 4
-PACK_VMEM = 60
+PACK_VMEM = 56
+DIRECT = 6
+TAIL_FLOPS = 20 * 10**9
 Z, Y, X, C = "section", "y", "x", "core"
 BF = jnp.bfloat16
 F32 = jnp.float32
@@ -26,6 +28,7 @@
 HALF = D // 2
 ROWS = D * 4 // R
 VM = pl.BlockSpec(memory_space=pltpu.VMEM)
+SPREAD = VM
 
 
 def mm(a, b, dims=NN):
@@ -40,93 +43,124 @@
     )
 
 
-def call(kernel, name, outs, ins, scratch=(), flops=0, size=1 << 21, trans=0, vmem=8):
+def call(kernel, name, outs, ins, scratch=(), flops=0, size=1 << 21, trans=0, vmem=8, to=None, alias=None):
     return pl.pallas_call(
         kernel,
         out_shape=tuple(jax.ShapeDtypeStruct(*o) for o in outs),
         in_specs=list(ins),
-        out_specs=(VM,) * len(outs),
+        out_specs=tuple(to or [VM] * len(outs)),
         scratch_shapes=list(scratch),
+        input_output_aliases=alias or {},
         compiler_params=pltpu.CompilerParams(vmem_limit_bytes=vmem << 20),
         cost_estimate=pl.CostEstimate(flops=flops, bytes_accessed=size, transcendentals=trans),
         name=name,
     )
 
 
-def pack_kernel(w_in_ref, w_out_ref, ls_ref, w2_ref, pay_ref, wide, turned, sem):
+def pack_kernel(w_in_ref, w_out_ref, ls_ref, pay_ref, rows, wide, turned, strip, sem):
     y, x, core = lax.axis_index(Y), lax.axis_index(X), lax.axis_index(C)
     q = (x * 2 + core) * 4 + y
-    step = D // 4
-    loads = [
-        pltpu.make_async_copy(w_out_ref.at[:, pl.ds(i * step, step)], wide.at[:, pl.ds(i * step, step)], sem.at[i])
-        for i in range(4)
-    ]
-    for cp in loads:
-        cp.start()
-
-    def piece(k):
-        return pl.ds(pl.multiple_of(SLICE * k + QUARTER * x, 16), QUARTER)
-
-    def feature_copies():
+    row_copy = pltpu.make_async_copy(w_out_ref.at[pl.ds(pl.multiple_of((q // 4) * 16, 16), 16)], rows, sem.at[0])
+    row_copy.start()
+    first = [SLICE * k + QUARTER * x for k in range(S)]
+
+    def in_copies():
         return [
-            pltpu.make_async_copy(w_in_ref.at[piece(k)], pay_ref.at[k, pl.ds(ROWS, QUARTER)], sem.at[4 + k])
+            pltpu.make_async_copy(
+                w_in_ref.at[pl.ds(pl.multiple_of(first[k], 16), QUARTER)],
+                pay_ref.at[k, pl.ds(ROWS, QUARTER)] if k < DIRECT else turned.at[k, pl.ds(0, QUARTER)],
+                sem.at[1 + k],
+            )
             for k in range(S)
         ]
 
+    def out_copies():
+        return [
+            pltpu.make_async_copy(
+                w_out_ref.at[:, pl.ds(pl.multiple_of((first[k] // R) * R, R), 2 * R)], wide.at[k], sem.at[1 + k]
+            )
+            for k in range(S)
+        ]
+
     @pl.when(core == 0)
     def _():
-        for cp in feature_copies():
+        for cp in in_copies():
             cp.start()
 
+    @pl.when(core != 0)
+    def _():
+        for cp in out_copies():
+            cp.start()
+
+    row_copy.wait()
+    block = rows[...].astype(F32) * ls_ref[...]
+    group = q % 4
+    mine = jnp.where(group < 2, block[:8], block[8:])
+    turn = pltpu.roll(mine, 4, axis=0)
+    odd = group % 2 == 1
+    low = lax.broadcasted_iota(jnp.int32, (8, HALF), 0) < 4
+    mine = jnp.where(
+        low,
+        jnp.where(odd, turn[:, :HALF], mine[:, :HALF]),
+        jnp.where(odd, mine[:, HALF:], turn[:, HALF:]),
+    )
+    for u in range(9):
+        two = jnp.concatenate([mine[:, 256 * u : 256 * u + R], mine[:, 256 * u + R : 256 * (u + 1)]], axis=0)
+        strip[16 * u : 16 * u + 16] = two.astype(BF)
+    sends = [pltpu.make_async_copy(strip, pay_ref.at[k, pl.ds(0, ROWS)], sem.at[9 + k]) for k in range(S)]
+    for cp in sends:
+        cp.start()
+
+    @pl.when(core == 0)
+    def _():
+        copies = in_copies()
+        outs = []
+        for k in range(DIRECT, S):
+            copies[k].wait()
+            out = pltpu.make_async_copy(turned.at[k, pl.ds(0, QUARTER)], pay_ref.at[k, pl.ds(ROWS, QUARTER)], sem.at[17 + k])
+            out.start()
+            outs.append(out)
+        for cp in copies[:DIRECT] + outs:
+            cp.wait()
+
+    @pl.when(core != 0)
+    def _():
+        copies = []
+        for k, cp in enumerate(out_copies()):
+            cp.wait()
+            base = pl.multiple_of((first[k] // R) * R, R)
+            for i in range(2):
+                part = wide[k, :, i * R : (i + 1) * R].astype(F32) * ls_ref[:, pl.ds(base + i * R, R)]
+                turned[k, i * R : (i + 1) * R, :] = part.T.astype(BF)
+            start = pl.multiple_of(first[k] % R, 16)
+            out = pltpu.make_async_copy(turned.at[k, pl.ds(start, QUARTER)], pay_ref.at[k, pl.ds(ROWS, QUARTER)], sem.at[17 + k])
+            out.start()
+            copies.append(out)
+        for out in copies:
+            out.wait()
+
+    for cp in sends:
+        cp.wait()
+
+
+def project_kernel(x_ref, c_ref, w_in_ref, w_out_ref, ls_ref, proj, scales, sq_ref, xt_ref, ct_ref, wide):
+    z = lax.axis_index(Z)
+    xv = x_ref[...]
     ls = ls_ref[...]
+    w2 = (w_out_ref[...].astype(F32) * ls).astype(BF)
+    proj[:T] = mm(xv, w_in_ref[...]).astype(BF)
+    proj[T : 2 * T] = mm(xv, w2, NT).astype(BF)
+    proj[2 * T :] = mm(c_ref[...], w2, NT).astype(BF)
     top = ls.astype(BF).astype(F32)
     low_part = ls - top
     for k in range(S):
-        rows = []
+        lines = []
         for part in (top, low_part):
-            rows += [part[:, SLICE * k + R * j : SLICE * k + R * (j + 1)] for j in range(4)]
+            lines += [part[:, SLICE * k + R * j : SLICE * k + R * (j + 1)] for j in range(4)]
             tail = part[:, SLICE * k + 512 : SLICE * (k + 1)]
-            rows.append(jnp.concatenate([tail, tail], axis=1))
-        rows.append(jnp.zeros((6, R), F32))
-        pay_ref[k, 2 * ROWS : 2 * ROWS + 16] = jnp.concatenate(rows, axis=0).astype(BF)
-    row = lax.broadcasted_iota(jnp.int32, (8, R), 0) % 4
-    col = lax.broadcasted_iota(jnp.int32, (8, R), 1)
-    pick = (col == q * 4 + row).astype(BF)
-    mine = []
-    for i, cp in enumerate(loads):
-        cp.wait()
-        at = slice(i * step, (i + 1) * step)
-        part = (wide[:, at].astype(F32) * ls[:, at]).astype(BF)
-        w2_ref[:, at] = part
-        mine.append(mm(pick, part))
-    mine = jnp.concatenate(mine, axis=1)
-    low = lax.broadcasted_iota(jnp.int32, (8, HALF), 0) < 4
-    mine = jnp.where(low, mine[:, :HALF], mine[:, HALF:])
-    for u in range(9):
-        two = jnp.concatenate([mine[:, 256 * u : 256 * u + R], mine[:, 256 * u + R : 256 * (u + 1)]], axis=0).astype(BF)
-        for k in range(S):
-            pay_ref[k, 16 * u : 16 * u + 16] = two
-
-    @pl.when(core == 0)
-    def _():
-        for cp in feature_copies():
-            cp.wait()
-
-    @pl.when(core != 0)
-    def _():
-        for t in range(D // R):
-            turned[t * R : (t + 1) * R, :] = w2_ref[:, t * R : (t + 1) * R].astype(F32).T.astype(BF)
-        for k in range(S):
-            pay_ref[k, ROWS : 2 * ROWS] = turned[piece(k), :]
-
-
-def project_kernel(x_ref, c_ref, w_in_ref, w2_ref, proj_ref, sq_ref, xt_ref, ct_ref, wide):
-    z = lax.axis_index(Z)
-    xv = x_ref[...]
-    w2 = w2_ref[...]
-    proj_ref[:, :R] = mm(xv, w_in_ref[...]).astype(BF)
-    proj_ref[:, R : 2 * R] = mm(xv, w2, NT).astype(BF)
-    proj_ref[:, 2 * R :] = mm(c_ref[...], w2, NT).astype(BF)
+            lines.append(jnp.concatenate([tail, tail], axis=1))
+        lines.append(jnp.zeros((6, R), F32))
+        scales[k] = jnp.concatenate(lines, axis=0).astype(BF)
     xf = xv.astype(F32)
     sq_ref[...] = jnp.sum(xf * xf, axis=1, keepdims=True)
     base = pl.multiple_of(((z * 9) // 2) * R, R)
@@ -137,8 +171,13 @@
         dst[...] = wide[pl.ds(off, SLICE), :]
 
 
-def gram_kernel(got_ref, w_in_ref, w2_ref, proj_ref, out_ref):
+def gram_kernel(got_ref, w_in_ref, w_out_ref, ls_ref, proj_ref, scales_ref, out_ref, row, sem):
     z = lax.axis_index(Z)
+    copies = [pltpu.make_async_copy(proj_ref, out_ref.at[k, pl.ds(32, 3 * T)], sem.at[k]) for k in range(S)]
+    copies.append(pltpu.make_async_copy(scales_ref, out_ref.at[:, pl.ds(32 + 3 * T, 16)], sem.at[S]))
+    for cp in copies:
+        cp.start()
+    ls = ls_ref[...]
     first, second = [], []
     for u in range(9):
         block = got_ref[:, 16 * u : 16 * u + 16, :].astype(F32)
@@ -150,18 +189,29 @@
     first = jnp.concatenate(first, axis=1)
     second = jnp.concatenate(second, axis=1)
     up = mm(first, w_in_ref[:HALF]) + mm(second, w_in_ref[HALF:])
-    down = mm(first, w2_ref[:, :HALF], NT) + mm(second, w2_ref[:, HALF:], NT)
+    down = mm((first.astype(F32) * ls[:, :HALF]).astype(BF), w_out_ref[:, :HALF], NT)
+    down = down + mm((second.astype(F32) * ls[:, HALF:]).astype(BF), w_out_ref[:, HALF:], NT)
     below = (lax.broadcasted_iota(jnp.int32, (32, R), 0) // 4) < z
     out = jnp.where(below, up, down).astype(BF)
-    for k in range(S):
-        out_ref[k, :32] = out
-        for i in range(3):
-            out_ref[k, 32 + T * i : 32 + T * (i + 1)] = proj_ref[:, i * R : (i + 1) * R]
+    row[...] = out
+    sends = [pltpu.make_async_copy(row, out_ref.at[k, pl.ds(0, 32)], sem.at[S + 1 + k]) for k in range(S)]
+    for cp in sends:
+        cp.start()
+    for cp in copies + sends:
+        cp.wait()
+
+
+def spread_kernel(part_ref, out_ref, sem):
+    copies = [pltpu.make_async_copy(part_ref.at[:, pl.ds(0, 32)], out_ref.at[i], sem.at[i]) for i in range(16)]
+    for cp in copies:
+        cp.start()
+    for cp in copies:
+        cp.wait()
 
 
 def main_kernel(own_ref, oth_ref, *refs):
-    proj_ref, sq_ref, wown_ref, woth_ref, xt_ref, ct_ref, ls_ref, gown_ref, goth_ref, norm_ref = refs[:10]
-    kmat, pre, qacc, hacc, slope, hs, hts, ps, sts, wbuf, xs, gos, sem = refs[10:]
+    proj_ref, sq_ref, wown_ref, woth_ref, xt_ref, ct_ref, gown_ref, goth_ref, norm_ref = refs[:9]
+    kmat, pre, qacc, hacc, slope, hs, hts, ps, sts, wbuf, xs, gos, sem = refs[9:]
     core = lax.axis_index(C)
     is0 = core == 0
     copies = []
@@ -256,7 +306,7 @@
             x = (xf + mm(weights(1, s), hs[s], NT)).astype(BF)
     g = ct_ref[...]
     for s in reversed(range(S)):
-        lsf = ls_ref[s].astype(F32)
+        lsf = proj_ref[s, 32 + 3 * T :].astype(F32)
         lsf = lsf[:5] + lsf[5:10]
         lrow = jnp.concatenate([lsf[j : j + 1] for j in range(4)] + [lsf[4:5, :64]], axis=1)
         gos[s] = mm(hts[s], g, NT) * lrow
@@ -313,16 +363,17 @@
     tail = jnp.concatenate([last[:, :64], last[:, 64:]], axis=0)
     go = jnp.concatenate([go[32 * t : 32 * t + 32] for t in range(4)] + [tail], axis=1).reshape(4, 8, SLICE)
     for i in range(4):
-        go_ref[2 * i] = go[i]
-        go_ref[2 * i + 1] = pltpu.roll(go[i], 4, axis=0)
+        go_ref[2 * i] = go[i][:4].astype(BF)
+        go_ref[2 * i + 1] = go[i][4:].astype(BF)
 
 
 def sum_in_kernel(got_ref, gi_ref):
     gi_ref[...] = fold(got_ref, slice(0, ROWS)).astype(BF)
 
 
-def join_kernel(got_ref, out_ref):
-    out_ref[0] = jnp.concatenate([got_ref[k, :4] for k in range(S)], axis=1)
+def join_kernel(got_ref, gi_ref, out_ref, in_ref):
+    in_ref[0] = gi_ref[...].astype(F32)
+    out_ref[0] = jnp.concatenate([got_ref[k].astype(F32) for k in range(S)], axis=1)
 
 
 def shifted(value, axis, size):
@@ -335,41 +386,52 @@
     flops = 2 * T * D * R
     anywhere = pl.BlockSpec(memory_space=pl.ANY)
 
-    w2, pay = call(
+    far = pl.BlockSpec(memory_space=pltpu.HBM)
+    (pay,) = call(
         pack_kernel, "pack",
-        [((R, D), BF), ((S, 2 * ROWS + 16, R), BF)],
+        [((S, 2 * ROWS, R), BF)],
         [anywhere, anywhere, VM],
-        [pltpu.VMEM((R, D), BF), pltpu.VMEM((D, R), BF), pltpu.SemaphoreType.DMA((12,))],
-        flops=flops // 16, size=4 << 20, vmem=PACK_VMEM,
+        [
+            pltpu.VMEM((16, D), BF),
+            pltpu.VMEM((S, R, 2 * R), BF),
+            pltpu.VMEM((S, 2 * R, R), BF),
+            pltpu.VMEM((ROWS, R), BF),
+            pltpu.SemaphoreType.DMA((25,)),
+        ],
+        flops=flops // 16, size=2 << 20, vmem=PACK_VMEM, to=[far],
     )(w1, w_out[0], layer_scale)
     got = lax.all_to_all(pay, Z, 0, 0)
 
-    proj, sq, xt, ct = call(
+    proj, scales, sq, xt, ct = call(
         project_kernel, "project",
-        [((T, 3 * R), BF), ((T, 1), F32), ((SLICE, T), BF), ((SLICE, T), BF)],
-        [VM, VM, VM, VM],
+        [((3 * T, R), BF), ((S, 16, R), BF), ((T, 1), F32), ((SLICE, T), BF), ((SLICE, T), BF)],
+        [VM, VM, VM, VM, VM],
         [pltpu.VMEM((5 * R, T), BF)], flops=3 * flops, size=5 << 20, vmem=12,
-    )(inputs, cotangent, w1, w2)
+    )(inputs, cotangent, w1, w_out[0], layer_scale)
 
     (part,) = call(
-        gram_kernel, "gram", [((S, 32 + 3 * T, R), BF)], [VM, VM, VM, VM], flops=flops // 2, size=3 << 20, vmem=12
-    )(got, w1, w2, proj)
+        gram_kernel, "gram", [((S, 48 + 3 * T, R), BF)], [VM] * 6,
+        [pltpu.VMEM((32, R), BF), pltpu.SemaphoreType.DMA((2 * S + 1,))],
+        flops=flops // 2, size=3 << 20, vmem=12, to=[far],
+    )(got, w1, w_out[0], layer_scale, proj, scales)
     part, got = lax.optimization_barrier((part, got))
     part = lax.all_to_all(part, Z, 0, 0)
     own_w = got[:, ROWS : 2 * ROWS]
-    ls = got[:, 2 * ROWS :]
     own_w = jnp.stack([own_w] + shifted(own_w, X, 4))
     part, own_w = lax.optimization_barrier((part, own_w))
 
-    kown = lax.all_to_all(jnp.broadcast_to(part[:, :32], (16, S, 32, R)), (Y, X), 0, 0)
+    (spread,) = call(
+        spread_kernel, "spread", [((16, S, 32, R), BF)], [VM], [pltpu.SemaphoreType.DMA((16,))], to=[SPREAD]
+    )(part)
+    kown = lax.all_to_all(spread, (Y, X), 0, 0)
+    kown, own_w = lax.optimization_barrier((kown, own_w))
+    koth = lax.ppermute(kown, C, swap)
     other_w = lax.ppermute(own_w, C, swap)
-    kown, other_w = lax.optimization_barrier((kown, other_w))
-    koth = lax.ppermute(kown, C, swap)
 
     gown, goth, norm = call(
         main_kernel, "main",
         [((16, 2 * ROWS, R), BF), ((16, 2 * ROWS, R), BF), ((2 * S, 8, R), F32)],
-        [VM, VM, VM, VM, anywhere, anywhere, VM, VM, VM],
+        [VM, VM, VM, VM, anywhere, anywhere, VM, VM],
         [
             pltpu.VMEM((S * R, S * R), BF),
             pltpu.VMEM((T, S * R), F32),
@@ -386,18 +448,19 @@
             pltpu.SemaphoreType.DMA((8,)),
         ],
         flops=2 * 32 * SLICE * T * R + 2 * 192 * T * R * R, size=10 << 20, trans=S * T * R, vmem=28,
-    )(kown, koth, part, sq, own_w, other_w, xt, ct, ls)
+    )(kown, koth, part, sq, own_w, other_w, xt, ct)
 
     ggot = lax.ppermute(goth, C, swap)
     norm = lax.all_to_all(norm, (Z, C), 0, 0)
     (both,) = call(mix_kernel, "mix", [((16, 2 * ROWS, R), BF)], [VM, VM, VM], size=4 << 20)(norm, gown, ggot)
     both = lax.all_to_all(both, (Y, X), 0, 0)
-    (go,) = call(sum_out_kernel, "sum_out", [((S, 8, SLICE), F32)], [VM], size=1 << 20)(both)
-    go = lax.all_to_all(go, Z, 0, 0)
-    (gi,) = call(sum_in_kernel, "sum_in", [((ROWS, R), BF)], [VM], size=1 << 20)(both)
+    (go_sent,) = call(sum_out_kernel, "sum_out", [((S, 4, SLICE), BF)], [VM], size=1 << 20)(both)
+    go = lax.all_to_all(go_sent, Z, 0, 0)
+    both, go_sent = lax.optimization_barrier((both, go_sent))
+    (gi,) = call(sum_in_kernel, "sum_in", [((ROWS, R), BF)], [VM], flops=TAIL_FLOPS, size=1 << 20)(both)
     route = [(k * 32 + s * 4 + j, s * 32 + k * 4 + j) for k in range(S) for s in range(S) for j in range(4)]
-    grad_in = lax.ppermute(gi, (Z, Y, X, C), route).astype(F32)[None]
-    (grad_out,) = call(join_kernel, "join", [((1, 4, D), F32)], [VM])(go)
+    gi = lax.ppermute(gi, (Z, Y, X, C), route)
+    grad_out, grad_in = call(join_kernel, "join", [((1, 4, D), F32), ((1, ROWS, R), F32)], [VM, VM])(go, gi)
     return grad_in, grad_out
 
 

time: 152 us -> 140 us (0.921)
  the two profiles are of different devices: /device:TPU:2 before, /device:TPU:160 now
where the time goes in v4:
time: 140 us
  blocking collectives  52.9 us (38%)
  starting transfers between devices  34.7 us (25%)
  waiting for transfers between devices  25.4 us (18%)
  Pallas kernels  22.4 us (16%)
  local copies, waits for them, and re-layouts  3.55 us (3%)
    all_to_all x1, blocking collectives, per_device(): both = lax.all_to_all(both, (Y, X), 0, 0)  21.3 us
    all_to_all x1, blocking collectives, per_device(): kown = lax.all_to_all(spread, (Y, X), 0, 0)  19.8 us
    all_to_all x1, blocking collectives, per_device(): norm = lax.all_to_all(norm, (Z, C), 0, 0)  11.8 us
    ppermute x1, waiting for transfers between devices, per_device(): gi = lax.ppermute(gi, (Z, Y, X, C), route)  10.3 us
    all_to_all x1, starting transfers between devices, per_device(): part = lax.all_to_all(part, Z, 0, 0)  9.53 us
    pallas_call x1, Pallas kernels, per_device(): call(pack_kernel, 'pack', [((S, 2 * ROWS, R), BF)], [anywhere, anywhere,...  8.86 us
    pallas_call x1, Pallas kernels, per_device(): call(main_kernel, 'main', [((16, 2 * ROWS, R), BF), ((16, 2 * ROWS, R), B...  8.15 us
    all_to_all x1, starting transfers between devices, per_device(): go = lax.all_to_all(go_sent, Z, 0, 0)  7.82 us
  transfers between devices with their start and end apart: 10, of which 7 were waited for; matrix products, arithmetic and copies ran while one was open for 0% of the time, Pallas kernels for 1%

profile of v4, /device:TPU:160, one launch (start us, length us, event | category | flops | bytes accessed | tf_op | source)
XLA Modules:
  0.0 139.8 jit_solution(17817180370693100022)
XLA Ops:
  0.6 0.0 copy-start.1
  0.6 0.0 copy-start.5
  0.6 8.9 %pack.1 = bf16[8,288,128]{2,1,0:T(8,128)(2,1)} custom-call(bf16[4608,128]{1,0:T(8,128)(2,1)} %bitcast.7, bf16[128,4608]{1,0:T(8,128)(2,1)} %bitcast.10, f32[1,4608]{1,0:T(1,128)} %ls_ref.5), custom_call_target="tpu_custom_call" | custom-call | flops 9437184 | bytes 2097152 | tf_op jit(solution)/shard_map/pack/pallas_call | solution.py:390
  9.5 0.0 copy-start
  9.5 6.9 %all-to-all-start = ((bf16[8,288,128]{2,1,0:T(8,128)(2,1)}), bf16[8,288,128]{2,1,0:T(8,128)(2,1)S(1)}, u32[]{:S(2)}, u32[]{:S(2)}) async-start(bf16[8,288,128]{2,1,0:T(8,128)(2,1)} %pack.1), calls=%async_computation | async-start | bytes 1179648 | tf_op jit(solution)/shard_map/all_to_all | solution.py:403
  16.4 0.0 copy-done.1
  16.4 0.0 copy-done.5
  16.4 0.0 copy-done
  16.4 0.0 copy-start.3
  16.5 1.3 copy-done.3
  17.7 0.0 copy-start.4
  17.7 1.3 copy-done.4
  19.0 1.1 project.1
  20.1 4.2 %all-to-all-done.got_ref = bf16[8,288,128]{2,1,0:T(8,128)(2,1)S(1)} async-done(((bf16[8,288,128]{2,1,0:T(8,128)(2,1)}), bf16[8,288,128]{2,1,0:T(8,128)(2,1)S(1)}, u32[]{:S(2)}, u32[]{:S(2)}) %all-to-all-start) | async-done | bytes 589856 | tf_op jit(solution)/shard_map/all_to_all | solution.py:403
  24.4 1.9 %gram.1 = bf16[8,432,128]{2,1,0:T(8,128)(2,1)S(1)} custom-call(bf16[8,288,128]{2,1,0:T(8,128)(2,1)S(1)} %all-to-all-done.got_ref, bf16[4608,128]{1,0:T(8,128)(2,1)S(1)} %bitcast.9, bf16[128,4608]{1,0:T(8,128)(2,1)S(1)} %bitcast.12, f32[1,4608]{1,0:T(1,128)S(1)} %copy-done.5, bf16[384,128]{1,0:T(8,128)(2,1)S(1)} %get-tuple-element.19.proj_ref, ...), custom_call_target="tpu_custom_call" | custom-call | flops 75497472 | bytes 3145728 | tf_op jit(solution)/shard_map/gram/pallas_call | solution.py:412
  26.3 0.0 copy-start.2
  26.3 0.9 copy-done.2
  27.2 9.5 %all-to-all-start.1 = ((bf16[8,432,128]{2,1,0:T(8,128)(2,1)}), bf16[8,432,128]{2,1,0:T(8,128)(2,1)S(1)}, u32[]{:S(2)}, u32[]{:S(2)}) async-start(bf16[8,432,128]{2,1,0:T(8,128)(2,1)} %copy-done.2), calls=%async_computation.1 | async-start | bytes 1769472 | tf_op jit(solution)/shard_map/all_to_all | solution.py:418
  36.7 0.1 slice_bitcast_fusion
  36.8 3.1 %collective-permute-start.1 = (bf16[8,144,128]{2,1,0:T(8,128)(2,1)S(1)}, bf16[8,144,128]{2,1,0:T(8,128)(2,1)S(1)}, u32[]{:S(2)}, u32[]{:S(2)}) collective-permute-start(bf16[8,144,128]{2,1,0:T(8,128)(2,1)S(1)} %get-tuple-element.37), channel_id=1, source_target_pairs={{0,4},{2,6},{4,0},{6,2},{1,5},{3,7},{5,1},{7,3},{8,12},{10,14},{12... | collective-permute-start | bytes 884744 | tf_op jit(solution)/shard_map/ppermute | solution.py:380
  39.9 0.6 collective-permute-start
  40.5 2.6 %collective-permute-start.2 = (bf16[8,144,128]{2,1,0:T(8,128)(2,1)S(1)}, bf16[8,144,128]{2,1,0:T(8,128)(2,1)S(1)}, u32[]{:S(2)}, u32[]{:S(2)}) collective-permute-start(bf16[8,144,128]{2,1,0:T(8,128)(2,1)S(1)} %get-tuple-element.37), channel_id=1, source_target_pairs={{0,6},{2,0},{4,2},{6,4},{1,7},{3,1},{5,3},{7,5},{8,14},{10,8},{12,... | collective-permute-start | bytes 884744 | tf_op jit(solution)/shard_map/ppermute | solution.py:380
  43.2 2.0 %collective-permute-done.1 = bf16[8,144,128]{2,1,0:T(8,128)(2,1)S(1)} collective-permute-done((bf16[8,144,128]{2,1,0:T(8,128)(2,1)S(1)}, bf16[8,144,128]{2,1,0:T(8,128)(2,1)S(1)}, u32[]{:S(2)}, u32[]{:S(2)}) %collective-permute-start.1) | collective-permute-done | bytes 294944 | tf_op jit(solution)/shard_map/ppermute | solution.py:380
  45.2 3.1 %collective-permute-done = bf16[8,144,128]{2,1,0:T(8,128)(2,1)S(1)} collective-permute-done((bf16[8,144,128]{2,1,0:T(8,128)(2,1)S(1)}, bf16[8,144,128]{2,1,0:T(8,128)(2,1)S(1)}, u32[]{:S(2)}, u32[]{:S(2)}) %collective-permute-start) | collective-permute-done | bytes 294944 | tf_op jit(solution)/shard_map/ppermute | solution.py:380
  48.3 0.1 collective-permute-done.2
  48.4 0.1 pad_maximum_fusion.refs_2_
  48.5 1.9 %all-to-all-done.1.part_ref.refs_0_ = bf16[8,432,128]{2,1,0:T(8,128)(2,1)S(1)} async-done(((bf16[8,432,128]{2,1,0:T(8,128)(2,1)}), bf16[8,432,128]{2,1,0:T(8,128)(2,1)S(1)}, u32[]{:S(2)}, u32[]{:S(2)}) %all-to-all-start.1) | async-done | bytes 884768 | tf_op jit(solution)/shard_map/all_to_all | solution.py:418
  50.4 0.3 spread.1
  50.7 19.8 %all_to_all.30.own_ref = bf16[16,8,32,128]{3,2,1,0:T(8,128)(2,1)S(1)} all-to-all(bf16[16,8,32,128]{3,2,1,0:T(8,128)(2,1)S(1)} %spread.1), channel_id=1, replica_groups=mesh['section'=8,'y'=4,'x'=4,'core'=2] {'y','x'}, dimensions={0} | all-to-all | bytes 2097152 | tf_op jit(solution)/shard_map/all_to_all | solution.py:426
  70.6 0.0 collective-permute-start.4
  70.6 0.5 collective-permute-start.3
  71.1 3.8 %collective-permute-done.3.oth_ref = bf16[16,8,32,128]{3,2,1,0:T(8,128)(2,1)S(1)} collective-permute-done((bf16[16,8,32,128]{3,2,1,0:T(8,128)(2,1)S(1)}, bf16[16,8,32,128]{3,2,1,0:T(8,128)(2,1)S(1)}, u32[]{:S(2)}, u32[]{:S(2)}) %collective-permute-start.3) | collective-permute-done | bytes 1048608 | tf_op jit(solution)/shard_map/ppermute | solution.py:428
  74.9 0.0 collective-permute-done.4.refs_3_
  74.9 8.1 %main.1 = (bf16[16,288,128]{2,1,0:T(8,128)(2,1)S(1)}, bf16[16,288,128]{2,1,0:T(8,128)(2,1)S(1)}, f32[16,8,128]{2,1,0:T(8,128)S(1)}) custom-call(bf16[16,8,32,128]{3,2,1,0:T(8,128)(2,1)S(1)} %all_to_all.30.own_ref, bf16[16,8,32,128]{3,2,1,0:T(8,128)(2,1)S(1)} %collective-permute-done.3.oth_ref, bf16[8,432,128]{2,1,0:T(8,128)(2,1)S(1)} %all-to-all-done.1.part_ref.refs_0_, ...), custom_call_target="tpu_custom_call" | custom-call | flops 1409286144 | bytes 10485760 | tf_op jit(solution)/shard_map/main/pallas_call | solution.py:431
  83.1 0.2 collective-permute-start.5
  83.3 11.8 %all_to_all.31.norm_ref = f32[16,8,128]{2,1,0:T(8,128)S(1)} all-to-all(f32[16,8,128]{2,1,0:T(8,128)S(1)} %get-tuple-element.30), channel_id=1, replica_groups=mesh['section'=8,'y'=4,'x'=4,'core'=2] {'section','core'}, dimensions={0} | all-to-all | bytes 131072 | tf_op jit(solution)/shard_map/all_to_all | solution.py:454
  95.0 0.0 collective-permute-done.5.got_ref
  95.1 0.4 mix.1
  95.5 21.3 %all_to_all.32.got_ref = bf16[16,288,128]{2,1,0:T(8,128)(2,1)S(1)} all-to-all(bf16[16,288,128]{2,1,0:T(8,128)(2,1)S(1)} %mix.1), channel_id=1, replica_groups=mesh['section'=8,'y'=4,'x'=4,'core'=2] {'y','x'}, dimensions={0} | all-to-all | bytes 2359296 | tf_op jit(solution)/shard_map/all_to_all | solution.py:456
  116.8 0.7 sum_out.1
  117.5 7.8 %all-to-all-start.5 = ((bf16[8,4,576]{2,1,0:T(4,128)(2,1)}), bf16[8,4,576]{2,1,0:T(4,128)(2,1)S(1)}, u32[]{:S(2)}, u32[]{:S(2)}) async-start(bf16[8,4,576]{2,1,0:T(4,128)(2,1)} %sum_out.1), calls=%async_computation.5 | async-start | bytes 81920 | tf_op jit(solution)/shard_map/all_to_all | solution.py:458
  125.4 0.1 sum_in.1
  125.5 3.4 %collective-permute-start.6 = (bf16[144,128]{1,0:T(8,128)(2,1)S(1)}, bf16[144,128]{1,0:T(8,128)(2,1)S(1)}, u32[]{:S(2)}, u32[]{:S(2)}) collective-permute-start(bf16[144,128]{1,0:T(8,128)(2,1)S(1)} %sum_in.1), channel_id=1, source_target_pairs={{0,0},{1,1},{2,2},{3,3},{4,32},{5,33},{6,34},{7,35},{8,64},{9,65},... | collective-permute-start | bytes 110600 | tf_op jit(solution)/shard_map/ppermute | solution.py:462
  128.8 10.3 %collective-permute-done.6.gi_ref = bf16[144,128]{1,0:T(8,128)(2,1)S(1)} collective-permute-done((bf16[144,128]{1,0:T(8,128)(2,1)S(1)}, bf16[144,128]{1,0:T(8,128)(2,1)S(1)}, u32[]{:S(2)}, u32[]{:S(2)}) %collective-permute-start.6) | collective-permute-done | bytes 36896 | tf_op jit(solution)/shard_map/ppermute | solution.py:462
  139.1 0.0 all-to-all-done.5.got_ref
  139.1 0.7 join.1
Async XLA Ops:
  0.6 15.8 %copy-start.1 = (bf16[1,128,4608]{2,1,0:T(8,128)(2,1)S(1)}, bf16[1,128,4608]{2,1,0:T(8,128)(2,1)}, u32[]{:S(2)}) copy-start(bf16[1,128,4608]{2,1,0:T(8,128)(2,1)} %param.7) | copy-start | bytes 3538948
  0.6 15.8 %copy-start.5 = (f32[1,4608]{1,0:T(1,128)S(1)}, f32[1,4608]{1,0:T(1,128)}, u32[]{:S(2)}) copy-start(f32[1,4608]{1,0:T(1,128)} %ls_ref.5) | copy-start | bytes 55300
  9.5 6.9 %copy-start = (bf16[1,4608,128]{2,1,0:T(8,128)(2,1)S(1)}, bf16[1,4608,128]{2,1,0:T(8,128)(2,1)}, u32[]{:S(2)}) copy-start(bf16[1,4608,128]{2,1,0:T(8,128)(2,1)} %param.6) | copy-start | bytes 3538948
  9.5 14.8 %all-to-all-start = ((bf16[8,288,128]{2,1,0:T(8,128)(2,1)}), bf16[8,288,128]{2,1,0:T(8,128)(2,1)S(1)}, u32[]{:S(2)}, u32[]{:S(2)}) async-start(bf16[8,288,128]{2,1,0:T(8,128)(2,1)} %pack.1), calls=%async_computation | async-start | bytes 1179648 | tf_op jit(solution)/shard_map/all_to_all | solution.py:403
  16.4 1.3 copy-start.3
  17.7 1.3 copy-start.4
  26.3 0.9 copy-start.2
  27.2 23.2 %all-to-all-start.1 = ((bf16[8,432,128]{2,1,0:T(8,128)(2,1)}), bf16[8,432,128]{2,1,0:T(8,128)(2,1)S(1)}, u32[]{:S(2)}, u32[]{:S(2)}) async-start(bf16[8,432,128]{2,1,0:T(8,128)(2,1)} %copy-done.2), calls=%async_computation.1 | async-start | bytes 1769472 | tf_op jit(solution)/shard_map/all_to_all | solution.py:418
  36.8 8.4 %collective-permute-start.1 = (bf16[8,144,128]{2,1,0:T(8,128)(2,1)S(1)}, bf16[8,144,128]{2,1,0:T(8,128)(2,1)S(1)}, u32[]{:S(2)}, u32[]{:S(2)}) collective-permute-start(bf16[8,144,128]{2,1,0:T(8,128)(2,1)S(1)} %get-tuple-element.37), channel_id=1, source_target_pairs={{0,4},{2,6},{4,0},{6,2},{1,5},{3,7},{5,1},{7,3},{8,12},{10,14},{12... | collective-permute-start | bytes 884744 | tf_op jit(solution)/shard_map/ppermute | solution.py:380
  39.9 8.4 %collective-permute-start = (bf16[8,144,128]{2,1,0:T(8,128)(2,1)S(1)}, bf16[8,144,128]{2,1,0:T(8,128)(2,1)S(1)}, u32[]{:S(2)}, u32[]{:S(2)}) collective-permute-start(bf16[8,144,128]{2,1,0:T(8,128)(2,1)S(1)} %get-tuple-element.37), channel_id=1, source_target_pairs={{0,2},{2,4},{4,6},{6,0},{1,3},{3,5},{5,7},{7,1},{8,10},{10,12},{12... | collective-permute-start | bytes 884744 | tf_op jit(solution)/shard_map/ppermute | solution.py:380
  40.5 7.9 %collective-permute-start.2 = (bf16[8,144,128]{2,1,0:T(8,128)(2,1)S(1)}, bf16[8,144,128]{2,1,0:T(8,128)(2,1)S(1)}, u32[]{:S(2)}, u32[]{:S(2)}) collective-permute-start(bf16[8,144,128]{2,1,0:T(8,128)(2,1)S(1)} %get-tuple-element.37), channel_id=1, source_target_pairs={{0,6},{2,0},{4,2},{6,4},{1,7},{3,1},{5,3},{7,5},{8,14},{10,8},{12,... | collective-permute-start | bytes 884744 | tf_op jit(solution)/shard_map/ppermute | solution.py:380
  70.6 4.4 %collective-permute-start.4 = (bf16[4,8,144,128]{3,2,1,0:T(8,128)(2,1)S(1)}, bf16[4,8,144,128]{3,2,1,0:T(8,128)(2,1)S(1)}, u32[]{:S(2)}, u32[]{:S(2)}) collective-permute-start(bf16[4,8,144,128]{3,2,1,0:T(8,128)(2,1)S(1)} %pad_maximum_fusion.refs_2_), channel_id=1, source_target_pairs={{0,1},{1,0},{2,3},{3,2},{4,5},{5,4},{6,7},{7,6},{8,9},{9,8},{10,11... | collective-permute-start | bytes 3538952 | tf_op jit(solution)/shard_map/ppermute | solution.py:429
  70.6 4.3 %collective-permute-start.3 = (bf16[16,8,32,128]{3,2,1,0:T(8,128)(2,1)S(1)}, bf16[16,8,32,128]{3,2,1,0:T(8,128)(2,1)S(1)}, u32[]{:S(2)}, u32[]{:S(2)}) collective-permute-start(bf16[16,8,32,128]{3,2,1,0:T(8,128)(2,1)S(1)} %all_to_all.30.own_ref), channel_id=1, source_target_pairs={{0,1},{1,0},{2,3},{3,2},{4,5},{5,4},{6,7},{7,6},{8,9},{9,8},{10,11... | collective-permute-start | bytes 3145736 | tf_op jit(solution)/shard_map/ppermute | solution.py:428
  83.1 12.0 %collective-permute-start.5 = (bf16[16,288,128]{2,1,0:T(8,128)(2,1)S(1)}, bf16[16,288,128]{2,1,0:T(8,128)(2,1)S(1)}, u32[]{:S(2)}, u32[]{:S(2)}) collective-permute-start(bf16[16,288,128]{2,1,0:T(8,128)(2,1)S(1)} %get-tuple-element.32), channel_id=1, source_target_pairs={{0,1},{1,0},{2,3},{3,2},{4,5},{5,4},{6,7},{7,6},{8,9},{9,8},{10,11... | collective-permute-start | bytes 3538952 | tf_op jit(solution)/shard_map/ppermute | solution.py:453
  117.5 21.6 %all-to-all-start.5 = ((bf16[8,4,576]{2,1,0:T(4,128)(2,1)}), bf16[8,4,576]{2,1,0:T(4,128)(2,1)S(1)}, u32[]{:S(2)}, u32[]{:S(2)}) async-start(bf16[8,4,576]{2,1,0:T(4,128)(2,1)} %sum_out.1), calls=%async_computation.5 | async-start | bytes 81920 | tf_op jit(solution)/shard_map/all_to_all | solution.py:458
  125.5 13.7 %collective-permute-start.6 = (bf16[144,128]{1,0:T(8,128)(2,1)S(1)}, bf16[144,128]{1,0:T(8,128)(2,1)S(1)}, u32[]{:S(2)}, u32[]{:S(2)}) collective-permute-start(bf16[144,128]{1,0:T(8,128)(2,1)S(1)} %sum_in.1), channel_id=1, source_target_pairs={{0,0},{1,1},{2,2},{3,3},{4,32},{5,33},{6,34},{7,35},{8,64},{9,65},... | collective-permute-start | bytes 110600 | tf_op jit(solution)/shard_map/ppermute | solution.py:462

commit v5 on v4

--- a/solution.py
+++ b/solution.py
@@ -16,8 +16,8 @@
 SLICE = D // S
 QUARTER = SLICE // 4
 PACK_VMEM = 56
-DIRECT = 6
-TAIL_FLOPS = 20 * 10**9
+LATE = 6
+BAND = D // 4
 Z, Y, X, C = "section", "y", "x", "core"
 BF = jnp.bfloat16
 F32 = jnp.float32
@@ -57,45 +57,51 @@
     )
 
 
-def pack_kernel(w_in_ref, w_out_ref, ls_ref, pay_ref, rows, wide, turned, strip, sem):
+def swap_units(count, picked=None):
+    row = lax.broadcasted_iota(jnp.int32, (count, R), 0)
+    col = lax.broadcasted_iota(jnp.int32, (count, R), 1)
+    outer = row // 16 if picked is None else picked
+    return (col == ((row % 16) // 2) * 16 + outer * 2 + row % 2).astype(BF)
+
+
+def pack_kernel(w_in_ref, w_out_ref, ls_ref, pay_ref, rows, wide, block, strip, sem):
     y, x, core = lax.axis_index(Y), lax.axis_index(X), lax.axis_index(C)
     q = (x * 2 + core) * 4 + y
     row_copy = pltpu.make_async_copy(w_out_ref.at[pl.ds(pl.multiple_of((q // 4) * 16, 16), 16)], rows, sem.at[0])
     row_copy.start()
-    first = [SLICE * k + QUARTER * x for k in range(S)]
-
-    def in_copies():
+    start = pl.multiple_of(x * BAND, R)
+
+    def in_copy():
+        return pltpu.make_async_copy(w_in_ref.at[pl.ds(start, BAND)], block, sem.at[1])
+
+    def out_copy():
+        return pltpu.make_async_copy(w_out_ref.at[:, pl.ds(start, BAND)], wide, sem.at[1])
+
+    def late_copies():
         return [
             pltpu.make_async_copy(
-                w_in_ref.at[pl.ds(pl.multiple_of(first[k], 16), QUARTER)],
-                pay_ref.at[k, pl.ds(ROWS, QUARTER)] if k < DIRECT else turned.at[k, pl.ds(0, QUARTER)],
-                sem.at[1 + k],
+                w_in_ref.at[pl.ds(pl.multiple_of(start + QUARTER * e + 16 * k, 16), 16)],
+                pay_ref.at[k, pl.ds(ROWS + 16 * e, 16)],
+                sem.at[2 + S + k * S + e],
             )
-            for k in range(S)
-        ]
-
-    def out_copies():
-        return [
-            pltpu.make_async_copy(
-                w_out_ref.at[:, pl.ds(pl.multiple_of((first[k] // R) * R, R), 2 * R)], wide.at[k], sem.at[1 + k]
-            )
-            for k in range(S)
+            for k in range(LATE)
+            for e in range(S)
         ]
 
     @pl.when(core == 0)
     def _():
-        for cp in in_copies():
+        for cp in late_copies():
             cp.start()
+        in_copy().start()
 
     @pl.when(core != 0)
     def _():
-        for cp in out_copies():
-            cp.start()
+        out_copy().start()
 
     row_copy.wait()
-    block = rows[...].astype(F32) * ls_ref[...]
+    part = rows[...].astype(F32) * ls_ref[...]
     group = q % 4
-    mine = jnp.where(group < 2, block[:8], block[8:])
+    mine = jnp.where(group < 2, part[:8], part[8:])
     turn = pltpu.roll(mine, 4, axis=0)
     odd = group % 2 == 1
     low = lax.broadcasted_iota(jnp.int32, (8, HALF), 0) < 4
@@ -105,42 +111,52 @@
         jnp.where(odd, mine[:, HALF:], turn[:, HALF:]),
     )
     for u in range(9):
-        two = jnp.concatenate([mine[:, 256 * u : 256 * u + R], mine[:, 256 * u + R : 256 * (u + 1)]], axis=0)
-        strip[16 * u : 16 * u + 16] = two.astype(BF)
-    sends = [pltpu.make_async_copy(strip, pay_ref.at[k, pl.ds(0, ROWS)], sem.at[9 + k]) for k in range(S)]
-    for cp in sends:
-        cp.start()
+        two = jnp.concatenate([mine[:, 256 * u : 256 * u + R], mine[:, 256 * u + R : 256 * (u + 1)]], axis=0).astype(BF)
+        for k in range(S):
+            strip[k, 16 * u : 16 * u + 16] = two
 
     @pl.when(core == 0)
     def _():
-        copies = in_copies()
-        outs = []
-        for k in range(DIRECT, S):
-            copies[k].wait()
-            out = pltpu.make_async_copy(turned.at[k, pl.ds(0, QUARTER)], pay_ref.at[k, pl.ds(ROWS, QUARTER)], sem.at[17 + k])
-            out.start()
-            outs.append(out)
-        for cp in copies[:DIRECT] + outs:
-            cp.wait()
+        in_copy().wait()
 
     @pl.when(core != 0)
     def _():
-        copies = []
-        for k, cp in enumerate(out_copies()):
+        out_copy().wait()
+        scale = ls_ref[:, pl.ds(start, BAND)]
+        for t in range(BAND // R):
+            tile = wide[:, t * R : (t + 1) * R].astype(F32) * scale[:, t * R : (t + 1) * R]
+            block[t * R : (t + 1) * R, :] = tile.T.astype(BF)
+
+    for k in range(S):
+        for e in range(S):
+            strip[k, ROWS + 16 * e : ROWS + 16 * e + 16] = block[QUARTER * e + 16 * k : QUARTER * e + 16 * k + 16]
+    left = jnp.concatenate([block[QUARTER * e + 128 : QUARTER * (e + 1)] for e in range(S)], axis=0)
+    left = mm(swap_units(R), left).astype(BF)
+    for k in range(S):
+        strip[k, ROWS + 128 :] = left[16 * k : 16 * k + 16]
+
+    def sends(late):
+        if not late:
+            return [pltpu.make_async_copy(strip.at[k], pay_ref.at[k], sem.at[2 + k]) for k in range(S)]
+        return [
+            pltpu.make_async_copy(strip.at[k, pl.ds(a, n)], pay_ref.at[k, pl.ds(a, n)], sem.at[2 + S + S * LATE + 2 * k + i])
+            for k in range(LATE)
+            for i, (a, n) in enumerate(((0, ROWS), (ROWS + 128, 16)))
+        ] + [pltpu.make_async_copy(strip.at[k], pay_ref.at[k], sem.at[2 + k]) for k in range(LATE, S)]
+
+    @pl.when(core == 0)
+    def _():
+        for cp in sends(True):
+            cp.start()
+        for cp in late_copies() + sends(True):
             cp.wait()
-            base = pl.multiple_of((first[k] // R) * R, R)
-            for i in range(2):
-                part = wide[k, :, i * R : (i + 1) * R].astype(F32) * ls_ref[:, pl.ds(base + i * R, R)]
-                turned[k, i * R : (i + 1) * R, :] = part.T.astype(BF)
-            start = pl.multiple_of(first[k] % R, 16)
-            out = pltpu.make_async_copy(turned.at[k, pl.ds(start, QUARTER)], pay_ref.at[k, pl.ds(ROWS, QUARTER)], sem.at[17 + k])
-            out.start()
-            copies.append(out)
-        for out in copies:
-            out.wait()
-
-    for cp in sends:
-        cp.wait()
+
+    @pl.when(core != 0)
+    def _():
+        for cp in sends(False):
+            cp.start()
+        for cp in sends(False):
+            cp.wait()
 
 
 def project_kernel(x_ref, c_ref, w_in_ref, w_out_ref, ls_ref, proj, scales, sq_ref, xt_ref, ct_ref, wide):
@@ -153,30 +169,33 @@
     proj[2 * T :] = mm(c_ref[...], w2, NT).astype(BF)
     top = ls.astype(BF).astype(F32)
     low_part = ls - top
+    bands = [part[:, BAND * j : BAND * (j + 1)] for part in (top, low_part) for j in range(4)]
+    bands = jnp.concatenate(bands, axis=0)
     for k in range(S):
-        lines = []
-        for part in (top, low_part):
-            lines += [part[:, SLICE * k + R * j : SLICE * k + R * (j + 1)] for j in range(4)]
-            tail = part[:, SLICE * k + 512 : SLICE * (k + 1)]
-            lines.append(jnp.concatenate([tail, tail], axis=1))
-        lines.append(jnp.zeros((6, R), F32))
-        scales[k] = jnp.concatenate(lines, axis=0).astype(BF)
+        main = [bands[:, QUARTER * e + 16 * k : QUARTER * e + 16 * k + 16] for e in range(S)]
+        rest = [bands[:, QUARTER * e + 128 + 2 * k : QUARTER * e + 130 + 2 * k] for e in range(S)]
+        rest = jnp.concatenate(rest + [jnp.zeros((S, R - 16), F32)], axis=1)
+        scales[k] = jnp.concatenate([jnp.concatenate(main, axis=1), rest], axis=0).astype(BF)
     xf = xv.astype(F32)
     sq_ref[...] = jnp.sum(xf * xf, axis=1, keepdims=True)
-    base = pl.multiple_of(((z * 9) // 2) * R, R)
-    off = pl.multiple_of((z % 2) * 64, 16)
+    mine = swap_units(16, z)
     for src, dst in ((x_ref, xt_ref), (c_ref, ct_ref)):
-        for t in range(5):
-            wide[t * R : (t + 1) * R, :] = src[:, pl.ds(base + t * R, R)].astype(F32).T.astype(BF)
-        dst[...] = wide[pl.ds(off, SLICE), :]
-
-
-def gram_kernel(got_ref, w_in_ref, w_out_ref, ls_ref, proj_ref, scales_ref, out_ref, row, sem):
+        for t in range(D // R):
+            wide[t * R : (t + 1) * R, :] = src[:, t * R : (t + 1) * R].astype(F32).T.astype(BF)
+        for j in range(4):
+            left = []
+            for e in range(S):
+                at = BAND * j + QUARTER * e
+                dst[R * j + 16 * e : R * j + 16 * e + 16] = wide[pl.ds(pl.multiple_of(at + 16 * z, 16), 16), :]
+                left.append(wide[at + 128 : at + QUARTER])
+            dst[512 + 16 * j : 512 + 16 * j + 16] = mm(mine, jnp.concatenate(left, axis=0)).astype(BF)
+
+
+def gram_kernel(got_ref, w_in_ref, w_out_ref, ls_ref, proj_ref, scales_ref, out_ref):
     z = lax.axis_index(Z)
-    copies = [pltpu.make_async_copy(proj_ref, out_ref.at[k, pl.ds(32, 3 * T)], sem.at[k]) for k in range(S)]
-    copies.append(pltpu.make_async_copy(scales_ref, out_ref.at[:, pl.ds(32 + 3 * T, 16)], sem.at[S]))
-    for cp in copies:
-        cp.start()
+    for k in range(S):
+        out_ref[k, 32 : 32 + 3 * T] = proj_ref[...]
+        out_ref[k, 32 + 3 * T :] = scales_ref[k]
     ls = ls_ref[...]
     first, second = [], []
     for u in range(9):
@@ -193,12 +212,8 @@
     down = down + mm((second.astype(F32) * ls[:, HALF:]).astype(BF), w_out_ref[:, HALF:], NT)
     below = (lax.broadcasted_iota(jnp.int32, (32, R), 0) // 4) < z
     out = jnp.where(below, up, down).astype(BF)
-    row[...] = out
-    sends = [pltpu.make_async_copy(row, out_ref.at[k, pl.ds(0, 32)], sem.at[S + 1 + k]) for k in range(S)]
-    for cp in sends:
-        cp.start()
-    for cp in copies + sends:
-        cp.wait()
+    for k in range(S):
+        out_ref[k, :32] = out
 
 
 def spread_kernel(part_ref, out_ref, sem):
@@ -211,7 +226,7 @@
 
 def main_kernel(own_ref, oth_ref, *refs):
     proj_ref, sq_ref, wown_ref, woth_ref, xt_ref, ct_ref, gown_ref, goth_ref, norm_ref = refs[:9]
-    kmat, pre, qacc, hacc, slope, hs, hts, ps, sts, wbuf, xs, gos, sem = refs[9:]
+    kmat, pre, qacc, hacc, slope, hs, hts, ps, sts, wbuf, xs, gos, lefts, sem = refs[9:]
     core = lax.axis_index(C)
     is0 = core == 0
     copies = []
@@ -287,28 +302,37 @@
         cp.wait()
 
     def weights(kind, s):
-        return wbuf[kind, :, s].reshape(SLICE, R)
-
-    total = jnp.zeros((QUARTER, R), F32)
+        return jnp.concatenate([wbuf[kind, j, s, :128] for j in range(4)] + [wbuf[kind, j, s, 128:] for j in range(4)], axis=0)
+
+    total = jnp.zeros((64, R), F32)
     x = xt_ref[...]
     for s in range(S):
         xs[s] = x
         xf = x.astype(F32)
         n = (xf * sts[s : s + 1, :]).astype(BF)
         gi = mm(n, ps[s])
-        for j1 in range(2):
-            a = gi[2 * j1 * QUARTER : (2 * j1 + 1) * QUARTER]
-            b = gi[(2 * j1 + 1) * QUARTER : (2 * j1 + 2) * QUARTER]
-            total = total + a * a + b * b
-            gown_ref[s * 2 + j1, :ROWS] = jnp.where(is0, a, b).astype(BF)
-            goth_ref[s * 2 + j1, :ROWS] = jnp.where(is0, b, a).astype(BF)
+        for j in range(9):
+            total = total + gi[64 * j : 64 * j + 64] * gi[64 * j : 64 * j + 64]
+        for i in range(16):
+            a, b = gi[32 * i : 32 * i + 16], gi[32 * i + 16 : 32 * i + 32]
+            gown_ref[i, 16 * s : 16 * s + 16] = jnp.where(is0, a, b).astype(BF)
+            goth_ref[i, 16 * s : 16 * s + 16] = jnp.where(is0, b, a).astype(BF)
+        for j in range(4):
+            lefts[j, 16 * s : 16 * s + 16] = gi[512 + 16 * j : 512 + 16 * j + 16].astype(BF)
         if s + 1 < S:
             x = (xf + mm(weights(1, s), hs[s], NT)).astype(BF)
+    units = swap_units(R)
+    for j in range(4):
+        left = mm(units, lefts[j])
+        for i in range(4):
+            a, b = left[32 * i : 32 * i + 16], left[32 * i + 16 : 32 * i + 32]
+            gown_ref[4 * j + i, 128:ROWS] = jnp.where(is0, a, b).astype(BF)
+            goth_ref[4 * j + i, 128:ROWS] = jnp.where(is0, b, a).astype(BF)
     g = ct_ref[...]
     for s in reversed(range(S)):
         lsf = proj_ref[s, 32 + 3 * T :].astype(F32)
-        lsf = lsf[:5] + lsf[5:10]
-        lrow = jnp.concatenate([lsf[j : j + 1] for j in range(4)] + [lsf[4:5, :64]], axis=1)
+        lsf = jnp.concatenate([lsf[:4] + lsf[4:8], lsf[8:12] + lsf[12:]], axis=0)
+        lrow = jnp.concatenate([lsf[j : j + 1] for j in range(4)] + [lsf[4 + j : 5 + j, :16] for j in range(4)], axis=1)
         gos[s] = mm(hts[s], g, NT) * lrow
         if s > 0:
             m = mm(weights(0, s), ps[s], NT)
@@ -350,30 +374,47 @@
         out_ref[i] = (own_ref[i].astype(F32) * mine + got_ref[i].astype(F32) * other).astype(BF)
 
 
-def fold(ref, rows):
-    total = ref[0, rows].astype(F32)
+def sum_kernel(got_ref, out_ref):
+    total = got_ref[0].astype(F32)
     for i in range(1, 16):
-        total = total + ref[i, rows].astype(F32)
-    return total
-
-
-def sum_out_kernel(got_ref, go_ref):
-    go = fold(got_ref, slice(ROWS, 2 * ROWS))
-    last = go[4 * 32 :]
+        total = total + got_ref[i].astype(F32)
+    tiles = [total[ROWS + 32 * t : ROWS + 32 * t + 32].reshape(4, 8, R) for t in range(4)]
+    last = total[ROWS + 128 :]
     tail = jnp.concatenate([last[:, :64], last[:, 64:]], axis=0)
-    go = jnp.concatenate([go[32 * t : 32 * t + 32] for t in range(4)] + [tail], axis=1).reshape(4, 8, SLICE)
-    for i in range(4):
-        go_ref[2 * i] = go[i][:4].astype(BF)
-        go_ref[2 * i + 1] = go[i][4:].astype(BF)
-
-
-def sum_in_kernel(got_ref, gi_ref):
-    gi_ref[...] = fold(got_ref, slice(0, ROWS)).astype(BF)
-
-
-def join_kernel(got_ref, gi_ref, out_ref, in_ref):
-    in_ref[0] = gi_ref[...].astype(F32)
-    out_ref[0] = jnp.concatenate([got_ref[k].astype(F32) for k in range(S)], axis=1)
+    tail = jnp.concatenate([tail, jnp.zeros((32, 64), F32)], axis=1).reshape(4, 8, R)
+    first = halves(tiles[0], tiles[1])
+    second = halves(tiles[2], tiles[3])
+    third = (tail, pltpu.roll(tail, 4, axis=1))
+    for s in range(S):
+        left = total[128 + 8 * (s // 4) : 136 + 8 * (s // 4)]
+        if s % 4:
+            left = pltpu.roll(left, 8 - 2 * (s % 4), axis=0)
+        parts = [total[16 * s : 16 * s + 16]] + [v[s % 2][s // 2] for v in (first, second, third)] + [left]
+        out_ref[s] = jnp.concatenate(parts, axis=0).astype(BF)
+
+
+def join_kernel(got_ref, out_ref, in_ref):
+    row = lax.broadcasted_iota(jnp.int32, (8, R), 0)
+    mains, rests, left = [], [], [None, None]
+    for k in range(S):
+        got = got_ref[k].astype(F32)
+        in_ref[0, 16 * k : 16 * k + 16] = got[:16]
+        unit = got[40:]
+        if k % 4:
+            unit = pltpu.roll(unit, 2 * (k % 4), axis=0)
+        left[k // 4] = unit if k % 4 == 0 else jnp.where(row // 2 == k % 4, unit, left[k // 4])
+        mains.append(got[16:32])
+        tail = jnp.concatenate([got[32:36, 16 * j : 16 * j + 16] for j in range(4)], axis=0)
+        rests.append(tail)
+    in_ref[0, 128:136] = left[0]
+    in_ref[0, 136:] = left[1]
+    pieces = []
+    for e in range(S):
+        pieces += [v[:, 16 * e : 16 * e + 16] for v in mains]
+        pieces += [v[:, 2 * e : 2 * e + 2] for v in rests]
+    whole = jnp.concatenate(pieces, axis=1)
+    for j in range(4):
+        out_ref[0, :, BAND * j : BAND * (j + 1)] = whole[4 * j : 4 * j + 4]
 
 
 def shifted(value, axis, size):
@@ -393,10 +434,10 @@
         [anywhere, anywhere, VM],
         [
             pltpu.VMEM((16, D), BF),
-            pltpu.VMEM((S, R, 2 * R), BF),
-            pltpu.VMEM((S, 2 * R, R), BF),
-            pltpu.VMEM((ROWS, R), BF),
-            pltpu.SemaphoreType.DMA((25,)),
+            pltpu.VMEM((R, BAND), BF),
+            pltpu.VMEM((BAND, R), BF),
+            pltpu.VMEM((S, 2 * ROWS, R), BF),
+            pltpu.SemaphoreType.DMA((2 + 3 * S + S * S,)),
         ],
         flops=flops // 16, size=2 << 20, vmem=PACK_VMEM, to=[far],
     )(w1, w_out[0], layer_scale)
@@ -406,13 +447,12 @@
         project_kernel, "project",
         [((3 * T, R), BF), ((S, 16, R), BF), ((T, 1), F32), ((SLICE, T), BF), ((SLICE, T), BF)],
         [VM, VM, VM, VM, VM],
-        [pltpu.VMEM((5 * R, T), BF)], flops=3 * flops, size=5 << 20, vmem=12,
+        [pltpu.VMEM((D, T), BF)], flops=3 * flops, size=5 << 20, vmem=16,
     )(inputs, cotangent, w1, w_out[0], layer_scale)
 
     (part,) = call(
         gram_kernel, "gram", [((S, 48 + 3 * T, R), BF)], [VM] * 6,
-        [pltpu.VMEM((32, R), BF), pltpu.SemaphoreType.DMA((2 * S + 1,))],
-        flops=flops // 2, size=3 << 20, vmem=12, to=[far],
+        flops=flops // 2, size=3 << 20, vmem=12,
     )(got, w1, w_out[0], layer_scale, proj, scales)
     part, got = lax.optimization_barrier((part, got))
     part = lax.all_to_all(part, Z, 0, 0)
@@ -445,6 +485,7 @@
             pltpu.VMEM((2, 4, S, QUARTER, R), BF),
             pltpu.VMEM((S, SLICE, T), BF),
             pltpu.VMEM((S, R, SLICE), F32),
+            pltpu.VMEM((4, R, R), BF),
             pltpu.SemaphoreType.DMA((8,)),
         ],
         flops=2 * 32 * SLICE * T * R + 2 * 192 * T * R * R, size=10 << 20, trans=S * T * R, vmem=28,
@@ -454,13 +495,9 @@
     norm = lax.all_to_all(norm, (Z, C), 0, 0)
     (both,) = call(mix_kernel, "mix", [((16, 2 * ROWS, R), BF)], [VM, VM, VM], size=4 << 20)(norm, gown, ggot)
     both = lax.all_to_all(both, (Y, X), 0, 0)
-    (go_sent,) = call(sum_out_kernel, "sum_out", [((S, 4, SLICE), BF)], [VM], size=1 << 20)(both)
-    go = lax.all_to_all(go_sent, Z, 0, 0)
-    both, go_sent = lax.optimization_barrier((both, go_sent))
-    (gi,) = call(sum_in_kernel, "sum_in", [((ROWS, R), BF)], [VM], flops=TAIL_FLOPS, size=1 << 20)(both)
-    route = [(k * 32 + s * 4 + j, s * 32 + k * 4 + j) for k in range(S) for s in range(S) for j in range(4)]
-    gi = lax.ppermute(gi, (Z, Y, X, C), route)
-    grad_out, grad_in = call(join_kernel, "join", [((1, 4, D), F32), ((1, ROWS, R), F32)], [VM, VM])(go, gi)
+    (sent,) = call(sum_kernel, "sum", [((S, 48, R), BF)], [VM], size=2 << 20)(both)
+    got = lax.all_to_all(sent, Z, 0, 0)
+    grad_out, grad_in = call(join_kernel, "join", [((1, 4, D), F32), ((1, ROWS, R), F32)], [VM])(got)
     return grad_in, grad_out
 
 

time: 140 us -> 134 us (0.957)
  the two profiles are of different devices: /device:TPU:160 before, /device:TPU:2 now
where the time goes in v5:
time: 134 us
  blocking collectives  62.4 us (47%)
  waiting for transfers between devices  28.3 us (21%)
  Pallas kernels  21.2 us (16%)
  starting transfers between devices  17.1 us (13%)
  local copies, waits for them, and re-layouts  3.54 us (3%)
    all_to_all x1, blocking collectives, per_device(): both = lax.all_to_all(both, (Y, X), 0, 0)  22 us
    all_to_all x1, blocking collectives, per_device(): kown = lax.all_to_all(spread, (Y, X), 0, 0)  18.9 us
    all_to_all x1, blocking collectives, per_device(): got = lax.all_to_all(sent, Z, 0, 0)  11.1 us
    all_to_all x1, blocking collectives, per_device(): norm = lax.all_to_all(norm, (Z, C), 0, 0)  10.4 us
    all_to_all x1, waiting for transfers between devices, per_device(): got = lax.all_to_all(pay, Z, 0, 0)  9.82 us
    pallas_call x1, Pallas kernels, per_device(): call(pack_kernel, 'pack', [((S, 2 * ROWS, R), BF)], [anywhere, anywhere,...  8.71 us
    all_to_all x1, starting transfers between devices, per_device(): got = lax.all_to_all(pay, Z, 0, 0)  8.61 us
    pallas_call x1, Pallas kernels, per_device(): call(main_kernel, 'main', [((16, 2 * ROWS, R), BF), ((16, 2 * ROWS, R), B...  8.31 us
  transfers between devices with their start and end apart: 8, of which 5 were waited for; matrix products, arithmetic and copies ran while one was open for 0% of the time, Pallas kernels for 1%

profile of v5, /device:TPU:2, one launch (start us, length us, event | category | flops | bytes accessed | tf_op | source)
XLA Modules:
  0.0 133.5 jit_solution(16054101631518960582)
XLA Ops:
  0.6 0.0 copy-start.1
  0.6 0.0 copy-start.5
  0.6 8.7 %pack.1 = bf16[8,288,128]{2,1,0:T(8,128)(2,1)} custom-call(bf16[4608,128]{1,0:T(8,128)(2,1)} %bitcast.7, bf16[128,4608]{1,0:T(8,128)(2,1)} %bitcast.10, f32[1,4608]{1,0:T(1,128)} %ls_ref.5), custom_call_target="tpu_custom_call" | custom-call | flops 9437184 | bytes 2097152 | tf_op jit(solution)/shard_map/pack/pallas_call | solution.py:431
  9.4 0.0 copy-start
  9.4 8.6 %all-to-all-start = ((bf16[8,288,128]{2,1,0:T(8,128)(2,1)}), bf16[8,288,128]{2,1,0:T(8,128)(2,1)S(1)}, u32[]{:S(2)}, u32[]{:S(2)}) async-start(bf16[8,288,128]{2,1,0:T(8,128)(2,1)} %pack.1), calls=%async_computation | async-start | bytes 1179648 | tf_op jit(solution)/shard_map/all_to_all | solution.py:444
  18.0 0.0 copy-done.1
  18.0 0.0 copy-done.5
  18.0 0.0 copy-done
  18.0 0.0 copy-start.3
  18.0 1.3 copy-done.3
  19.3 0.0 copy-start.4
  19.3 1.3 copy-done.4
  20.6 1.7 %project.1 = (bf16[384,128]{1,0:T(8,128)(2,1)S(1)}, bf16[8,16,128]{2,1,0:T(8,128)(2,1)S(1)}, f32[128,1]{1,0:T(8,128)S(1)}, bf16[576,128]{1,0:T(8,128)(2,1)S(1)}, bf16[576,128]{1,0:T(8,128)(2,1)S(1)}) custom-call(bf16[128,4608]{1,0:T(8,128)(2,1)S(1)} %copy-done.3, bf16[128,4608]{1,0:T(8,128)(2,1)S(1)} %copy-done.4, bf16[4608,128]{1,0:T(8,128)(2,1)S(1)} %bitcast.8, ...), custom_call_target="tpu_custom_call" | custom-call | flops 452984832 | bytes 5242880 | tf_op jit(solution)/shard_map/project/pallas_call | solution.py:446
  22.3 9.8 %all-to-all-done.got_ref = bf16[8,288,128]{2,1,0:T(8,128)(2,1)S(1)} async-done(((bf16[8,288,128]{2,1,0:T(8,128)(2,1)}), bf16[8,288,128]{2,1,0:T(8,128)(2,1)S(1)}, u32[]{:S(2)}, u32[]{:S(2)}) %all-to-all-start) | async-done | bytes 589856 | tf_op jit(solution)/shard_map/all_to_all | solution.py:444
  32.1 0.7 gram.1
  32.7 0.0 copy-start.2
  32.8 0.9 copy-done.2
  33.7 3.5 %all-to-all-start.1 = ((bf16[8,432,128]{2,1,0:T(8,128)(2,1)}), bf16[8,432,128]{2,1,0:T(8,128)(2,1)S(1)}, u32[]{:S(2)}, u32[]{:S(2)}) async-start(bf16[8,432,128]{2,1,0:T(8,128)(2,1)} %copy-done.2), calls=%async_computation.1 | async-start | bytes 1769472 | tf_op jit(solution)/shard_map/all_to_all | solution.py:458
  37.2 0.1 slice_bitcast_fusion
  37.3 2.2 %collective-permute-start.1 = (bf16[8,144,128]{2,1,0:T(8,128)(2,1)S(1)}, bf16[8,144,128]{2,1,0:T(8,128)(2,1)S(1)}, u32[]{:S(2)}, u32[]{:S(2)}) collective-permute-start(bf16[8,144,128]{2,1,0:T(8,128)(2,1)S(1)} %get-tuple-element.35), channel_id=1, source_target_pairs={{0,4},{2,6},{4,0},{6,2},{1,5},{3,7},{5,1},{7,3},{8,12},{10,14},{12... | collective-permute-start | bytes 884744 | tf_op jit(solution)/shard_map/ppermute | solution.py:421
  39.5 0.0 collective-permute-start
  39.5 2.0 %collective-permute-start.2 = (bf16[8,144,128]{2,1,0:T(8,128)(2,1)S(1)}, bf16[8,144,128]{2,1,0:T(8,128)(2,1)S(1)}, u32[]{:S(2)}, u32[]{:S(2)}) collective-permute-start(bf16[8,144,128]{2,1,0:T(8,128)(2,1)S(1)} %get-tuple-element.35), channel_id=1, source_target_pairs={{0,6},{2,0},{4,2},{6,4},{1,7},{3,1},{5,3},{7,5},{8,14},{10,8},{12,... | collective-permute-start | bytes 884744 | tf_op jit(solution)/shard_map/ppermute | solution.py:421
  41.5 4.2 %collective-permute-done.1 = bf16[8,144,128]{2,1,0:T(8,128)(2,1)S(1)} collective-permute-done((bf16[8,144,128]{2,1,0:T(8,128)(2,1)S(1)}, bf16[8,144,128]{2,1,0:T(8,128)(2,1)S(1)}, u32[]{:S(2)}, u32[]{:S(2)}) %collective-permute-start.1) | collective-permute-done | bytes 294944 | tf_op jit(solution)/shard_map/ppermute | solution.py:421
  45.7 3.1 %collective-permute-done = bf16[8,144,128]{2,1,0:T(8,128)(2,1)S(1)} collective-permute-done((bf16[8,144,128]{2,1,0:T(8,128)(2,1)S(1)}, bf16[8,144,128]{2,1,0:T(8,128)(2,1)S(1)}, u32[]{:S(2)}, u32[]{:S(2)}) %collective-permute-start) | collective-permute-done | bytes 294944 | tf_op jit(solution)/shard_map/ppermute | solution.py:421
  48.9 0.0 collective-permute-done.2
  48.9 0.1 pad_maximum_fusion.refs_2_
  49.0 7.3 %all-to-all-done.1.part_ref.refs_0_ = bf16[8,432,128]{2,1,0:T(8,128)(2,1)S(1)} async-done(((bf16[8,432,128]{2,1,0:T(8,128)(2,1)}), bf16[8,432,128]{2,1,0:T(8,128)(2,1)S(1)}, u32[]{:S(2)}, u32[]{:S(2)}) %all-to-all-start.1) | async-done | bytes 884768 | tf_op jit(solution)/shard_map/all_to_all | solution.py:458
  56.3 0.3 spread.1
  56.7 18.9 %all_to_all.30.own_ref = bf16[16,8,32,128]{3,2,1,0:T(8,128)(2,1)S(1)} all-to-all(bf16[16,8,32,128]{3,2,1,0:T(8,128)(2,1)S(1)} %spread.1), channel_id=1, replica_groups=mesh['section'=8,'y'=4,'x'=4,'core'=2] {'y','x'}, dimensions={0} | all-to-all | bytes 2097152 | tf_op jit(solution)/shard_map/all_to_all | solution.py:466
  75.6 0.0 collective-permute-start.4
  75.6 0.5 collective-permute-start.3
  76.1 3.8 %collective-permute-done.3.oth_ref = bf16[16,8,32,128]{3,2,1,0:T(8,128)(2,1)S(1)} collective-permute-done((bf16[16,8,32,128]{3,2,1,0:T(8,128)(2,1)S(1)}, bf16[16,8,32,128]{3,2,1,0:T(8,128)(2,1)S(1)}, u32[]{:S(2)}, u32[]{:S(2)}) %collective-permute-start.3) | collective-permute-done | bytes 1048608 | tf_op jit(solution)/shard_map/ppermute | solution.py:468
  79.9 0.0 collective-permute-done.4.refs_3_
  79.9 8.3 %main.1 = (bf16[16,288,128]{2,1,0:T(8,128)(2,1)S(1)}, bf16[16,288,128]{2,1,0:T(8,128)(2,1)S(1)}, f32[16,8,128]{2,1,0:T(8,128)S(1)}) custom-call(bf16[16,8,32,128]{3,2,1,0:T(8,128)(2,1)S(1)} %all_to_all.30.own_ref, bf16[16,8,32,128]{3,2,1,0:T(8,128)(2,1)S(1)} %collective-permute-done.3.oth_ref, bf16[8,432,128]{2,1,0:T(8,128)(2,1)S(1)} %all-to-all-done.1.part_ref.refs_0_, ...), custom_call_target="tpu_custom_call" | custom-call | flops 1409286144 | bytes 10485760 | tf_op jit(solution)/shard_map/main/pallas_call | solution.py:471
  88.2 0.2 collective-permute-start.5
  88.5 10.4 %all_to_all.31.norm_ref = f32[16,8,128]{2,1,0:T(8,128)S(1)} all-to-all(f32[16,8,128]{2,1,0:T(8,128)S(1)} %get-tuple-element.29), channel_id=1, replica_groups=mesh['section'=8,'y'=4,'x'=4,'core'=2] {'section','core'}, dimensions={0} | all-to-all | bytes 131072 | tf_op jit(solution)/shard_map/all_to_all | solution.py:495
  98.8 0.0 collective-permute-done.5.got_ref
  98.8 0.4 mix.1
  99.3 22.0 %all_to_all.32.got_ref = bf16[16,288,128]{2,1,0:T(8,128)(2,1)S(1)} all-to-all(bf16[16,288,128]{2,1,0:T(8,128)(2,1)S(1)} %mix.1), channel_id=1, replica_groups=mesh['section'=8,'y'=4,'x'=4,'core'=2] {'y','x'}, dimensions={0} | all-to-all | bytes 2359296 | tf_op jit(solution)/shard_map/all_to_all | solution.py:497
  121.3 0.2 sum.1
  121.5 11.1 %all_to_all.33.got_ref = bf16[8,48,128]{2,1,0:T(8,128)(2,1)S(1)} all-to-all(bf16[8,48,128]{2,1,0:T(8,128)(2,1)S(1)} %sum.1), channel_id=1, replica_groups=mesh['section'=8,'y'=4,'x'=4,'core'=2] {'section'}, dimensions={0} | all-to-all | bytes 196608 | tf_op jit(solution)/shard_map/all_to_all | solution.py:499
  132.7 0.8 join.1
Async XLA Ops:
  0.6 17.4 %copy-start.1 = (bf16[1,128,4608]{2,1,0:T(8,128)(2,1)S(1)}, bf16[1,128,4608]{2,1,0:T(8,128)(2,1)}, u32[]{:S(2)}) copy-start(bf16[1,128,4608]{2,1,0:T(8,128)(2,1)} %param.7) | copy-start | bytes 3538948
  0.6 17.4 %copy-start.5 = (f32[1,4608]{1,0:T(1,128)S(1)}, f32[1,4608]{1,0:T(1,128)}, u32[]{:S(2)}) copy-start(f32[1,4608]{1,0:T(1,128)} %ls_ref.5) | copy-start | bytes 55300
  9.4 8.6 %copy-start = (bf16[1,4608,128]{2,1,0:T(8,128)(2,1)S(1)}, bf16[1,4608,128]{2,1,0:T(8,128)(2,1)}, u32[]{:S(2)}) copy-start(bf16[1,4608,128]{2,1,0:T(8,128)(2,1)} %param.6) | copy-start | bytes 3538948
  9.4 22.7 %all-to-all-start = ((bf16[8,288,128]{2,1,0:T(8,128)(2,1)}), bf16[8,288,128]{2,1,0:T(8,128)(2,1)S(1)}, u32[]{:S(2)}, u32[]{:S(2)}) async-start(bf16[8,288,128]{2,1,0:T(8,128)(2,1)} %pack.1), calls=%async_computation | async-start | bytes 1179648 | tf_op jit(solution)/shard_map/all_to_all | solution.py:444
  18.0 1.3 copy-start.3
  19.3 1.3 copy-start.4
  32.7 0.9 copy-start.2
  33.7 22.7 %all-to-all-start.1 = ((bf16[8,432,128]{2,1,0:T(8,128)(2,1)}), bf16[8,432,128]{2,1,0:T(8,128)(2,1)S(1)}, u32[]{:S(2)}, u32[]{:S(2)}) async-start(bf16[8,432,128]{2,1,0:T(8,128)(2,1)} %copy-done.2), calls=%async_computation.1 | async-start | bytes 1769472 | tf_op jit(solution)/shard_map/all_to_all | solution.py:458
  37.3 8.4 %collective-permute-start.1 = (bf16[8,144,128]{2,1,0:T(8,128)(2,1)S(1)}, bf16[8,144,128]{2,1,0:T(8,128)(2,1)S(1)}, u32[]{:S(2)}, u32[]{:S(2)}) collective-permute-start(bf16[8,144,128]{2,1,0:T(8,128)(2,1)S(1)} %get-tuple-element.35), channel_id=1, source_target_pairs={{0,4},{2,6},{4,0},{6,2},{1,5},{3,7},{5,1},{7,3},{8,12},{10,14},{12... | collective-permute-start | bytes 884744 | tf_op jit(solution)/shard_map/ppermute | solution.py:421
  39.5 9.3 %collective-permute-start = (bf16[8,144,128]{2,1,0:T(8,128)(2,1)S(1)}, bf16[8,144,128]{2,1,0:T(8,128)(2,1)S(1)}, u32[]{:S(2)}, u32[]{:S(2)}) collective-permute-start(bf16[8,144,128]{2,1,0:T(8,128)(2,1)S(1)} %get-tuple-element.35), channel_id=1, source_target_pairs={{0,2},{2,4},{4,6},{6,0},{1,3},{3,5},{5,7},{7,1},{8,10},{10,12},{12... | collective-permute-start | bytes 884744 | tf_op jit(solution)/shard_map/ppermute | solution.py:421
  39.5 9.3 %collective-permute-start.2 = (bf16[8,144,128]{2,1,0:T(8,128)(2,1)S(1)}, bf16[8,144,128]{2,1,0:T(8,128)(2,1)S(1)}, u32[]{:S(2)}, u32[]{:S(2)}) collective-permute-start(bf16[8,144,128]{2,1,0:T(8,128)(2,1)S(1)} %get-tuple-element.35), channel_id=1, source_target_pairs={{0,6},{2,0},{4,2},{6,4},{1,7},{3,1},{5,3},{7,5},{8,14},{10,8},{12,... | collective-permute-start | bytes 884744 | tf_op jit(solution)/shard_map/ppermute | solution.py:421
  75.6 4.4 %collective-permute-start.4 = (bf16[4,8,144,128]{3,2,1,0:T(8,128)(2,1)S(1)}, bf16[4,8,144,128]{3,2,1,0:T(8,128)(2,1)S(1)}, u32[]{:S(2)}, u32[]{:S(2)}) collective-permute-start(bf16[4,8,144,128]{3,2,1,0:T(8,128)(2,1)S(1)} %pad_maximum_fusion.refs_2_), channel_id=1, source_target_pairs={{0,1},{1,0},{2,3},{3,2},{4,5},{5,4},{6,7},{7,6},{8,9},{9,8},{10,11... | collective-permute-start | bytes 3538952 | tf_op jit(solution)/shard_map/ppermute | solution.py:469
  75.6 4.3 %collective-permute-start.3 = (bf16[16,8,32,128]{3,2,1,0:T(8,128)(2,1)S(1)}, bf16[16,8,32,128]{3,2,1,0:T(8,128)(2,1)S(1)}, u32[]{:S(2)}, u32[]{:S(2)}) collective-permute-start(bf16[16,8,32,128]{3,2,1,0:T(8,128)(2,1)S(1)} %all_to_all.30.own_ref), channel_id=1, source_target_pairs={{0,1},{1,0},{2,3},{3,2},{4,5},{5,4},{6,7},{7,6},{8,9},{9,8},{10,11... | collective-permute-start | bytes 3145736 | tf_op jit(solution)/shard_map/ppermute | solution.py:468
  88.2 10.6 %collective-permute-start.5 = (bf16[16,288,128]{2,1,0:T(8,128)(2,1)S(1)}, bf16[16,288,128]{2,1,0:T(8,128)(2,1)S(1)}, u32[]{:S(2)}, u32[]{:S(2)}) collective-permute-start(bf16[16,288,128]{2,1,0:T(8,128)(2,1)S(1)} %get-tuple-element.31), channel_id=1, source_target_pairs={{0,1},{1,0},{2,3},{3,2},{4,5},{5,4},{6,7},{7,6},{8,9},{9,8},{10,11... | collective-permute-start | bytes 3538952 | tf_op jit(solution)/shard_map/ppermute | solution.py:494

commit v6 on v5

--- a/solution.py
+++ b/solution.py
@@ -18,6 +18,7 @@
 PACK_VMEM = 56
 LATE = 6
 BAND = D // 4
+LAST = 2 + 2 * S + S * S
 Z, Y, X, C = "section", "y", "x", "core"
 BF = jnp.bfloat16
 F32 = jnp.float32
@@ -64,11 +65,13 @@
     return (col == ((row % 16) // 2) * 16 + outer * 2 + row % 2).astype(BF)
 
 
-def pack_kernel(w_in_ref, w_out_ref, ls_ref, pay_ref, rows, wide, block, strip, sem):
+def pack_kernel(w_in_ref, w_out_ref, far_ls_ref, pay_ref, rows, wide, block, strip, head, ls_ref, sem):
     y, x, core = lax.axis_index(Y), lax.axis_index(X), lax.axis_index(C)
     q = (x * 2 + core) * 4 + y
     row_copy = pltpu.make_async_copy(w_out_ref.at[pl.ds(pl.multiple_of((q // 4) * 16, 16), 16)], rows, sem.at[0])
     row_copy.start()
+    ls_copy = pltpu.make_async_copy(far_ls_ref, ls_ref, sem.at[LAST])
+    ls_copy.start()
     start = pl.multiple_of(x * BAND, R)
 
     def in_copy():
@@ -98,6 +101,7 @@
     def _():
         out_copy().start()
 
+    ls_copy.wait()
     row_copy.wait()
     part = rows[...].astype(F32) * ls_ref[...]
     group = q % 4
@@ -112,8 +116,10 @@
     )
     for u in range(9):
         two = jnp.concatenate([mine[:, 256 * u : 256 * u + R], mine[:, 256 * u + R : 256 * (u + 1)]], axis=0).astype(BF)
-        for k in range(S):
-            strip[k, 16 * u : 16 * u + 16] = two
+        head[16 * u : 16 * u + 16] = two
+    heads = [pltpu.make_async_copy(head, pay_ref.at[k, pl.ds(0, ROWS)], sem.at[2 + k]) for k in range(S)]
+    for cp in heads:
+        cp.start()
 
     @pl.when(core == 0)
     def _():
@@ -129,20 +135,19 @@
 
     for k in range(S):
         for e in range(S):
-            strip[k, ROWS + 16 * e : ROWS + 16 * e + 16] = block[QUARTER * e + 16 * k : QUARTER * e + 16 * k + 16]
+            strip[k, 16 * e : 16 * e + 16] = block[QUARTER * e + 16 * k : QUARTER * e + 16 * k + 16]
     left = jnp.concatenate([block[QUARTER * e + 128 : QUARTER * (e + 1)] for e in range(S)], axis=0)
     left = mm(swap_units(R), left).astype(BF)
     for k in range(S):
-        strip[k, ROWS + 128 :] = left[16 * k : 16 * k + 16]
+        strip[k, 128:] = left[16 * k : 16 * k + 16]
 
     def sends(late):
-        if not late:
-            return [pltpu.make_async_copy(strip.at[k], pay_ref.at[k], sem.at[2 + k]) for k in range(S)]
         return [
-            pltpu.make_async_copy(strip.at[k, pl.ds(a, n)], pay_ref.at[k, pl.ds(a, n)], sem.at[2 + S + S * LATE + 2 * k + i])
-            for k in range(LATE)
-            for i, (a, n) in enumerate(((0, ROWS), (ROWS + 128, 16)))
-        ] + [pltpu.make_async_copy(strip.at[k], pay_ref.at[k], sem.at[2 + k]) for k in range(LATE, S)]
+            pltpu.make_async_copy(strip.at[k, pl.ds(128, 16)], pay_ref.at[k, pl.ds(ROWS + 128, 16)], sem.at[2 + S + S * S + k])
+            if late and k < LATE
+            else pltpu.make_async_copy(strip.at[k], pay_ref.at[k, pl.ds(ROWS, ROWS)], sem.at[2 + S + S * S + k])
+            for k in range(S)
+        ]
 
     @pl.when(core == 0)
     def _():
@@ -157,6 +162,9 @@
             cp.start()
         for cp in sends(False):
             cp.wait()
+
+    for cp in heads:
+        cp.wait()
 
 
 def project_kernel(x_ref, c_ref, w_in_ref, w_out_ref, ls_ref, proj, scales, sq_ref, xt_ref, ct_ref, wide):
@@ -226,7 +234,7 @@
 
 def main_kernel(own_ref, oth_ref, *refs):
     proj_ref, sq_ref, wown_ref, woth_ref, xt_ref, ct_ref, gown_ref, goth_ref, norm_ref = refs[:9]
-    kmat, pre, qacc, hacc, slope, hs, hts, ps, sts, wbuf, xs, gos, lefts, sem = refs[9:]
+    kmat, pre, qacc, hacc, slope, hs, hts, sts, wbuf, xs, gos, lefts, sem = refs[9:]
     core = lax.axis_index(C)
     is0 = core == 0
     copies = []
@@ -259,9 +267,17 @@
         for i, acc in enumerate((pre, qacc, hacc)):
             acc[:, s * R : (s + 1) * R] = proj_ref[s, 32 + T * i : 32 + T * (i + 1)].astype(F32)
     sq = sq_ref[...]
+    for cp in copies:
+        cp.wait()
+
+    def weights(kind, s):
+        return jnp.concatenate([wbuf[kind, j, s, :128] for j in range(4)] + [wbuf[kind, j, s, 128:] for j in range(4)], axis=0)
+
     lane = lax.broadcasted_iota(jnp.int32, (T, R), 1)
     scal = jnp.zeros((T, R), F32)
     inv = []
+    x = xt_ref[...]
+    xs[0] = x
     for s in range(S):
         here = slice(s * R, (s + 1) * R)
         r = lax.rsqrt(sq * (1.0 / D) + EPS)
@@ -274,43 +290,36 @@
         slope[:, here] = 0.5 * (1.0 + th) + 0.5 * v * (1.0 - th * th) * (GELU_A * (1.0 + 3.0 * GELU_B * v * v))
         hs[s] = h
         hf = h.astype(F32)
-        hts[s] = hf.T.astype(BF)
         if s + 1 < S:
             before = qacc[:, here]
             qacc[:, s * R :] += mm(h, kmat[s * R :, here], NT)
-            sq = sq + jnp.sum(hf * (before + qacc[:, here]), axis=1, keepdims=True)
+            sq = jnp.maximum(sq + jnp.sum(hf * (before + qacc[:, here]), axis=1, keepdims=True), 0.0)
             pre[:, (s + 1) * R :] += mm(h, kmat[here, (s + 1) * R :])
+            x = (x.astype(F32) + mm(weights(1, s), h, NT)).astype(BF)
+            xs[s + 1] = x
+        hts[s] = hf.T.astype(BF)
+    sts[...] = scal.T
     gam = jnp.zeros((T, 1), F32)
+    total = jnp.zeros((64, R), F32)
+    g = ct_ref[...]
     for s in reversed(range(S)):
         here = slice(s * R, (s + 1) * R)
         hg = hacc[:, here]
         if s + 1 < S:
             hg = hg - gam * qacc[:, here]
         p = (hg * slope[:, here]).astype(BF)
-        ps[s] = p
         r = inv[s]
         cen = r * r * (jnp.sum(p.astype(F32) * pre[:, here], axis=1, keepdims=True) * (1.0 / D))
-        scal = jnp.where(lane == S + s, cen, scal)
         if s > 0:
             upd = r * mm(p, kmat[: s * R, here], NT)
             if s + 1 < S:
                 upd = upd - gam * mm(hs[s], kmat[here, : s * R])
             hacc[:, : s * R] += upd
         gam = gam + cen
-    sts[...] = scal.T
-    for cp in copies:
-        cp.wait()
-
-    def weights(kind, s):
-        return jnp.concatenate([wbuf[kind, j, s, :128] for j in range(4)] + [wbuf[kind, j, s, 128:] for j in range(4)], axis=0)
-
-    total = jnp.zeros((64, R), F32)
-    x = xt_ref[...]
-    for s in range(S):
-        xs[s] = x
-        xf = x.astype(F32)
-        n = (xf * sts[s : s + 1, :]).astype(BF)
-        gi = mm(n, ps[s])
+
+        xf = xs[s].astype(F32)
+        rrow = sts[s : s + 1, :]
+        gi = mm((xf * rrow).astype(BF), p)
         for j in range(9):
             total = total + gi[64 * j : 64 * j + 64] * gi[64 * j : 64 * j + 64]
         for i in range(16):
@@ -319,8 +328,13 @@
             goth_ref[i, 16 * s : 16 * s + 16] = jnp.where(is0, b, a).astype(BF)
         for j in range(4):
             lefts[j, 16 * s : 16 * s + 16] = gi[512 + 16 * j : 512 + 16 * j + 16].astype(BF)
-        if s + 1 < S:
-            x = (xf + mm(weights(1, s), hs[s], NT)).astype(BF)
+        lsf = proj_ref[s, 32 + 3 * T :].astype(F32)
+        lsf = jnp.concatenate([lsf[:4] + lsf[4:8], lsf[8:12] + lsf[12:]], axis=0)
+        lrow = jnp.concatenate([lsf[j : j + 1] for j in range(4)] + [lsf[4 + j : 5 + j, :16] for j in range(4)], axis=1)
+        gos[s] = mm(hts[s], g, NT) * lrow
+        if s > 0:
+            crow = jnp.broadcast_to(cen, (T, R)).T[:1]
+            g = (g.astype(F32) + rrow * mm(weights(0, s), p, NT) - crow * xf).astype(BF)
     units = swap_units(R)
     for j in range(4):
         left = mm(units, lefts[j])
@@ -328,15 +342,6 @@
             a, b = left[32 * i : 32 * i + 16], left[32 * i + 16 : 32 * i + 32]
             gown_ref[4 * j + i, 128:ROWS] = jnp.where(is0, a, b).astype(BF)
             goth_ref[4 * j + i, 128:ROWS] = jnp.where(is0, b, a).astype(BF)
-    g = ct_ref[...]
-    for s in reversed(range(S)):
-        lsf = proj_ref[s, 32 + 3 * T :].astype(F32)
-        lsf = jnp.concatenate([lsf[:4] + lsf[4:8], lsf[8:12] + lsf[12:]], axis=0)
-        lrow = jnp.concatenate([lsf[j : j + 1] for j in range(4)] + [lsf[4 + j : 5 + j, :16] for j in range(4)], axis=1)
-        gos[s] = mm(hts[s], g, NT) * lrow
-        if s > 0:
-            m = mm(weights(0, s), ps[s], NT)
-            g = (g.astype(F32) + sts[s : s + 1, :] * m - sts[S + s : S + s + 1, :] * xs[s].astype(F32)).astype(BF)
     acc = jnp.zeros((R, SLICE), F32)
     for s in range(S):
         acc = acc + gos[s] * gos[s]
@@ -431,13 +436,15 @@
     (pay,) = call(
         pack_kernel, "pack",
         [((S, 2 * ROWS, R), BF)],
-        [anywhere, anywhere, VM],
+        [anywhere, anywhere, anywhere],
         [
             pltpu.VMEM((16, D), BF),
             pltpu.VMEM((R, BAND), BF),
             pltpu.VMEM((BAND, R), BF),
-            pltpu.VMEM((S, 2 * ROWS, R), BF),
-            pltpu.SemaphoreType.DMA((2 + 3 * S + S * S,)),
+            pltpu.VMEM((S, ROWS, R), BF),
+            pltpu.VMEM((ROWS, R), BF),
+            pltpu.VMEM((1, D), F32),
+            pltpu.SemaphoreType.DMA((LAST + 1,)),
         ],
         flops=flops // 16, size=2 << 20, vmem=PACK_VMEM, to=[far],
     )(w1, w_out[0], layer_scale)
@@ -480,7 +487,6 @@
             pltpu.VMEM((T, S * R), F32),
             pltpu.VMEM((S, T, R), BF),
             pltpu.VMEM((S, R, T), BF),
-            pltpu.VMEM((S, T, R), BF),
             pltpu.VMEM((R, T), F32),
             pltpu.VMEM((2, 4, S, QUARTER, R), BF),
             pltpu.VMEM((S, SLICE, T), BF),

time: 134 us -> 131 us (0.978)
  Pallas kernels: 21.2 us -> 18.5 us
    pallas_call x1, Pallas kernels: 8.31 us -> 6.45 us  [per_device(): call(main_kernel, 'main', [((16, 2 * ROWS, R), BF), ((16, 2 * ROWS, R), B...]
where the time goes in v6:
time: 131 us
  blocking collectives  62.4 us (48%)
  waiting for transfers between devices  28.3 us (22%)
  Pallas kernels  18.5 us (14%)
  starting transfers between devices  17.1 us (13%)
  local copies, waits for them, and re-layouts  3.54 us (3%)
    all_to_all x1, blocking collectives, per_device(): both = lax.all_to_all(both, (Y, X), 0, 0)  22 us
    all_to_all x1, blocking collectives, per_device(): kown = lax.all_to_all(spread, (Y, X), 0, 0)  18.9 us
    all_to_all x1, blocking collectives, per_device(): got = lax.all_to_all(sent, Z, 0, 0)  11.1 us
    all_to_all x1, blocking collectives, per_device(): norm = lax.all_to_all(norm, (Z, C), 0, 0)  10.4 us
    all_to_all x1, waiting for transfers between devices, per_device(): got = lax.all_to_all(pay, Z, 0, 0)  9.81 us
    all_to_all x1, starting transfers between devices, per_device(): got = lax.all_to_all(pay, Z, 0, 0)  8.61 us
    pallas_call x1, Pallas kernels, per_device(): call(pack_kernel, 'pack', [((S, 2 * ROWS, R), BF)], [anywhere, anywhere,...  7.85 us
    all_to_all x1, waiting for transfers between devices, per_device(): part = lax.all_to_all(part, Z, 0, 0)  7.32 us
  transfers between devices with their start and end apart: 8, of which 5 were waited for; matrix products, arithmetic and copies ran while one was open for 0% of the time, Pallas kernels for 1%

profile of v6, /device:TPU:2, one launch (start us, length us, event | category | flops | bytes accessed | tf_op | source)
XLA Modules:
  0.0 130.8 jit_solution(5774628962526876271)
XLA Ops:
  0.6 0.0 copy-start.1
  0.6 0.0 copy-start.5
  0.6 7.9 %pack.1 = bf16[8,288,128]{2,1,0:T(8,128)(2,1)} custom-call(bf16[4608,128]{1,0:T(8,128)(2,1)} %bitcast.7, bf16[128,4608]{1,0:T(8,128)(2,1)} %bitcast.10, f32[1,4608]{1,0:T(1,128)} %ls_ref.3), custom_call_target="tpu_custom_call" | custom-call | flops 9437184 | bytes 2097152 | tf_op jit(solution)/shard_map/pack/pallas_call | solution.py:436
  8.5 0.0 copy-start
  8.5 8.6 %all-to-all-start = ((bf16[8,288,128]{2,1,0:T(8,128)(2,1)}), bf16[8,288,128]{2,1,0:T(8,128)(2,1)S(1)}, u32[]{:S(2)}, u32[]{:S(2)}) async-start(bf16[8,288,128]{2,1,0:T(8,128)(2,1)} %pack.1), calls=%async_computation | async-start | bytes 1179648 | tf_op jit(solution)/shard_map/all_to_all | solution.py:451
  17.1 0.0 copy-done.1
  17.1 0.0 copy-done.5
  17.1 0.0 copy-done
  17.2 0.0 copy-start.3
  17.2 1.3 copy-done.3
  18.4 0.0 copy-start.4
  18.4 1.3 copy-done.4
  19.7 1.7 %project.1 = (bf16[384,128]{1,0:T(8,128)(2,1)S(1)}, bf16[8,16,128]{2,1,0:T(8,128)(2,1)S(1)}, f32[128,1]{1,0:T(8,128)S(1)}, bf16[576,128]{1,0:T(8,128)(2,1)S(1)}, bf16[576,128]{1,0:T(8,128)(2,1)S(1)}) custom-call(bf16[128,4608]{1,0:T(8,128)(2,1)S(1)} %copy-done.3, bf16[128,4608]{1,0:T(8,128)(2,1)S(1)} %copy-done.4, bf16[4608,128]{1,0:T(8,128)(2,1)S(1)} %bitcast.8, ...), custom_call_target="tpu_custom_call" | custom-call | flops 452984832 | bytes 5242880 | tf_op jit(solution)/shard_map/project/pallas_call | solution.py:453
  21.4 9.8 %all-to-all-done.got_ref = bf16[8,288,128]{2,1,0:T(8,128)(2,1)S(1)} async-done(((bf16[8,288,128]{2,1,0:T(8,128)(2,1)}), bf16[8,288,128]{2,1,0:T(8,128)(2,1)S(1)}, u32[]{:S(2)}, u32[]{:S(2)}) %all-to-all-start) | async-done | bytes 589856 | tf_op jit(solution)/shard_map/all_to_all | solution.py:451
  31.2 0.7 gram.1
  31.9 0.0 copy-start.2
  31.9 0.9 copy-done.2
  32.8 3.5 %all-to-all-start.1 = ((bf16[8,432,128]{2,1,0:T(8,128)(2,1)}), bf16[8,432,128]{2,1,0:T(8,128)(2,1)S(1)}, u32[]{:S(2)}, u32[]{:S(2)}) async-start(bf16[8,432,128]{2,1,0:T(8,128)(2,1)} %copy-done.2), calls=%async_computation.1 | async-start | bytes 1769472 | tf_op jit(solution)/shard_map/all_to_all | solution.py:465
  36.4 0.1 slice_bitcast_fusion
  36.4 2.2 %collective-permute-start.1 = (bf16[8,144,128]{2,1,0:T(8,128)(2,1)S(1)}, bf16[8,144,128]{2,1,0:T(8,128)(2,1)S(1)}, u32[]{:S(2)}, u32[]{:S(2)}) collective-permute-start(bf16[8,144,128]{2,1,0:T(8,128)(2,1)S(1)} %get-tuple-element.35), channel_id=1, source_target_pairs={{0,4},{2,6},{4,0},{6,2},{1,5},{3,7},{5,1},{7,3},{8,12},{10,14},{12... | collective-permute-start | bytes 884744 | tf_op jit(solution)/shard_map/ppermute | solution.py:426
  38.7 0.0 collective-permute-start
  38.7 2.0 %collective-permute-start.2 = (bf16[8,144,128]{2,1,0:T(8,128)(2,1)S(1)}, bf16[8,144,128]{2,1,0:T(8,128)(2,1)S(1)}, u32[]{:S(2)}, u32[]{:S(2)}) collective-permute-start(bf16[8,144,128]{2,1,0:T(8,128)(2,1)S(1)} %get-tuple-element.35), channel_id=1, source_target_pairs={{0,6},{2,0},{4,2},{6,4},{1,7},{3,1},{5,3},{7,5},{8,14},{10,8},{12,... | collective-permute-start | bytes 884744 | tf_op jit(solution)/shard_map/ppermute | solution.py:426
  40.7 4.2 %collective-permute-done.1 = bf16[8,144,128]{2,1,0:T(8,128)(2,1)S(1)} collective-permute-done((bf16[8,144,128]{2,1,0:T(8,128)(2,1)S(1)}, bf16[8,144,128]{2,1,0:T(8,128)(2,1)S(1)}, u32[]{:S(2)}, u32[]{:S(2)}) %collective-permute-start.1) | collective-permute-done | bytes 294944 | tf_op jit(solution)/shard_map/ppermute | solution.py:426
  44.9 3.1 %collective-permute-done = bf16[8,144,128]{2,1,0:T(8,128)(2,1)S(1)} collective-permute-done((bf16[8,144,128]{2,1,0:T(8,128)(2,1)S(1)}, bf16[8,144,128]{2,1,0:T(8,128)(2,1)S(1)}, u32[]{:S(2)}, u32[]{:S(2)}) %collective-permute-start) | collective-permute-done | bytes 294944 | tf_op jit(solution)/shard_map/ppermute | solution.py:426
  48.0 0.0 collective-permute-done.2
  48.0 0.1 pad_maximum_fusion.refs_2_
  48.2 7.3 %all-to-all-done.1.part_ref.refs_0_ = bf16[8,432,128]{2,1,0:T(8,128)(2,1)S(1)} async-done(((bf16[8,432,128]{2,1,0:T(8,128)(2,1)}), bf16[8,432,128]{2,1,0:T(8,128)(2,1)S(1)}, u32[]{:S(2)}, u32[]{:S(2)}) %all-to-all-start.1) | async-done | bytes 884768 | tf_op jit(solution)/shard_map/all_to_all | solution.py:465
  55.5 0.3 spread.1
  55.8 18.9 %all_to_all.30.own_ref = bf16[16,8,32,128]{3,2,1,0:T(8,128)(2,1)S(1)} all-to-all(bf16[16,8,32,128]{3,2,1,0:T(8,128)(2,1)S(1)} %spread.1), channel_id=1, replica_groups=mesh['section'=8,'y'=4,'x'=4,'core'=2] {'y','x'}, dimensions={0} | all-to-all | bytes 2097152 | tf_op jit(solution)/shard_map/all_to_all | solution.py:473
  74.7 0.0 collective-permute-start.4
  74.7 0.5 collective-permute-start.3
  75.2 3.8 %collective-permute-done.3.oth_ref = bf16[16,8,32,128]{3,2,1,0:T(8,128)(2,1)S(1)} collective-permute-done((bf16[16,8,32,128]{3,2,1,0:T(8,128)(2,1)S(1)}, bf16[16,8,32,128]{3,2,1,0:T(8,128)(2,1)S(1)}, u32[]{:S(2)}, u32[]{:S(2)}) %collective-permute-start.3) | collective-permute-done | bytes 1048608 | tf_op jit(solution)/shard_map/ppermute | solution.py:475
  79.1 0.0 collective-permute-done.4.refs_3_
  79.1 6.5 %main.1 = (bf16[16,288,128]{2,1,0:T(8,128)(2,1)S(1)}, bf16[16,288,128]{2,1,0:T(8,128)(2,1)S(1)}, f32[16,8,128]{2,1,0:T(8,128)S(1)}) custom-call(bf16[16,8,32,128]{3,2,1,0:T(8,128)(2,1)S(1)} %all_to_all.30.own_ref, bf16[16,8,32,128]{3,2,1,0:T(8,128)(2,1)S(1)} %collective-permute-done.3.oth_ref, bf16[8,432,128]{2,1,0:T(8,128)(2,1)S(1)} %all-to-all-done.1.part_ref.refs_0_, ...), custom_call_target="tpu_custom_call" | custom-call | flops 1409286144 | bytes 10485760 | tf_op jit(solution)/shard_map/main/pallas_call | solution.py:478
  85.5 0.2 collective-permute-start.5
  85.8 10.4 %all_to_all.31.norm_ref = f32[16,8,128]{2,1,0:T(8,128)S(1)} all-to-all(f32[16,8,128]{2,1,0:T(8,128)S(1)} %get-tuple-element.29), channel_id=1, replica_groups=mesh['section'=8,'y'=4,'x'=4,'core'=2] {'section','core'}, dimensions={0} | all-to-all | bytes 131072 | tf_op jit(solution)/shard_map/all_to_all | solution.py:501
  96.1 0.0 collective-permute-done.5.got_ref
  96.1 0.4 mix.1
  96.6 22.0 %all_to_all.32.got_ref = bf16[16,288,128]{2,1,0:T(8,128)(2,1)S(1)} all-to-all(bf16[16,288,128]{2,1,0:T(8,128)(2,1)S(1)} %mix.1), channel_id=1, replica_groups=mesh['section'=8,'y'=4,'x'=4,'core'=2] {'y','x'}, dimensions={0} | all-to-all | bytes 2359296 | tf_op jit(solution)/shard_map/all_to_all | solution.py:503
  118.6 0.2 sum.1
  118.8 11.1 %all_to_all.33.got_ref = bf16[8,48,128]{2,1,0:T(8,128)(2,1)S(1)} all-to-all(bf16[8,48,128]{2,1,0:T(8,128)(2,1)S(1)} %sum.1), channel_id=1, replica_groups=mesh['section'=8,'y'=4,'x'=4,'core'=2] {'section'}, dimensions={0} | all-to-all | bytes 196608 | tf_op jit(solution)/shard_map/all_to_all | solution.py:505
  130.0 0.8 join.1
Async XLA Ops:
  0.6 16.5 %copy-start.1 = (bf16[1,128,4608]{2,1,0:T(8,128)(2,1)S(1)}, bf16[1,128,4608]{2,1,0:T(8,128)(2,1)}, u32[]{:S(2)}) copy-start(bf16[1,128,4608]{2,1,0:T(8,128)(2,1)} %param.7) | copy-start | bytes 3538948
  0.6 16.5 %copy-start.5 = (f32[1,4608]{1,0:T(1,128)S(1)}, f32[1,4608]{1,0:T(1,128)}, u32[]{:S(2)}) copy-start(f32[1,4608]{1,0:T(1,128)} %ls_ref.3) | copy-start | bytes 55300
  8.5 8.6 %copy-start = (bf16[1,4608,128]{2,1,0:T(8,128)(2,1)S(1)}, bf16[1,4608,128]{2,1,0:T(8,128)(2,1)}, u32[]{:S(2)}) copy-start(bf16[1,4608,128]{2,1,0:T(8,128)(2,1)} %param.6) | copy-start | bytes 3538948
  8.5 22.7 %all-to-all-start = ((bf16[8,288,128]{2,1,0:T(8,128)(2,1)}), bf16[8,288,128]{2,1,0:T(8,128)(2,1)S(1)}, u32[]{:S(2)}, u32[]{:S(2)}) async-start(bf16[8,288,128]{2,1,0:T(8,128)(2,1)} %pack.1), calls=%async_computation | async-start | bytes 1179648 | tf_op jit(solution)/shard_map/all_to_all | solution.py:451
  17.2 1.3 copy-start.3
  18.4 1.3 copy-start.4
  31.9 0.9 copy-start.2
  32.8 22.7 %all-to-all-start.1 = ((bf16[8,432,128]{2,1,0:T(8,128)(2,1)}), bf16[8,432,128]{2,1,0:T(8,128)(2,1)S(1)}, u32[]{:S(2)}, u32[]{:S(2)}) async-start(bf16[8,432,128]{2,1,0:T(8,128)(2,1)} %copy-done.2), calls=%async_computation.1 | async-start | bytes 1769472 | tf_op jit(solution)/shard_map/all_to_all | solution.py:465
  36.4 8.4 %collective-permute-start.1 = (bf16[8,144,128]{2,1,0:T(8,128)(2,1)S(1)}, bf16[8,144,128]{2,1,0:T(8,128)(2,1)S(1)}, u32[]{:S(2)}, u32[]{:S(2)}) collective-permute-start(bf16[8,144,128]{2,1,0:T(8,128)(2,1)S(1)} %get-tuple-element.35), channel_id=1, source_target_pairs={{0,4},{2,6},{4,0},{6,2},{1,5},{3,7},{5,1},{7,3},{8,12},{10,14},{12... | collective-permute-start | bytes 884744 | tf_op jit(solution)/shard_map/ppermute | solution.py:426
  38.7 9.3 %collective-permute-start = (bf16[8,144,128]{2,1,0:T(8,128)(2,1)S(1)}, bf16[8,144,128]{2,1,0:T(8,128)(2,1)S(1)}, u32[]{:S(2)}, u32[]{:S(2)}) collective-permute-start(bf16[8,144,128]{2,1,0:T(8,128)(2,1)S(1)} %get-tuple-element.35), channel_id=1, source_target_pairs={{0,2},{2,4},{4,6},{6,0},{1,3},{3,5},{5,7},{7,1},{8,10},{10,12},{12... | collective-permute-start | bytes 884744 | tf_op jit(solution)/shard_map/ppermute | solution.py:426
  38.7 9.3 %collective-permute-start.2 = (bf16[8,144,128]{2,1,0:T(8,128)(2,1)S(1)}, bf16[8,144,128]{2,1,0:T(8,128)(2,1)S(1)}, u32[]{:S(2)}, u32[]{:S(2)}) collective-permute-start(bf16[8,144,128]{2,1,0:T(8,128)(2,1)S(1)} %get-tuple-element.35), channel_id=1, source_target_pairs={{0,6},{2,0},{4,2},{6,4},{1,7},{3,1},{5,3},{7,5},{8,14},{10,8},{12,... | collective-permute-start | bytes 884744 | tf_op jit(solution)/shard_map/ppermute | solution.py:426
  74.7 4.4 %collective-permute-start.4 = (bf16[4,8,144,128]{3,2,1,0:T(8,128)(2,1)S(1)}, bf16[4,8,144,128]{3,2,1,0:T(8,128)(2,1)S(1)}, u32[]{:S(2)}, u32[]{:S(2)}) collective-permute-start(bf16[4,8,144,128]{3,2,1,0:T(8,128)(2,1)S(1)} %pad_maximum_fusion.refs_2_), channel_id=1, source_target_pairs={{0,1},{1,0},{2,3},{3,2},{4,5},{5,4},{6,7},{7,6},{8,9},{9,8},{10,11... | collective-permute-start | bytes 3538952 | tf_op jit(solution)/shard_map/ppermute | solution.py:476
  74.7 4.3 %collective-permute-start.3 = (bf16[16,8,32,128]{3,2,1,0:T(8,128)(2,1)S(1)}, bf16[16,8,32,128]{3,2,1,0:T(8,128)(2,1)S(1)}, u32[]{:S(2)}, u32[]{:S(2)}) collective-permute-start(bf16[16,8,32,128]{3,2,1,0:T(8,128)(2,1)S(1)} %all_to_all.30.own_ref), channel_id=1, source_target_pairs={{0,1},{1,0},{2,3},{3,2},{4,5},{5,4},{6,7},{7,6},{8,9},{9,8},{10,11... | collective-permute-start | bytes 3145736 | tf_op jit(solution)/shard_map/ppermute | solution.py:475
  85.5 10.6 %collective-permute-start.5 = (bf16[16,288,128]{2,1,0:T(8,128)(2,1)S(1)}, bf16[16,288,128]{2,1,0:T(8,128)(2,1)S(1)}, u32[]{:S(2)}, u32[]{:S(2)}) collective-permute-start(bf16[16,288,128]{2,1,0:T(8,128)(2,1)S(1)} %get-tuple-element.31), channel_id=1, source_target_pairs={{0,1},{1,0},{2,3},{3,2},{4,5},{5,4},{6,7},{7,6},{8,9},{9,8},{10,11... | collective-permute-start | bytes 3538952 | tf_op jit(solution)/shard_map/ppermute | solution.py:500

commit v7 on v6

--- a/solution.py
+++ b/solution.py
@@ -18,6 +18,7 @@
 PACK_VMEM = 56
 LATE = 6
 BAND = D // 4
+THIRD = BAND // 3
 LAST = 2 + 2 * S + S * S
 Z, Y, X, C = "section", "y", "x", "core"
 BF = jnp.bfloat16
@@ -77,8 +78,13 @@
     def in_copy():
         return pltpu.make_async_copy(w_in_ref.at[pl.ds(start, BAND)], block, sem.at[1])
 
-    def out_copy():
-        return pltpu.make_async_copy(w_out_ref.at[:, pl.ds(start, BAND)], wide, sem.at[1])
+    def out_copies():
+        return [
+            pltpu.make_async_copy(
+                w_out_ref.at[:, pl.ds(pl.multiple_of(start + THIRD * i, R), THIRD)], wide.at[i], sem.at[10 + i]
+            )
+            for i in range(3)
+        ]
 
     def late_copies():
         return [
@@ -99,7 +105,8 @@
 
     @pl.when(core != 0)
     def _():
-        out_copy().start()
+        for cp in out_copies():
+            cp.start()
 
     ls_copy.wait()
     row_copy.wait()
@@ -127,10 +134,12 @@
 
     @pl.when(core != 0)
     def _():
-        out_copy().wait()
+        parts = out_copies()
         scale = ls_ref[:, pl.ds(start, BAND)]
         for t in range(BAND // R):
-            tile = wide[:, t * R : (t + 1) * R].astype(F32) * scale[:, t * R : (t + 1) * R]
+            if t % 3 == 0:
+                parts[t // 3].wait()
+            tile = wide[t // 3, :, t % 3 * R : (t % 3 + 1) * R].astype(F32) * scale[:, t * R : (t + 1) * R]
             block[t * R : (t + 1) * R, :] = tile.T.astype(BF)
 
     for k in range(S):
@@ -301,6 +310,8 @@
     sts[...] = scal.T
     gam = jnp.zeros((T, 1), F32)
     total = jnp.zeros((64, R), F32)
+    acc = jnp.zeros((R, SLICE), F32)
+    tails = {}
     g = ct_ref[...]
     for s in reversed(range(S)):
         here = slice(s * R, (s + 1) * R)
@@ -331,10 +342,25 @@
         lsf = proj_ref[s, 32 + 3 * T :].astype(F32)
         lsf = jnp.concatenate([lsf[:4] + lsf[4:8], lsf[8:12] + lsf[12:]], axis=0)
         lrow = jnp.concatenate([lsf[j : j + 1] for j in range(4)] + [lsf[4 + j : 5 + j, :16] for j in range(4)], axis=1)
-        gos[s] = mm(hts[s], g, NT) * lrow
+        part = mm(hts[s], g, NT) * lrow
+        acc = acc + part * part
+        gos[s] = part
         if s > 0:
             crow = jnp.broadcast_to(cen, (T, R)).T[:1]
             g = (g.astype(F32) + rrow * mm(weights(0, s), p, NT) - crow * xf).astype(BF)
+        if s % 4 == 0:
+            v = [gos[s + i].reshape(16, 8, SLICE) for i in range(4)]
+            a0, a1 = halves(v[0], v[1])
+            b0, b1 = halves(v[2], v[3])
+            even = jnp.concatenate([a0, b0], axis=1)
+            odd = jnp.concatenate([a1, b1], axis=1)
+            mine = jnp.where(is0, even, odd)
+            rest = jnp.where(is0, odd, even)
+            for t in range(4):
+                at = slice(ROWS + 32 * t + 4 * s, ROWS + 32 * t + 4 * s + 16)
+                gown_ref[:, at] = mine[:, :, t * R : (t + 1) * R].astype(BF)
+                goth_ref[:, at] = rest[:, :, t * R : (t + 1) * R].astype(BF)
+            tails[s // 4] = (mine[:, :, 4 * R :], rest[:, :, 4 * R :])
     units = swap_units(R)
     for j in range(4):
         left = mm(units, lefts[j])
@@ -342,23 +368,6 @@
             a, b = left[32 * i : 32 * i + 16], left[32 * i + 16 : 32 * i + 32]
             gown_ref[4 * j + i, 128:ROWS] = jnp.where(is0, a, b).astype(BF)
             goth_ref[4 * j + i, 128:ROWS] = jnp.where(is0, b, a).astype(BF)
-    acc = jnp.zeros((R, SLICE), F32)
-    for s in range(S):
-        acc = acc + gos[s] * gos[s]
-    tails = []
-    for quad in range(2):
-        v = [gos[quad * 4 + i].reshape(16, 8, SLICE) for i in range(4)]
-        a0, a1 = halves(v[0], v[1])
-        b0, b1 = halves(v[2], v[3])
-        even = jnp.concatenate([a0, b0], axis=1)
-        odd = jnp.concatenate([a1, b1], axis=1)
-        mine = jnp.where(is0, even, odd)
-        rest = jnp.where(is0, odd, even)
-        for t in range(4):
-            at = slice(ROWS + 32 * t + 16 * quad, ROWS + 32 * t + 16 * quad + 16)
-            gown_ref[:, at] = mine[:, :, t * R : (t + 1) * R].astype(BF)
-            goth_ref[:, at] = rest[:, :, t * R : (t + 1) * R].astype(BF)
-        tails.append((mine[:, :, 4 * R :], rest[:, :, 4 * R :]))
     gown_ref[:, ROWS + 128 :] = jnp.concatenate([tails[0][0], tails[1][0]], axis=2).astype(BF)
     goth_ref[:, ROWS + 128 :] = jnp.concatenate([tails[0][1], tails[1][1]], axis=2).astype(BF)
     one = jnp.sum(jnp.sum(total, axis=0, keepdims=True), axis=1, keepdims=True)
@@ -439,7 +448,7 @@
         [anywhere, anywhere, anywhere],
         [
             pltpu.VMEM((16, D), BF),
-            pltpu.VMEM((R, BAND), BF),
+            pltpu.VMEM((3, R, THIRD), BF),
             pltpu.VMEM((BAND, R), BF),
             pltpu.VMEM((S, ROWS, R), BF),
             pltpu.VMEM((ROWS, R), BF),

time: 131 us -> 131 us (level)
  no operation moved by 1% of the time
where the time goes in v7:
time: 131 us
  blocking collectives  62.4 us (48%)
  waiting for transfers between devices  28.4 us (22%)
  Pallas kernels  18.5 us (14%)
  starting transfers between devices  17.1 us (13%)
  local copies, waits for them, and re-layouts  3.54 us (3%)
    all_to_all x1, blocking collectives, per_device(): both = lax.all_to_all(both, (Y, X), 0, 0)  22 us
    all_to_all x1, blocking collectives, per_device(): kown = lax.all_to_all(spread, (Y, X), 0, 0)  18.9 us
    all_to_all x1, blocking collectives, per_device(): got = lax.all_to_all(sent, Z, 0, 0)  11.1 us
    all_to_all x1, blocking collectives, per_device(): norm = lax.all_to_all(norm, (Z, C), 0, 0)  10.4 us
    all_to_all x1, waiting for transfers between devices, per_device(): got = lax.all_to_all(pay, Z, 0, 0)  9.87 us
    all_to_all x1, starting transfers between devices, per_device(): got = lax.all_to_all(pay, Z, 0, 0)  8.61 us
    pallas_call x1, Pallas kernels, per_device(): call(pack_kernel, 'pack', [((S, 2 * ROWS, R), BF)], [anywhere, anywhere,...  7.85 us
    all_to_all x1, waiting for transfers between devices, per_device(): part = lax.all_to_all(part, Z, 0, 0)  7.34 us
  transfers between devices with their start and end apart: 8, of which 5 were waited for; matrix products, arithmetic and copies ran while one was open for 0% of the time, Pallas kernels for 1%

profile of v7, /device:TPU:2, one launch (start us, length us, event | category | flops | bytes accessed | tf_op | source)
XLA Modules:
  0.0 130.8 jit_solution(4013852536062832937)
XLA Ops:
  0.6 0.0 copy-start.1
  0.6 0.0 copy-start.5
  0.6 7.9 %pack.1 = bf16[8,288,128]{2,1,0:T(8,128)(2,1)} custom-call(bf16[4608,128]{1,0:T(8,128)(2,1)} %bitcast.7, bf16[128,4608]{1,0:T(8,128)(2,1)} %bitcast.10, f32[1,4608]{1,0:T(1,128)} %ls_ref.3), custom_call_target="tpu_custom_call" | custom-call | flops 9437184 | bytes 2097152 | tf_op jit(solution)/shard_map/pack/pallas_call | solution.py:445
  8.5 0.0 copy-start
  8.5 8.6 %all-to-all-start = ((bf16[8,288,128]{2,1,0:T(8,128)(2,1)}), bf16[8,288,128]{2,1,0:T(8,128)(2,1)S(1)}, u32[]{:S(2)}, u32[]{:S(2)}) async-start(bf16[8,288,128]{2,1,0:T(8,128)(2,1)} %pack.1), calls=%async_computation | async-start | bytes 1179648 | tf_op jit(solution)/shard_map/all_to_all | solution.py:460
  17.1 0.0 copy-done.1
  17.1 0.0 copy-done.5
  17.1 0.0 copy-done
  17.2 0.0 copy-start.3
  17.2 1.3 copy-done.3
  18.4 0.0 copy-start.4
  18.4 1.3 copy-done.4
  19.7 1.7 %project.1 = (bf16[384,128]{1,0:T(8,128)(2,1)S(1)}, bf16[8,16,128]{2,1,0:T(8,128)(2,1)S(1)}, f32[128,1]{1,0:T(8,128)S(1)}, bf16[576,128]{1,0:T(8,128)(2,1)S(1)}, bf16[576,128]{1,0:T(8,128)(2,1)S(1)}) custom-call(bf16[128,4608]{1,0:T(8,128)(2,1)S(1)} %copy-done.3, bf16[128,4608]{1,0:T(8,128)(2,1)S(1)} %copy-done.4, bf16[4608,128]{1,0:T(8,128)(2,1)S(1)} %bitcast.8, ...), custom_call_target="tpu_custom_call" | custom-call | flops 452984832 | bytes 5242880 | tf_op jit(solution)/shard_map/project/pallas_call | solution.py:462
  21.4 9.9 %all-to-all-done.got_ref = bf16[8,288,128]{2,1,0:T(8,128)(2,1)S(1)} async-done(((bf16[8,288,128]{2,1,0:T(8,128)(2,1)}), bf16[8,288,128]{2,1,0:T(8,128)(2,1)S(1)}, u32[]{:S(2)}, u32[]{:S(2)}) %all-to-all-start) | async-done | bytes 589856 | tf_op jit(solution)/shard_map/all_to_all | solution.py:460
  31.3 0.7 gram.1
  32.0 0.0 copy-start.2
  32.0 0.9 copy-done.2
  32.9 3.5 %all-to-all-start.1 = ((bf16[8,432,128]{2,1,0:T(8,128)(2,1)}), bf16[8,432,128]{2,1,0:T(8,128)(2,1)S(1)}, u32[]{:S(2)}, u32[]{:S(2)}) async-start(bf16[8,432,128]{2,1,0:T(8,128)(2,1)} %copy-done.2), calls=%async_computation.1 | async-start | bytes 1769472 | tf_op jit(solution)/shard_map/all_to_all | solution.py:474
  36.4 0.1 slice_bitcast_fusion
  36.5 2.2 %collective-permute-start.1 = (bf16[8,144,128]{2,1,0:T(8,128)(2,1)S(1)}, bf16[8,144,128]{2,1,0:T(8,128)(2,1)S(1)}, u32[]{:S(2)}, u32[]{:S(2)}) collective-permute-start(bf16[8,144,128]{2,1,0:T(8,128)(2,1)S(1)} %get-tuple-element.35), channel_id=1, source_target_pairs={{0,4},{2,6},{4,0},{6,2},{1,5},{3,7},{5,1},{7,3},{8,12},{10,14},{12... | collective-permute-start | bytes 884744 | tf_op jit(solution)/shard_map/ppermute | solution.py:435
  38.7 0.0 collective-permute-start
  38.7 2.0 %collective-permute-start.2 = (bf16[8,144,128]{2,1,0:T(8,128)(2,1)S(1)}, bf16[8,144,128]{2,1,0:T(8,128)(2,1)S(1)}, u32[]{:S(2)}, u32[]{:S(2)}) collective-permute-start(bf16[8,144,128]{2,1,0:T(8,128)(2,1)S(1)} %get-tuple-element.35), channel_id=1, source_target_pairs={{0,6},{2,0},{4,2},{6,4},{1,7},{3,1},{5,3},{7,5},{8,14},{10,8},{12,... | collective-permute-start | bytes 884744 | tf_op jit(solution)/shard_map/ppermute | solution.py:435
  40.7 4.2 %collective-permute-done.1 = bf16[8,144,128]{2,1,0:T(8,128)(2,1)S(1)} collective-permute-done((bf16[8,144,128]{2,1,0:T(8,128)(2,1)S(1)}, bf16[8,144,128]{2,1,0:T(8,128)(2,1)S(1)}, u32[]{:S(2)}, u32[]{:S(2)}) %collective-permute-start.1) | collective-permute-done | bytes 294944 | tf_op jit(solution)/shard_map/ppermute | solution.py:435
  44.9 3.1 %collective-permute-done = bf16[8,144,128]{2,1,0:T(8,128)(2,1)S(1)} collective-permute-done((bf16[8,144,128]{2,1,0:T(8,128)(2,1)S(1)}, bf16[8,144,128]{2,1,0:T(8,128)(2,1)S(1)}, u32[]{:S(2)}, u32[]{:S(2)}) %collective-permute-start) | collective-permute-done | bytes 294944 | tf_op jit(solution)/shard_map/ppermute | solution.py:435
  48.1 0.0 collective-permute-done.2
  48.1 0.1 pad_maximum_fusion.refs_2_
  48.2 7.3 %all-to-all-done.1.part_ref.refs_0_ = bf16[8,432,128]{2,1,0:T(8,128)(2,1)S(1)} async-done(((bf16[8,432,128]{2,1,0:T(8,128)(2,1)}), bf16[8,432,128]{2,1,0:T(8,128)(2,1)S(1)}, u32[]{:S(2)}, u32[]{:S(2)}) %all-to-all-start.1) | async-done | bytes 884768 | tf_op jit(solution)/shard_map/all_to_all | solution.py:474
  55.6 0.3 spread.1
  55.9 18.9 %all_to_all.30.own_ref = bf16[16,8,32,128]{3,2,1,0:T(8,128)(2,1)S(1)} all-to-all(bf16[16,8,32,128]{3,2,1,0:T(8,128)(2,1)S(1)} %spread.1), channel_id=1, replica_groups=mesh['section'=8,'y'=4,'x'=4,'core'=2] {'y','x'}, dimensions={0} | all-to-all | bytes 2097152 | tf_op jit(solution)/shard_map/all_to_all | solution.py:482
  74.8 0.0 collective-permute-start.4
  74.8 0.5 collective-permute-start.3
  75.3 3.8 %collective-permute-done.3.oth_ref = bf16[16,8,32,128]{3,2,1,0:T(8,128)(2,1)S(1)} collective-permute-done((bf16[16,8,32,128]{3,2,1,0:T(8,128)(2,1)S(1)}, bf16[16,8,32,128]{3,2,1,0:T(8,128)(2,1)S(1)}, u32[]{:S(2)}, u32[]{:S(2)}) %collective-permute-start.3) | collective-permute-done | bytes 1048608 | tf_op jit(solution)/shard_map/ppermute | solution.py:484
  79.1 0.0 collective-permute-done.4.refs_3_
  79.2 6.4 %main.1 = (bf16[16,288,128]{2,1,0:T(8,128)(2,1)S(1)}, bf16[16,288,128]{2,1,0:T(8,128)(2,1)S(1)}, f32[16,8,128]{2,1,0:T(8,128)S(1)}) custom-call(bf16[16,8,32,128]{3,2,1,0:T(8,128)(2,1)S(1)} %all_to_all.30.own_ref, bf16[16,8,32,128]{3,2,1,0:T(8,128)(2,1)S(1)} %collective-permute-done.3.oth_ref, bf16[8,432,128]{2,1,0:T(8,128)(2,1)S(1)} %all-to-all-done.1.part_ref.refs_0_, ...), custom_call_target="tpu_custom_call" | custom-call | flops 1409286144 | bytes 10485760 | tf_op jit(solution)/shard_map/main/pallas_call | solution.py:487
  85.6 0.2 collective-permute-start.5
  85.8 10.4 %all_to_all.31.norm_ref = f32[16,8,128]{2,1,0:T(8,128)S(1)} all-to-all(f32[16,8,128]{2,1,0:T(8,128)S(1)} %get-tuple-element.29), channel_id=1, replica_groups=mesh['section'=8,'y'=4,'x'=4,'core'=2] {'section','core'}, dimensions={0} | all-to-all | bytes 131072 | tf_op jit(solution)/shard_map/all_to_all | solution.py:510
  96.2 0.0 collective-permute-done.5.got_ref
  96.2 0.4 mix.1
  96.6 22.0 %all_to_all.32.got_ref = bf16[16,288,128]{2,1,0:T(8,128)(2,1)S(1)} all-to-all(bf16[16,288,128]{2,1,0:T(8,128)(2,1)S(1)} %mix.1), channel_id=1, replica_groups=mesh['section'=8,'y'=4,'x'=4,'core'=2] {'y','x'}, dimensions={0} | all-to-all | bytes 2359296 | tf_op jit(solution)/shard_map/all_to_all | solution.py:512
  118.6 0.2 sum.1
  118.9 11.1 %all_to_all.33.got_ref = bf16[8,48,128]{2,1,0:T(8,128)(2,1)S(1)} all-to-all(bf16[8,48,128]{2,1,0:T(8,128)(2,1)S(1)} %sum.1), channel_id=1, replica_groups=mesh['section'=8,'y'=4,'x'=4,'core'=2] {'section'}, dimensions={0} | all-to-all | bytes 196608 | tf_op jit(solution)/shard_map/all_to_all | solution.py:514
  130.0 0.8 join.1
Async XLA Ops:
  0.6 16.5 %copy-start.1 = (bf16[1,128,4608]{2,1,0:T(8,128)(2,1)S(1)}, bf16[1,128,4608]{2,1,0:T(8,128)(2,1)}, u32[]{:S(2)}) copy-start(bf16[1,128,4608]{2,1,0:T(8,128)(2,1)} %param.7) | copy-start | bytes 3538948
  0.6 16.5 %copy-start.5 = (f32[1,4608]{1,0:T(1,128)S(1)}, f32[1,4608]{1,0:T(1,128)}, u32[]{:S(2)}) copy-start(f32[1,4608]{1,0:T(1,128)} %ls_ref.3) | copy-start | bytes 55300
  8.5 8.6 %copy-start = (bf16[1,4608,128]{2,1,0:T(8,128)(2,1)S(1)}, bf16[1,4608,128]{2,1,0:T(8,128)(2,1)}, u32[]{:S(2)}) copy-start(bf16[1,4608,128]{2,1,0:T(8,128)(2,1)} %param.6) | copy-start | bytes 3538948
  8.5 22.8 %all-to-all-start = ((bf16[8,288,128]{2,1,0:T(8,128)(2,1)}), bf16[8,288,128]{2,1,0:T(8,128)(2,1)S(1)}, u32[]{:S(2)}, u32[]{:S(2)}) async-start(bf16[8,288,128]{2,1,0:T(8,128)(2,1)} %pack.1), calls=%async_computation | async-start | bytes 1179648 | tf_op jit(solution)/shard_map/all_to_all | solution.py:460
  17.2 1.3 copy-start.3
  18.4 1.3 copy-start.4
  32.0 0.9 copy-start.2
  32.9 22.7 %all-to-all-start.1 = ((bf16[8,432,128]{2,1,0:T(8,128)(2,1)}), bf16[8,432,128]{2,1,0:T(8,128)(2,1)S(1)}, u32[]{:S(2)}, u32[]{:S(2)}) async-start(bf16[8,432,128]{2,1,0:T(8,128)(2,1)} %copy-done.2), calls=%async_computation.1 | async-start | bytes 1769472 | tf_op jit(solution)/shard_map/all_to_all | solution.py:474
  36.5 8.4 %collective-permute-start.1 = (bf16[8,144,128]{2,1,0:T(8,128)(2,1)S(1)}, bf16[8,144,128]{2,1,0:T(8,128)(2,1)S(1)}, u32[]{:S(2)}, u32[]{:S(2)}) collective-permute-start(bf16[8,144,128]{2,1,0:T(8,128)(2,1)S(1)} %get-tuple-element.35), channel_id=1, source_target_pairs={{0,4},{2,6},{4,0},{6,2},{1,5},{3,7},{5,1},{7,3},{8,12},{10,14},{12... | collective-permute-start | bytes 884744 | tf_op jit(solution)/shard_map/ppermute | solution.py:435
  38.7 9.3 %collective-permute-start = (bf16[8,144,128]{2,1,0:T(8,128)(2,1)S(1)}, bf16[8,144,128]{2,1,0:T(8,128)(2,1)S(1)}, u32[]{:S(2)}, u32[]{:S(2)}) collective-permute-start(bf16[8,144,128]{2,1,0:T(8,128)(2,1)S(1)} %get-tuple-element.35), channel_id=1, source_target_pairs={{0,2},{2,4},{4,6},{6,0},{1,3},{3,5},{5,7},{7,1},{8,10},{10,12},{12... | collective-permute-start | bytes 884744 | tf_op jit(solution)/shard_map/ppermute | solution.py:435
  38.7 9.3 %collective-permute-start.2 = (bf16[8,144,128]{2,1,0:T(8,128)(2,1)S(1)}, bf16[8,144,128]{2,1,0:T(8,128)(2,1)S(1)}, u32[]{:S(2)}, u32[]{:S(2)}) collective-permute-start(bf16[8,144,128]{2,1,0:T(8,128)(2,1)S(1)} %get-tuple-element.35), channel_id=1, source_target_pairs={{0,6},{2,0},{4,2},{6,4},{1,7},{3,1},{5,3},{7,5},{8,14},{10,8},{12,... | collective-permute-start | bytes 884744 | tf_op jit(solution)/shard_map/ppermute | solution.py:435
  74.8 4.4 %collective-permute-start.4 = (bf16[4,8,144,128]{3,2,1,0:T(8,128)(2,1)S(1)}, bf16[4,8,144,128]{3,2,1,0:T(8,128)(2,1)S(1)}, u32[]{:S(2)}, u32[]{:S(2)}) collective-permute-start(bf16[4,8,144,128]{3,2,1,0:T(8,128)(2,1)S(1)} %pad_maximum_fusion.refs_2_), channel_id=1, source_target_pairs={{0,1},{1,0},{2,3},{3,2},{4,5},{5,4},{6,7},{7,6},{8,9},{9,8},{10,11... | collective-permute-start | bytes 3538952 | tf_op jit(solution)/shard_map/ppermute | solution.py:485
  74.8 4.3 %collective-permute-start.3 = (bf16[16,8,32,128]{3,2,1,0:T(8,128)(2,1)S(1)}, bf16[16,8,32,128]{3,2,1,0:T(8,128)(2,1)S(1)}, u32[]{:S(2)}, u32[]{:S(2)}) collective-permute-start(bf16[16,8,32,128]{3,2,1,0:T(8,128)(2,1)S(1)} %all_to_all.30.own_ref), channel_id=1, source_target_pairs={{0,1},{1,0},{2,3},{3,2},{4,5},{5,4},{6,7},{7,6},{8,9},{9,8},{10,11... | collective-permute-start | bytes 3145736 | tf_op jit(solution)/shard_map/ppermute | solution.py:484
  85.6 10.6 %collective-permute-start.5 = (bf16[16,288,128]{2,1,0:T(8,128)(2,1)S(1)}, bf16[16,288,128]{2,1,0:T(8,128)(2,1)S(1)}, u32[]{:S(2)}, u32[]{:S(2)}) collective-permute-start(bf16[16,288,128]{2,1,0:T(8,128)(2,1)S(1)} %get-tuple-element.31), channel_id=1, source_target_pairs={{0,1},{1,0},{2,3},{3,2},{4,5},{5,4},{6,7},{7,6},{8,9},{9,8},{10,11... | collective-permute-start | bytes 3538952 | tf_op jit(solution)/shard_map/ppermute | solution.py:509
